TPU v7x, 32 devices: a whole 2x2x4 slice. The times are simulated.
32 devices in a mesh: rows: 8 (over z, y), tp: 4 (over x, core).
Axes of the slice: x: 2, y: 2, z: 4, core: 2. Of those that a mesh axis runs over, the one named last changes fastest.
Arguments:
- patches: bfloat16 [80, 240, 512], P('rows'), may hold values from -6 to 6
- cotangent: bfloat16 [80, 240, 512], P('rows'), may hold values from -6 to 6
- page_bounds: int32 [8, 2], P('rows'), may hold values from 0 to 7, as said below
- attn_gain: bfloat16 [512], replicated, may hold values from 0.5 to 1.5
- attn_shift: bfloat16 [512], replicated, may hold values from -1.75 to 1.75
- qkv_weight: bfloat16 [3, 512, 512], P(None, None, 'tp'), may hold values from -0.25 to 0.25
- qv_bias: bfloat16 [2, 512], P(None, 'tp'), may hold values from -1.75 to 1.75
- pos_table: bfloat16 [361, 16], P(None, 'tp'), may hold values from -6 to 6
- proj_weight: bfloat16 [512, 512], P('tp'), may hold values from -1 to 1
- proj_bias: bfloat16 [512], replicated, may hold values from -1.75 to 1.75
- mlp_gain: bfloat16 [512], replicated, may hold values from 0.5 to 1.5
- mlp_shift: bfloat16 [512], replicated, may hold values from -1.75 to 1.75
- up_weight: bfloat16 [512, 2048], P(None, 'tp'), may hold values from -0.25 to 0.25
- up_bias: bfloat16 [2048], P('tp'), may hold values from -1.75 to 1.75
- down_weight: bfloat16 [2048, 512], P('tp'), may hold values from -0.1875 to 0.1875
- down_bias: bfloat16 [512], replicated, may hold values from -1.75 to 1.75
Outputs:
- block_out: bfloat16 [80, 240, 512], P('rows')
- grad_patches: bfloat16 [80, 240, 512], P('rows')
- grad_attn_gain: float32 [512], replicated
- grad_attn_shift: float32 [512], replicated
- grad_qkv: float32 [3, 512, 512], P(None, None, 'tp')
- grad_qv_bias: float32 [2, 512], P(None, 'tp')
- grad_pos_table: float32 [361, 16], P(None, 'tp')
- grad_proj: float32 [512, 512], P('tp')
- grad_proj_bias: float32 [512], replicated
- grad_mlp_gain: float32 [512], replicated
- grad_mlp_shift: float32 [512], replicated
- grad_up: float32 [512, 2048], P(None, 'tp')
- grad_up_bias: float32 [2048], P('tp')
- grad_down: float32 [2048, 512], P('tp')
- grad_down_bias: float32 [512], replicated
Inputs may be any that keep to these rules, and one draw needn't show every extreme that they name: `page_bounds`: row w holds the first and the last window row of the page that contains w; the 5 pages are consecutive runs of window rows of random lengths covering all 8 rows.
All inputs are finite; a program needn't handle non-finite values.
Results may differ from a plain program's by a relative error of at most 0.012.
The roundings to bfloat16 on the way count: a program that leaves them out, or rounds other values in their place, can miss the bound.
Values may be sent and summed in bfloat16 or wider, within the bound.
No kernel may reach another device: no remote copies, remote signals or barrier semaphores. Data moves between devices by JAX's collectives and lax.ppermute only.
A program may use at most 128 MiB of HBM per device.

v0:
```python
import functools

import jax
import jax.numpy as jnp
import numpy as np
from jax import lax
from jax.experimental import pallas as pl
from jax.experimental.pallas import tpu as pltpu
from jax.sharding import PartitionSpec as P

D = 512
HD = 32
WIN = 10
SHIFT = 5
TABLE = 361
TABLE_PAD = 384
NORM_EPS = 1e-05
MASKED = -1000000000.0
HIDDEN_KEY = -1e30

TP = 4
HEADS_HERE = 4
LANES = 128
TOKENS = WIN * WIN
WROW = 112
SEG = 64
STRIP = SHIFT * SEG
COLBLK = 16
NBLK = 5
SLAB = SHIFT * NBLK * COLBLK
STACK = HEADS_HERE * WROW
SPAN = 2 * WIN - 1
REACH = SPAN * (WIN - 1) + WIN - 1
PACK1 = 4 * D + 32
SMALL_VECS = 6 * (D // LANES)
SMALL_SHARD = 24
PACK2 = 2 * D + 16

F32 = jnp.float32
BF = jnp.bfloat16
VMEM_LIMIT = 56 * 1024 * 1024
COST_RATE = 2e8


def dot(a, b):
    return lax.dot_general(a, b, (((1,), (0,)), ((), ())), preferred_element_type=F32)


def dot_nt(a, b):
    return lax.dot_general(a, b, (((1,), (1,)), ((), ())), preferred_element_type=F32)


def dot_tn(a, b):
    return lax.dot_general(a, b, (((0,), (0,)), ((), ())), preferred_element_type=F32)


def onehot(idx, width):
    lanes = lax.broadcasted_iota(jnp.int32, (idx.shape[0], width), 1)
    return jnp.where(idx == lanes, 1.0, 0.0).astype(BF)


def rows_of(nwl):
    return -(-(nwl * WROW + 16) // 64) * 64


@functools.lru_cache(None)
def index_tables(nwl):
    rows = rows_of(nwl)
    slab_w = NBLK * COLBLK
    strip = np.full((STRIP, 1), -1000, np.int32)
    out_up = np.full((STRIP, 1), -1000, np.int32)
    out_low = np.full((STRIP, 1), -1000, np.int32)
    win_up = np.full((rows, 1), -1000, np.int32)
    win_low = np.full((rows, 1), -1000, np.int32)
    for a in range(SHIFT):
        for cc in range(nwl * WIN):
            j, b = divmod(cc, WIN)
            strip[a * SEG + cc, 0] = a * slab_w + cc
            out_up[a * SEG + cc, 0] = j * WROW + a * WIN + b
            out_low[a * SEG + cc, 0] = j * WROW + (a + SHIFT) * WIN + b
            win_up[j * WROW + a * WIN + b, 0] = a * slab_w + cc
            win_low[j * WROW + (a + SHIFT) * WIN + b, 0] = a * SEG + cc
    return strip, win_up, win_low, out_up, out_low


@functools.lru_cache(None)
def attention_tables():
    emask = np.zeros((WROW, LANES), np.float32)
    fmask = np.zeros((WROW, LANES), np.float32)
    i = np.arange(TOKENS)
    a, b = i // WIN, i % WIN
    emask[:TOKENS, :TOKENS] = (a[:, None] >= SHIFT) != (a[None] >= SHIFT)
    fmask[:TOKENS, :TOKENS] = (b[:, None] >= SHIFT) != (b[None] >= SHIFT)
    spread = np.zeros((2 * LANES, LANES), np.float32)
    spread[SPAN * a + b, i] = 1.0
    back = np.zeros((LANES, TABLE_PAD), np.float32)
    back[i, REACH - (SPAN * a + b)] = 1.0
    groups = np.zeros((WIN * 8, STACK), np.float32)
    for h in range(HEADS_HERE):
        groups[a * 8 + h, h * WROW + i] = 1.0
    return emask * MASKED, fmask * MASKED, spread, back, groups


KERNEL_US = {
    "head": 3.0,
    "rest": 5.0,
    "attn_fwd": 14.0,
    "mlp_fwd_a": 8.0,
    "mlp_fwd_b": 8.0,
    "mlp_bwd_a": 8.0,
    "mlp_bwd_b": 9.0,
    "attn_bwd_13": 13.0,
    "attn_bwd_2": 9.0,
    "attn_bwd_0": 11.0,
    "page_y": 4.0,
    "page_g": 4.0,
}


def cost(name):
    return pl.CostEstimate(
        flops=int(KERNEL_US.get(name, 2.0) * COST_RATE), bytes_accessed=1024, transcendentals=0
    )


def vspec():
    return pl.BlockSpec(memory_space=pltpu.VMEM)


def after(x, *others):
    return lax.optimization_barrier((x, *others))[0]


def call(kernel, args, outs, scratch=(), scalars=(), name=None):
    return pl.pallas_call(
        kernel,
        out_shape=[jax.ShapeDtypeStruct(s, d) for s, d in outs],
        in_specs=[pl.BlockSpec(memory_space=pltpu.SMEM) for _ in scalars] + [vspec() for _ in args],
        out_specs=[vspec() for _ in outs],
        scratch_shapes=list(scratch),
        compiler_params=pltpu.CompilerParams(vmem_limit_bytes=VMEM_LIMIT),
        cost_estimate=cost(name),
        name=name,
    )(*scalars, *args)


def column_block(ref, start):
    main = (NBLK - 1) * COLBLK
    last = lax.rem(start + main, ref.shape[1])
    parts = [
        ref[:, pl.ds(pl.multiple_of(start, COLBLK), main), :],
        ref[:, pl.ds(pl.multiple_of(last, COLBLK), COLBLK), :],
    ]
    return jnp.concatenate(parts, axis=1).reshape(SLAB, D)


def first_column(width):
    c = lax.axis_index("tp") * width + SHIFT
    off = lax.rem(c, COLBLK)
    return c - off, off


def head_kernel(width, x_up, idx, wqkv, wproj, table, bias, strip, pack):
    start, off = first_column(width)
    strip[...] = dot(onehot(idx[...] + off, SLAB), column_block(x_up, start)).astype(BF)
    for m in range(3):
        pack[m * D : (m + 1) * D, :] = wqkv[m]
    for c in range(D // LANES):
        pack[3 * D + c * LANES : 3 * D + (c + 1) * LANES, :] = wproj[:, c * LANES : (c + 1) * LANES]
    row = lax.broadcasted_iota(jnp.int32, (TABLE, TABLE_PAD), 0)
    lane = lax.broadcasted_iota(jnp.int32, (TABLE, TABLE_PAD), 1)
    flip = jnp.where(row + lane == TABLE - 1, 1.0, 0.0).astype(BF)
    rev = dot(table[...], flip)
    lines = [rev[:, c * LANES : (c + 1) * LANES] for c in range(TABLE_PAD // LANES)]
    lines += [bias[...].astype(F32), jnp.zeros((PACK1 - 4 * D - 14, LANES), F32)]
    pack[4 * D :, :] = jnp.concatenate(lines, axis=0).astype(BF)


def half_spec(field, half):
    return pl.BlockSpec((SHIFT,) + field.shape[1:], lambda g: (half, 0, 0))


def whole_spec(a):
    return pl.BlockSpec(a.shape, lambda g: (0,) * a.ndim)


def windowed_call(kernel, args, specs, outs, name):
    return pl.pallas_call(
        kernel,
        grid=(1,),
        in_specs=specs,
        out_specs=[pl.BlockSpec(s, lambda g, n=len(s): (0,) * n) for s, _ in outs],
        out_shape=[jax.ShapeDtypeStruct(s, d) for s, d in outs],
        compiler_params=pltpu.CompilerParams(vmem_limit_bytes=VMEM_LIMIT),
        cost_estimate=cost(name),
        name=name,
    )(*args)


def rest_kernel(width, g_up, x_low, g_low, idx_strip, idx_win, up, down, ubias, strip_g, win_x, win_g, pack):
    start, off = first_column(width)
    strip_g[...] = dot(onehot(idx_strip[...] + off, SLAB), column_block(g_up, start)).astype(BF)
    hot = onehot(idx_win[...] + off, SLAB)
    win_x[...] = dot(hot, column_block(x_low, start)).astype(BF)
    win_g[...] = dot(hot, column_block(g_low, start)).astype(BF)
    pack[:D, :] = up[...]
    pack[D : 2 * D, :] = down[...]
    pack[2 * D :, :] = jnp.broadcast_to(ubias[...], (PACK2 - 2 * D, D))


def norm_stats(x):
    mean = jnp.mean(x, axis=-1, keepdims=True)
    center = x - mean
    spread = jnp.mean(center * center, axis=-1, keepdims=True)
    inv = lax.rsqrt(spread + NORM_EPS)
    return center * inv, inv


def norm_back(dz, n, inv, gain):
    gz = dz * gain
    m1 = jnp.mean(gz, axis=-1, keepdims=True)
    m2 = jnp.mean(gz * n, axis=-1, keepdims=True)
    return (gz - m1 - n * m2) * inv


def row_chunks(rows, count):
    size = rows // count
    return [(c * size, size) for c in range(count)]


def head_masks():
    lane = lax.broadcasted_iota(jnp.int32, (1, LANES), 1)
    return [(lane >= h * HD) & (lane < (h + 1) * HD) for h in range(HEADS_HERE)]


def stacked(x, masks):
    return jnp.concatenate([jnp.where(m, x, jnp.zeros_like(x)) for m in masks], axis=0)


def unstacked(y, masks):
    total = jnp.where(masks[0], y[:WROW], 0.0)
    for h in range(1, HEADS_HERE):
        total = jnp.where(masks[h], y[h * WROW : (h + 1) * WROW], total)
    return total


def attn_fwd_kernel(nwl, bounds, upx, recv, idx_low, vecs, em, fm, spread, *refs):
    packs = refs[:TP]
    refs = refs[TP:]
    qkv, probs, o_out = refs[:TP], refs[TP : 2 * TP], refs[2 * TP : 3 * TP]
    x_out, z1_out, hs_out, z2_out, bias_sc, roll_sc, row_sc, w_sc = refs[3 * TP :]
    rows = x_out.shape[0]
    is_end = jnp.where(bounds[0, 1] == lax.axis_index("rows"), 1.0, 0.0)
    last = jnp.where(lax.axis_index("tp") == TP - 1, 1.0, 0.0)
    g1, b1, g2, b2, bp = (vecs[i : i + 1, :] for i in range(5))

    table = jnp.concatenate(
        [
            jnp.concatenate(
                [packs[s][4 * D + 4 * c : 4 * D + 4 * c + 4, :].astype(F32) for c in range(TABLE_PAD // LANES)],
                axis=1,
            )
            for s in range(TP)
        ],
        axis=0,
    )
    for i in range(TOKENS):
        shift = TABLE_PAD - REACH + SPAN * (i // WIN) + i % WIN
        rolled = pltpu.roll(table, shift, 1)
        roll_sc[i * TP * HEADS_HERE : (i + 1) * TP * HEADS_HERE, :] = rolled[:, : 2 * LANES].astype(BF)
    n16 = TOKENS * TP * HEADS_HERE
    row_sc[:n16, :] = dot(roll_sc[...], spread[...])
    row_sc[n16:, :] = jnp.zeros((WROW * TP * HEADS_HERE - n16, LANES), F32)
    lane = lax.broadcasted_iota(jnp.int32, (WROW, LANES), 1)
    extra = em[...] * is_end + jnp.where(lane < TOKENS, 0.0, HIDDEN_KEY)
    for s in range(TP):
        for h in range(HEADS_HERE):
            rows_h = row_sc[pl.ds(s * HEADS_HERE + h, WROW, TP * HEADS_HERE), :]
            bias_sc[s, h * WROW : (h + 1) * WROW, :] = rows_h + extra

    for r0, n in row_chunks(rows, 4):
        x = upx[r0 : r0 + n, :].astype(F32) + dot(onehot(idx_low[r0 : r0 + n, :], STRIP), recv[...])
        x_out[r0 : r0 + n, :] = x.astype(BF)
        z, _ = norm_stats(x)
        z1_out[r0 : r0 + n, :] = (z * g1 + b1).astype(BF)
    scale = HD ** (-0.5)
    for m in range(3):
        for s in range(TP):
            w_sc[:, s * LANES : (s + 1) * LANES] = packs[s][m * D : (m + 1) * D, :]
        for r0, n in row_chunks(rows, 2):
            y = dot(z1_out[r0 : r0 + n, :], w_sc[...])
            for s in range(TP):
                part = y[:, s * LANES : (s + 1) * LANES]
                bq = packs[s][4 * D + 12 : 4 * D + 14, :].astype(F32)
                if m == 0:
                    part = (part + bq[0:1, :]) * scale
                if m == 2:
                    part = part + bq[1:2, :]
                qkv[s][m, r0 : r0 + n, :] = part.astype(BF)
    for s in range(TP):
        o_out[s][nwl * WROW :, :] = jnp.zeros((rows - nwl * WROW, LANES), BF)
        for c in range(D // LANES):
            w_sc[s * LANES : (s + 1) * LANES, c * LANES : (c + 1) * LANES] = packs[s][
                3 * D + c * LANES : 3 * D + (c + 1) * LANES, :
            ]

    def window(j, carry):
        masks = head_masks()
        base = pl.multiple_of(j * WROW, 16)
        flag = jnp.where(j == nwl - 1, last, 0.0)
        fm4 = jnp.concatenate([fm[...] * flag] * HEADS_HERE, axis=0)
        for s in range(TP):
            q = qkv[s][0, pl.ds(base, WROW), :]
            k = qkv[s][1, pl.ds(base, LANES), :]
            v = qkv[s][2, pl.ds(base, LANES), :]
            sco = dot_nt(stacked(q, masks), k) + bias_sc[s] + fm4
            top = jnp.max(sco, axis=-1, keepdims=True)
            e = jnp.exp(sco - top)
            total = jnp.sum(e, axis=-1, keepdims=True)
            p = (e / total).astype(BF)
            probs[s][j] = p
            o = unstacked(dot(p, v), masks)
            o_out[s][pl.ds(base, WROW), :] = o.astype(BF)
        return carry

    lax.fori_loop(0, nwl, window, 0)
    for r0, n in row_chunks(rows, 2):
        o = jnp.concatenate([o_out[s][r0 : r0 + n, :] for s in range(TP)], axis=1)
        acc = x_out[r0 : r0 + n, :].astype(F32) + bp + dot(o, w_sc[...])
        hs_out[r0 : r0 + n, :] = acc
        z, _ = norm_stats(acc)
        z2_out[r0 : r0 + n, :] = (z * g2 + b2).astype(BF)


def my_block(blocks):
    w = lax.axis_index("rows")
    mine = 0
    size = blocks
    while size > 1:
        size //= 2
        mine = mine * 2 + lax.rem(w, 2)
        w = lax.div(w, 2)
    return mine


def store_blocks(out, r0, value, blocks, cols=None):
    size = value.shape[0] // blocks
    mine = my_block(blocks)
    for b in range(blocks):
        at = pl.multiple_of(r0 + jnp.bitwise_xor(mine, b) * size, size)
        part = value[b * size : (b + 1) * size, :]
        if cols is None:
            out[pl.ds(at, size), :] = part
        else:
            out[pl.ds(at, size), cols[0] : cols[1]] = part


def mlp_fwd_kernel(shards, first, blocks, *refs):
    ns = len(shards)
    refs = list(refs)
    packs = refs[:ns]
    z2 = refs[ns]
    refs = refs[ns + 1 :]
    if first:
        gup, grecv, idx_low = refs[:3]
        refs = refs[3:]
    else:
        gs, acc_in, hs, idx_up_out, idx_low_out, vecs = refs[:6]
        refs = refs[6:]
    grads, slopes = refs[:ns], refs[ns : 2 * ns]
    refs = refs[2 * ns :]
    if first:
        gs, acc, act_sc = refs
    else:
        out_ul, acc, act_sc = refs
    rows = z2.shape[0]
    if first:
        for r0, n in row_chunks(rows, 4):
            gs[r0 : r0 + n, :] = (
                gup[r0 : r0 + n, :].astype(F32)
                + dot(onehot(idx_low[r0 : r0 + n, :], STRIP), grecv[...])
            ).astype(BF)
    for k in range(ns):
        ub = packs[k][2 * D : 2 * D + 1, :].astype(F32)
        for r0, n in row_chunks(rows, 4):
            sl = slice(r0, r0 + n)
            u = dot(z2[sl, :], packs[k][:D, :]) + ub
            phi = 0.5 * (1.0 + lax.erf(u * np.float32(np.sqrt(0.5))))
            act = (u * phi).astype(BF)
            slope = phi + u * (jnp.exp(-0.5 * u * u) * np.float32(1 / np.sqrt(2 * np.pi)))
            slopes[k][sl, :] = slope.astype(BF)
            act_sc[sl, :] = act
            y = dot(act, packs[k][D : 2 * D, :])
            if k > 0:
                acc[sl, :] += y
            elif first:
                acc[sl, :] = y
            else:
                acc[sl, :] = y + acc_in[sl, :]
        store_blocks(grads[k], 0, dot_tn(act_sc[...], gs[...]).astype(BF), blocks)
    if first:
        return
    bd = vecs[5:6, :]
    for r0, n in row_chunks(rows, 4):
        sl = slice(r0, r0 + n)
        act_sc[sl, :] = (hs[sl, :] + acc[sl, :] + bd).astype(BF)
    y = act_sc[...]
    out_ul[:STRIP, :] = dot(onehot(idx_up_out[...], rows), y).astype(BF)
    out_ul[STRIP:, :] = dot(onehot(idx_low_out[...], rows), y).astype(BF)


def mlp_bwd_kernel(order, first, blocks, *refs):
    refs = list(refs)
    packs = refs[:2]
    z2, gs, slopes = refs[2], refs[3], refs[4:6]
    refs = refs[6:]
    if not first:
        acc_in, hs, vecs = refs[:3]
        refs = refs[3:]
    grads, dub = refs[:2]
    refs = refs[2:]
    if first:
        acc, du_sc = refs
    else:
        dh_out, dhb_out, vec_out, acc, du_sc = refs
    rows = z2.shape[0]
    for k in range(2):
        dub_total = jnp.zeros((1, D), F32)
        for r0, n in row_chunks(rows, 4):
            sl = slice(r0, r0 + n)
            ga = dot_nt(gs[sl, :], packs[k][D : 2 * D, :])
            du = (slopes[k][sl, :].astype(F32) * ga).astype(BF)
            du_sc[sl, :] = du
            dub_total += jnp.sum(du.astype(F32), axis=0, keepdims=True)
            z = dot_nt(du, packs[k][:D, :])
            if k > 0:
                acc[sl, :] += z
            elif first:
                acc[sl, :] = z
            else:
                acc[sl, :] = z + acc_in[sl, :]
        for c in range(D // LANES):
            line = k * (D // LANES) + c
            dub[line : line + 1, :] = dub_total[:, c * LANES : (c + 1) * LANES]
        store_blocks(grads, k * D, dot_tn(z2[...], du_sc[...]).astype(BF), blocks)
    if first:
        return
    g2 = vecs[2:3, :]
    sums = [jnp.zeros((1, D), F32) for _ in range(4)]
    for r0, n in row_chunks(rows, 4):
        sl = slice(r0, r0 + n)
        dz = acc[sl, :]
        g = gs[sl, :].astype(F32)
        nrm, inv = norm_stats(hs[sl, :])
        dh = g + norm_back(dz, nrm, inv, g2)
        dh_out[sl, :] = dh
        dhb_out[sl, :] = dh.astype(BF)
        for i, term in enumerate((dz * nrm, dz, g, dh)):
            sums[i] = sums[i] + jnp.sum(term, axis=0, keepdims=True)
    for i in range(4):
        for c in range(D // LANES):
            line = i * (D // LANES) + c
            vec_out[line : line + 1, :] = sums[i][:, c * LANES : (c + 1) * LANES]


def attn_bwd_kernel(ns, first, last, nwl, blocks, dhb, z1, *refs):
    refs = list(refs)
    o, qkv, probs, packs = (refs[i * ns : (i + 1) * ns] for i in range(4))
    refs = refs[4 * ns :]
    back, groups = refs[:2]
    refs = refs[2:]
    dz_in = None if first else refs.pop(0)
    if last:
        x_ref, dh, vecs, idx_up_out, idx_low_out, vec_mlp, small13, small2, dub13, dub02 = refs[:10]
        refs = refs[10:]
    if last:
        grads, out_ul, small_out, dpos = refs[:4]
        refs = refs[4:]
    else:
        grads, dpos = refs[:2]
        refs = refs[2:]
    dz, dsum, do_sc, dx_sc = refs
    rows = dhb.shape[0]
    scale = HD ** (-0.5)
    for k in range(ns):
        total = None
        for c in range(D // LANES):
            w = packs[k][3 * D + c * LANES : 3 * D + (c + 1) * LANES, :]
            term = dot_nt(dhb[:, c * LANES : (c + 1) * LANES], w)
            total = term if total is None else total + term
        do_sc[k] = total.astype(BF)
        gp = dot_tn(o[k][...], dhb[...]).astype(BF)
        gp = jnp.concatenate([gp[:, c * LANES : (c + 1) * LANES] for c in range(D // LANES)], axis=0)
        store_blocks(grads, k * D, gp, blocks, (3 * LANES, 4 * LANES))
        dx_sc[k, nwl * WROW :, :] = jnp.zeros((rows - nwl * WROW, 3 * LANES), BF)
    dsum[...] = jnp.zeros(dsum.shape, F32)

    def window(j, carry):
        masks = head_masks()
        base = pl.multiple_of(j * WROW, 16)
        for k in range(ns):
            q = stacked(qkv[k][0, pl.ds(base, WROW), :], masks)
            key = qkv[k][1, pl.ds(base, LANES), :]
            v = qkv[k][2, pl.ds(base, LANES), :]
            do = stacked(do_sc[k, pl.ds(base, WROW), :], masks)
            p = probs[k][j]
            p32 = p.astype(F32)
            pdp = p32 * dot_nt(do, v)
            ds = (pdp - p32 * jnp.sum(pdp, axis=-1, keepdims=True)).astype(BF)
            dsum[k] += ds.astype(F32)
            dv = dot_tn(p, do)
            dk = dot_tn(ds, q)
            dq = unstacked(dot(ds, key), masks) * scale
            dx_sc[k, pl.ds(base, WROW), :LANES] = dq.astype(BF)
            dx_sc[k, pl.ds(base, WROW), LANES : 2 * LANES] = dk[:WROW].astype(BF)
            dx_sc[k, pl.ds(base, WROW), 2 * LANES :] = dv[:WROW].astype(BF)
        return carry

    lax.fori_loop(0, nwl, window, 0)
    for k in range(ns):
        store_blocks(grads, k * D, dot_tn(z1[...], dx_sc[k]).astype(BF), blocks, (0, 3 * LANES))
        high = dsum[k].astype(BF)
        low = (dsum[k] - high.astype(F32)).astype(BF)
        lanes = dot(high, back[...]) + dot(low, back[...])
        turned = jnp.concatenate(
            [
                pltpu.roll(lanes[h * WROW : (h + 1) * WROW, :], 0, 1, stride=1, stride_axis=0)
                for h in range(HEADS_HERE)
            ],
            axis=0,
        )
        high = turned.astype(BF)
        low = (turned - high.astype(F32)).astype(BF)
        summed = dot(groups[...], high) + dot(groups[...], low)
        total = summed[:8, :]
        for a in range(1, WIN):
            total = total + pltpu.roll(summed[a * 8 : (a + 1) * 8, :], (SPAN - WIN) * a, 1)
        per = 16
        for h in range(HEADS_HERE):
            for c in range(TABLE_PAD // LANES):
                line = k * per + h * (TABLE_PAD // LANES) + c
                dpos[line : line + 1, :] = total[h : h + 1, c * LANES : (c + 1) * LANES]
        for i, m in enumerate((0, 2)):
            part = dx_sc[k, :, m * LANES : (m + 1) * LANES].astype(F32)
            line = k * per + 12 + i
            dpos[line : line + 1, :] = jnp.sum(part, axis=0, keepdims=True)
        dpos[k * per + 14 : (k + 1) * per, :] = jnp.zeros((2, LANES), F32)
    sums = [jnp.zeros((1, D), F32) for _ in range(2)]
    for r0, n in row_chunks(rows, 4):
        sl = slice(r0, r0 + n)
        total = None if first else dz_in[sl, :]
        for k in range(ns):
            for m in range(3):
                term = dot_nt(
                    dx_sc[k, sl, m * LANES : (m + 1) * LANES], packs[k][m * D : (m + 1) * D, :]
                )
                total = term if total is None else total + term
        if not last:
            dz[sl, :] = total
            continue
        nrm, inv = norm_stats(x_ref[sl, :].astype(F32))
        dz[sl, :] = (dh[sl, :] + norm_back(total, nrm, inv, vecs[0:1, :])).astype(BF)
        sums[0] = sums[0] + jnp.sum(total * nrm, axis=0, keepdims=True)
        sums[1] = sums[1] + jnp.sum(total, axis=0, keepdims=True)
    if not last:
        return
    n_mlp = vec_mlp.shape[0]
    small_out[:n_mlp, :] = vec_mlp[...]
    for i in range(2):
        for c in range(D // LANES):
            line = n_mlp + i * (D // LANES) + c
            small_out[line : line + 1, :] = sums[i][:, c * LANES : (c + 1) * LANES]
    t = lax.axis_index("tp")
    pieces = [
        (dpos[...], dub02[:4, :]),
        (small13[:16, :], dub13[:4, :]),
        (small2[...], dub02[4:, :]),
        (small13[16:, :], dub13[4:, :]),
    ]
    for s, (lines, dub) in enumerate(pieces):
        at = pl.multiple_of(SMALL_VECS + jnp.bitwise_xor(t, s) * SMALL_SHARD, 8)
        both = jnp.concatenate([lines, dub, jnp.zeros((4, LANES), F32)], axis=0)
        small_out[pl.ds(at, SMALL_SHARD), :] = both
    out_ul[:STRIP, :] = dot(onehot(idx_up_out[...], rows), dz[...]).astype(BF)
    out_ul[STRIP:, :] = dot(onehot(idx_low_out[...], rows), dz[...]).astype(BF)


def page_kernel(*refs):
    out = refs[TP]
    pw = out.shape[1]
    t = lax.axis_index("tp")
    width = pw // TP
    col = lax.broadcasted_iota(jnp.int32, (pw, 1), 0)
    hots = []
    for s in range(TP):
        v = col - width * jnp.bitwise_xor(t, s) - SHIFT
        v = jnp.where(v < 0, v + pw, v)
        v = jnp.where(v < width, v, -1000)
        hots.append(onehot(v, SEG))
    hot = jnp.concatenate(hots, axis=1)
    for r in range(WIN):
        off = STRIP + r * SEG if r < SHIFT else (r - SHIFT) * SEG
        parts = [ul[off : off + SEG, :] for ul in refs[:TP]]
        out[r] = dot(hot, jnp.concatenate(parts, axis=0)).astype(BF)


def swap_tp(x, bit):
    return lax.ppermute(x, "tp", [(i, i ^ bit) for i in range(TP)])


def swap_rows(x, bit):
    return lax.ppermute(x, "rows", [(i, i ^ bit) for i in range(lax.axis_size("rows"))])


def shift_rows(x, distance):
    n = lax.axis_size("rows")
    return lax.ppermute(x, "rows", [(i, (i + distance) % n) for i in range(n)])


def row_bits():
    n = lax.axis_size("rows")
    bits = []
    while 1 << len(bits) < n:
        bits.append(1 << len(bits))
    return bits


def blocks_for(rows):
    blocks = 1
    while 2 * blocks <= lax.axis_size("rows") and rows % (2 * blocks) == 0 and rows // (2 * blocks) >= 16:
        blocks *= 2
    return blocks


def added(arrays):
    total = arrays[0].astype(F32)
    for extra in arrays[1:]:
        total = total + extra.astype(F32)
    return total.astype(BF)


def scatter_step(arrays, bit, blocks):
    total = added(arrays)
    if bit < blocks:
        half = total.shape[0] // 2
        return [total[:half], swap_rows(total[half:], bit)]
    return [total, swap_rows(total, bit)]


def gather_step(total, bit):
    return jnp.concatenate([total, swap_rows(total, bit)], axis=0)


def finish_kernel(blocks, n_in, *refs):
    ins, outs = refs[:n_in], refs[n_in:]
    part = ins[0].shape[0] * n_in // blocks
    each = blocks // n_in
    mine = my_block(blocks)
    both = len(outs) == 2
    half = part // 2
    for p in range(blocks):
        b = jnp.bitwise_xor(mine, p)
        piece = ins[p // each][(p % each) * part : (p % each + 1) * part, :].astype(F32)
        if both:
            at = pl.ds(pl.multiple_of(b * half, half), half)
            outs[0][at, :] = piece[:half]
            outs[1][at, :] = piece[half:]
        else:
            outs[2][pl.ds(pl.multiple_of(b * part, part), part), :] = piece
    if both:
        return
    qkv, proj, whole = outs
    for c in range(D // LANES):
        if c < 3:
            qkv[c] = whole[:, c * LANES : (c + 1) * LANES]
        proj[:, c * LANES : (c + 1) * LANES] = whole[c * LANES : (c + 1) * LANES, 3 * LANES :]


def finish(pieces, blocks, name):
    attn = name == "finish_attn"
    return call(
        functools.partial(finish_kernel, blocks, len(pieces)),
        pieces,
        [((3, D, LANES), F32), ((LANES, D), F32)] if attn else [((D, D), F32)] * 2,
        scratch=[pltpu.VMEM((D, D), F32)] if attn else [],
        name=name,
    )


def small_step(x, hop):
    axis, bit = hop
    return x + (swap_tp(x, bit) if axis == "tp" else swap_rows(x, bit))


def page(pieces, page_shape, name):
    return call(page_kernel, pieces, [(page_shape, BF)], name=name)[0]


def per_device(
    patches,
    cotangent,
    page_bounds,
    attn_gain,
    attn_shift,
    qkv_weight,
    qv_bias,
    pos_table,
    proj_weight,
    proj_bias,
    mlp_gain,
    mlp_shift,
    up_weight,
    up_bias,
    down_weight,
    down_bias,
):
    t = lax.axis_index("tp")
    pw = patches.shape[1]
    nwl = pw // WIN // TP
    width = nwl * WIN
    rows = rows_of(nwl)
    idx_strip, idx_win_up, idx_win_low, idx_out_up, idx_out_low = index_tables(nwl)
    em_np, fm_np, spread_np, back_np, groups_np = attention_tables()
    spread, back, groups = (jnp.asarray(a, BF) for a in (spread_np, back_np, groups_np))
    bits = row_bits()
    blocks = blocks_for(D)

    args = [patches, idx_strip, qkv_weight, proj_weight, pos_table.T, qv_bias]
    strip_x, pack1 = windowed_call(
        functools.partial(head_kernel, width),
        args,
        [half_spec(patches, 0)] + [whole_spec(a) for a in args[1:]],
        [((STRIP, D), BF), ((PACK1, LANES), BF)],
        "head",
    )
    recv_x = shift_rows(strip_x, -1)
    pack1_x = swap_tp(pack1, 2)
    pack1_c = swap_tp(pack1, 1)
    field_g = after(cotangent, strip_x)
    args = [field_g, patches, cotangent, idx_strip, idx_win_up, up_weight, down_weight, up_bias[None]]
    strip_g, up_x, up_g, pack2 = windowed_call(
        functools.partial(rest_kernel, width),
        args,
        [half_spec(cotangent, 0), half_spec(patches, 1), half_spec(cotangent, 1)]
        + [whole_spec(a) for a in args[3:]],
        [((STRIP, D), BF), ((rows, D), BF), ((rows, D), BF), ((PACK2, D), BF)],
        "rest",
    )
    recv_g = shift_rows(strip_g, -1)
    vecs = jnp.stack([attn_gain, attn_shift, mlp_gain, mlp_shift, proj_bias, down_bias]).astype(F32)
    pack1_cx = swap_tp(after(pack1_x, strip_g, recv_x), 1)
    packs1 = [pack1, pack1_c, pack1_x, pack1_cx]
    pack2 = after(pack2, pack1_x)
    pack2_x = swap_tp(pack2, 2)
    pack2_c = swap_tp(pack2, 1)

    outs = call(
        functools.partial(attn_fwd_kernel, nwl),
        [up_x, recv_x, idx_win_low, vecs, em_np, fm_np, spread] + packs1,
        [((3, rows, LANES), BF)] * TP
        + [((nwl, STACK, LANES), BF)] * TP
        + [((rows, LANES), BF)] * TP
        + [((rows, D), BF), ((rows, D), BF), ((rows, D), F32), ((rows, D), BF)],
        scratch=[
            pltpu.VMEM((TP, STACK, LANES), F32),
            pltpu.VMEM((TOKENS * TP * HEADS_HERE, 2 * LANES), BF),
            pltpu.VMEM((WROW * TP * HEADS_HERE, LANES), F32),
            pltpu.VMEM((D, D), BF),
        ],
        scalars=[page_bounds],
        name="attn_fwd",
    )
    qkv, probs, o = outs[:TP], outs[TP : 2 * TP], outs[2 * TP : 3 * TP]
    x_win, z1, hs, z2 = outs[3 * TP :]

    def mlp_fwd(shards, packs, first, extra):
        ns = len(shards)
        outs = [((D, D), BF)] * ns + [((rows, D), BF)] * ns
        outs += [((rows, D), BF), ((rows, D), F32)] if first else [((2 * STRIP, D), BF)]
        scratch = [pltpu.VMEM((rows, D), BF)]
        return call(
            functools.partial(mlp_fwd_kernel, shards, first, blocks),
            packs + [z2] + extra,
            outs,
            scratch=scratch if first else [pltpu.VMEM((rows, D), F32)] + scratch,
            name="mlp_fwd_a" if first else "mlp_fwd_b",
        )

    gd0, gd1, slope0, slope1, gs, acc_y = mlp_fwd(
        (0, 1), [pack2, pack2_c], True, [up_g, recv_g, idx_win_low]
    )
    got_d1 = swap_tp(gd1, 1)
    pack2_cx = swap_tp(after(pack2_x, acc_y), 1)
    packs2 = [pack2, pack2_c, pack2_x, pack2_cx]
    gd2, gd3, slope2, slope3, out_ul = mlp_fwd(
        (2, 3), packs2[2:], False, [gs, acc_y, hs, idx_out_up, idx_out_low, vecs]
    )
    got_d3 = swap_tp(gd3, 1)
    lower_y = shift_rows(out_ul[STRIP:], 1)
    slopes = [slope0, slope1, slope2, slope3]

    def mlp_bwd(shards, first, z2, extra):
        outs = [((2 * D, D), BF), ((2 * D // LANES, LANES), F32)]
        if first:
            outs += [((rows, D), F32)]
        else:
            outs += [((rows, D), F32), ((rows, D), BF), ((4 * D // LANES, LANES), F32)]
        scratch = [pltpu.VMEM((rows, D), BF)]
        return call(
            functools.partial(mlp_bwd_kernel, shards, first, blocks),
            [packs2[s] for s in shards] + [z2, gs] + [slopes[s] for s in shards] + extra,
            outs,
            scratch=scratch if first else [pltpu.VMEM((rows, D), F32)] + scratch,
            name="mlp_bwd_a" if first else "mlp_bwd_b",
        )

    gu13, dub13, acc_z = mlp_bwd((1, 3), True, z2, [])
    got_u13 = swap_tp(gu13, 1)
    across_d = added([gd2, got_d3])
    got_dx = swap_tp(across_d, 2)
    gu02, dub02, dh, dhb, vec_mlp = mlp_bwd((0, 2), False, after(z2, across_d), [acc_z, hs, vecs])
    across_u = added([gu02[D:], got_u13[D:]])
    got_ux = swap_tp(across_u, 2)

    def attn_bwd(shards, dhb, extra, last):
        ns = len(shards)
        outs = [((ns * D, D), BF)]
        if last:
            outs += [((2 * STRIP, D), BF), ((SMALL_VECS + TP * SMALL_SHARD, LANES), F32)]
        else:
            outs += [((ns * 16, LANES), F32)]
        scratch = [
            pltpu.VMEM((ns, STACK, LANES), F32),
            pltpu.VMEM((ns, rows, LANES), BF),
            pltpu.VMEM((ns, rows, 3 * LANES), BF),
        ]
        if last:
            scratch = [pltpu.VMEM((16, LANES), F32), pltpu.VMEM((rows, D), BF)] + scratch
        else:
            outs += [((rows, D), F32)]
        return call(
            functools.partial(attn_bwd_kernel, ns, not extra, last, nwl, blocks),
            [dhb, z1]
            + [a[s] for a in (o, qkv, probs, packs1) for s in shards]
            + [back, groups]
            + extra,
            outs,
            scratch=scratch,
            name="attn_bwd_" + "".join(map(str, shards)),
        )

    a13, small13, dz = attn_bwd((1, 3), after(dhb, across_u), [], False)
    got_a13 = swap_tp(a13, 1)
    page_own = jnp.concatenate([after(out_ul, a13)[:STRIP], lower_y], axis=0)
    from_x = swap_tp(page_own, 2)
    from_c = swap_tp(page_own, 1)
    down = scatter_step([gd0, got_d1, got_dx], bits[0], blocks)
    a2, small2, dz = attn_bwd((2,), after(dhb, down[0], page_own), [dz], False)
    across_a = added([a2, got_a13[D:]])
    got_ax = swap_tp(across_a, 2)
    up = scatter_step([gu02[:D], got_u13[:D], got_ux], bits[0], blocks)
    down = scatter_step(down, bits[1], blocks) if len(bits) > 1 else down
    a0, out_g, small = attn_bwd(
        (0,),
        after(dhb, across_a, up[0], down[0]),
        [dz, x_win, dh, vecs, idx_out_up, idx_out_low, vec_mlp, small13, small2, dub13, dub02],
        True,
    )

    lower_g = shift_rows(out_g[STRIP:], 1)
    attn = [a0, got_a13[:D], got_ax]
    small_bits = [("tp", 1), ("tp", 2)] + [("rows", bit) for bit in bits]
    pair = None
    for i, bit in enumerate(bits):
        attn[0] = added(attn)
        mark = attn[0]
        attn = scatter_step(attn[:1], bit, blocks)
        small = small_step(after(small, mark), small_bits.pop(0))
        if i + 1 < len(bits):
            up = scatter_step([after(up[0], mark)] + up[1:], bits[i + 1], blocks)
        if i + 2 < len(bits):
            down = scatter_step([after(down[0], mark)] + down[1:], bits[i + 2], blocks)
        if i == 0:
            from_cx = swap_tp(after(from_x, mark), 1)
        if i == 1:
            own_g = jnp.concatenate([out_g[:STRIP], after(lower_g, mark)], axis=0)
            g_x = swap_tp(own_g, 2)
            g_c = swap_tp(own_g, 1)
    down, up = after(added(down), mark), added(up)
    mlp = jnp.concatenate([down, up], axis=0)
    inner = [b for b in bits if b < blocks]
    mlp = gather_step(mlp, inner[-1])
    attn = added(attn)
    for i in reversed(range(1, len(inner))):
        small = small_step(after(small, attn), small_bits.pop(0)) if small_bits else small
        mlp_next = swap_rows(after(mlp, attn), inner[i - 1])
        attn = gather_step(attn, inner[i])
        if i > 1:
            mlp = jnp.concatenate([mlp, mlp_next], axis=0)
    while small_bits:
        small = small_step(small, small_bits.pop(0))
    g_cx = swap_tp(after(g_x, attn), 1)
    attn_next = swap_rows(attn, inner[0])
    block_out = page([page_own, from_c, from_x, from_cx], patches.shape, "page_y")
    grad_patches = page([own_g, g_c, g_x, g_cx], patches.shape, "page_g")
    grad_down, grad_up = finish([mlp, mlp_next], blocks, "finish_mlp")
    grad_qkv, grad_proj = finish([attn, attn_next], blocks, "finish_attn")

    v = small[:SMALL_VECS].reshape(6, D)
    mine = lax.dynamic_slice_in_dim(small, SMALL_VECS + t * SMALL_SHARD, SMALL_SHARD, 0)
    grad_pos_table = mine[:12].reshape(HEADS_HERE, TABLE_PAD)[:, :TABLE].T

    return (
        block_out,
        grad_patches,
        v[4],
        v[5],
        grad_qkv,
        mine[12:14],
        grad_pos_table,
        grad_proj,
        v[3],
        v[0],
        v[1],
        grad_up,
        mine[16:20].reshape(D),
        grad_down,
        v[2],
    )


def solution(mesh):
    placed = (
        P("rows", None, None),
        P("rows", None, None),
        P("rows", None),
        P(),
        P(),
        P(None, None, "tp"),
        P(None, "tp"),
        P(None, "tp"),
        P("tp", None),
        P(),
        P(),
        P(),
        P(None, "tp"),
        P("tp"),
        P("tp", None),
        P(),
    )
    return jax.shard_map(
        per_device,
        mesh=mesh,
        in_specs=placed,
        out_specs=(
            P("rows", None, None),
            P("rows", None, None),
            P(),
            P(),
            P(None, None, "tp"),
            P(None, "tp"),
            P(None, "tp"),
            P("tp", None),
            P(),
            P(),
            P(),
            P(None, "tp"),
            P("tp"),
            P("tp", None),
            P(),
        ),
        check_vma=False,
    )
```

profile of v0, /device:TPU:0, one launch (start us, length us, event | category | flops | bytes accessed | tf_op | source)
XLA Modules:
  0.0 211.3 jit_solution(17555041495791313591)
XLA Ops:
  0.7 2.8 %head.1 = (bf16[320,512]{1,0:T(8,128)(2,1)}, bf16[2080,128]{1,0:T(8,128)(2,1)}) custom-call(bf16[10,240,512]{2,1,0:T(8,128)(2,1)} %x_low.1, s32[320,1]{1,0:T(8,128)} %constant.34.clone.idx.idx_strip, bf16[3,512,128]{2,1,0:T(8,128)(2,1)} %wqkv.1, bf16[128,512]{1,0:T(8,128)(2,1)} %wproj.1, bf16[4,361]{1,0:T(4,128)(2,1)} %bitcast.17, bf16[2,128]{1,0:T(2,128)(2,1)} %bias.1), custom_call_target="tpu_custom_call" | custom-call | flops 600000000 | bytes 1024 | tf_op jit(solution)/shard_map/head/pallas_call | solution.py:188
  3.5 2.9 %collective-permute-start = (bf16[2080,128]{1,0:T(8,128)(2,1)}, bf16[2080,128]{1,0:T(8,128)(2,1)S(1)}, u32[]{:S(2)}, u32[]{:S(2)}) collective-permute-start(bf16[2080,128]{1,0:T(8,128)(2,1)} %get-tuple-element.95.refs_0_.refs_3_), channel_id=1, source_target_pairs={{0,2},{1,3},{2,0},{3,1},{4,6},{5,7},{6,4},{7,5},{8,10},{9,11},{10,... | collective-permute-start | bytes 1597448 | tf_op jit(solution)/shard_map/ppermute | solution.py:608
  6.4 4.6 %collective-permute-start.3 = (bf16[320,512]{1,0:T(8,128)(2,1)}, bf16[320,512]{1,0:T(8,128)(2,1)S(1)}, u32[]{:S(2)}, u32[]{:S(2)}) collective-permute-start(bf16[320,512]{1,0:T(8,128)(2,1)} %get-tuple-element.92), channel_id=1, source_target_pairs={{0,28},{4,0},{8,4},{12,8},{16,12},{20,16},{24,20},{28,24},{1,29},{... | collective-permute-start | bytes 983048 | tf_op jit(solution)/shard_map/ppermute | solution.py:617
  11.6 4.9 %rest.1 = (bf16[320,512]{1,0:T(8,128)(2,1)}, bf16[704,512]{1,0:T(8,128)(2,1)}, bf16[704,512]{1,0:T(8,128)(2,1)}, bf16[1040,512]{1,0:T(8,128)(2,1)}) custom-call(bf16[10,240,512]{2,1,0:T(8,128)(2,1)} %g_low.1, bf16[10,240,512]{2,1,0:T(8,128)(2,1)} %x_low.1, bf16[10,240,512]{2,1,0:T(8,128)(2,1)} %g_low.1, s32[320,1]{1,0:T(8,128)} %constant.34.clone.idx.idx_strip, ...), custom_call_target="tpu_custom_call" | custom-call | flops 1000000000 | bytes 1024 | tf_op jit(solution)/shard_map/rest/pallas_call | solution.py:188
  16.5 2.2 %collective-permute-done.refs_2_.refs_3_ = bf16[2080,128]{1,0:T(8,128)(2,1)S(1)} collective-permute-done((bf16[2080,128]{1,0:T(8,128)(2,1)}, bf16[2080,128]{1,0:T(8,128)(2,1)S(1)}, u32[]{:S(2)}, u32[]{:S(2)}) %collective-permute-start) | collective-permute-done | bytes 532512 | tf_op jit(solution)/shard_map/ppermute | solution.py:608
  18.7 1.7 collective-permute-start.1
  21.0 4.6 %collective-permute-start.6 = (bf16[320,512]{1,0:T(8,128)(2,1)}, bf16[320,512]{1,0:T(8,128)(2,1)}, u32[]{:S(2)}, u32[]{:S(2)}) collective-permute-start(bf16[320,512]{1,0:T(8,128)(2,1)} %get-tuple-element.98), channel_id=1, source_target_pairs={{0,28},{4,0},{8,4},{12,8},{16,12},{20,16},{24,20},{28,24},{1,29},{... | collective-permute-start | bytes 983048 | tf_op jit(solution)/shard_map/ppermute | solution.py:617
  26.3 14.5 %attn_fwd.1 = (bf16[3,704,128]{2,1,0:T(8,128)(2,1)}, bf16[3,704,128]{2,1,0:T(8,128)(2,1)}, bf16[3,704,128]{2,1,0:T(8,128)(2,1)}, bf16[3,704,128]{2,1,0:T(8,128)(...) custom-call(s32[1,2]{1,0:T(1,128)} %bounds.1, ...), custom_call_target="tpu_custom_call" | custom-call | flops 2800000000 | bytes 1024 | tf_op jit(solution)/shard_map/attn_fwd/pallas_call | solution.py:135
  40.8 1.0 copy-done.26
  41.8 7.9 %mlp_fwd_a.1 = (bf16[512,512]{1,0:T(8,128)(2,1)}, bf16[512,512]{1,0:T(8,128)(2,1)}, bf16[704,512]{1,0:T(8,128)(2,1)}, bf16[704,512]{1,0:T(8,128)(2,1)}, bf16[704,512]{1,0:T(8,128)(2,1)}, /*index=5*/f32[704,512]{1,0:T(8,128)}) custom-call(bf16[1040,512]{1,0:T(8,128)(2,1)} %get-tuple-element.96.refs_0_, bf16[1040,512]{1,0:T(8,128)(2,1)} %copy-done.26, ...), custom_call_target="tpu_custom_call" | custom-call | flops 1600000000 | bytes 1024 | tf_op jit(solution)/shard_map/mlp_fwd_a/pallas_call | solution.py:135
  49.8 2.7 %collective-permute-done.7.refs_1_ = bf16[1040,512]{1,0:T(8,128)(2,1)S(1)} collective-permute-done((bf16[1040,512]{1,0:T(8,128)(2,1)S(1)}, bf16[1040,512]{1,0:T(8,128)(2,1)S(1)}, u32[]{:S(2)}, u32[]{:S(2)}) %collective-permute-start.7) | collective-permute-done | bytes 1064992 | tf_op jit(solution)/shard_map/ppermute | solution.py:608
  52.4 1.0 copy-done.3
  53.4 8.2 %mlp_fwd_b.1 = (bf16[512,512]{1,0:T(8,128)(2,1)}, bf16[512,512]{1,0:T(8,128)(2,1)}, bf16[704,512]{1,0:T(8,128)(2,1)}, bf16[704,512]{1,0:T(8,128)(2,1)}, bf16[640,512]{1,0:T(8,128)(2,1)}) custom-call(bf16[1040,512]{1,0:T(8,128)(2,1)} %copy-done, bf16[1040,512]{1,0:T(8,128)(2,1)} %copy-done.3, bf16[704,512]{1,0:T(8,128)(2,1)} %get-tuple-element.109.refs_2_, ...), custom_call_target="tpu_custom_call" | custom-call | flops 1600000000 | bytes 1024 | tf_op jit(solution)/shard_map/mlp_fwd_b/pallas_call | solution.py:135
  61.7 7.9 %mlp_bwd_a.1 = (bf16[1024,512]{1,0:T(8,128)(2,1)}, f32[8,128]{1,0:T(8,128)}, f32[704,512]{1,0:T(8,128)}) custom-call(bf16[1040,512]{1,0:T(8,128)(2,1)} %copy-done.26, bf16[1040,512]{1,0:T(8,128)(2,1)} %copy-done.3, bf16[704,512]{1,0:T(8,128)(2,1)} %get-tuple-element.109.refs_2_, bf16[704,512]{1,0:T(8,128)(2,1)} %get-tuple-element.104.refs_3_, ...), custom_call_target="tpu_custom_call" | custom-call | flops 1600000000 | bytes 1024 | tf_op jit(solution)/shard_map/mlp_bwd_a/pallas_call | solution.py:135
  70.5 2.4 %collective-permute-done.8 = bf16[512,512]{1,0:T(8,128)(2,1)S(1)} collective-permute-done((bf16[512,512]{1,0:T(8,128)(2,1)S(1)}, bf16[512,512]{1,0:T(8,128)(2,1)S(1)}, u32[]{:S(2)}, u32[]{:S(2)}) %collective-permute-start.8) | collective-permute-done | bytes 524320 | tf_op jit(solution)/shard_map/ppermute | solution.py:608
  73.7 9.2 %mlp_bwd_b.1 = (bf16[1024,512]{1,0:T(8,128)(2,1)}, f32[8,128]{1,0:T(8,128)}, f32[704,512]{1,0:T(8,128)}, bf16[704,512]{1,0:T(8,128)(2,1)}, f32[16,128]{1,0:T(8,128)}) custom-call(bf16[1040,512]{1,0:T(8,128)(2,1)} %get-tuple-element.96.refs_0_, bf16[1040,512]{1,0:T(8,128)(2,1)} %copy-done, bf16[704,512]{1,0:T(8,128)(2,1)} %get-tuple-element.109.refs_2_, ...), custom_call_target="tpu_custom_call" | custom-call | flops 1800000000 | bytes 1024 | tf_op jit(solution)/shard_map/mlp_bwd_b/pallas_call | solution.py:135
  82.9 1.2 add_convert_fusion.4
  84.0 1.6 collective-permute-start.16
  85.6 13.1 %attn_bwd_13.1 = (bf16[1024,512]{1,0:T(8,128)(2,1)}, f32[32,128]{1,0:T(8,128)}, f32[704,512]{1,0:T(8,128)}) custom-call(bf16[704,512]{1,0:T(8,128)(2,1)} %get-tuple-element.136.dhb, bf16[704,512]{1,0:T(8,128)(2,1)} %get-tuple-element.119.z1, bf16[704,128]{1,0:T(8,128)(2,1)} %get-tuple-element.120.refs_0_, bf16[704,128]{1,0:T(8,128)(2,1)} %get-tuple-element.121.refs_1_, ...), custom_call_target="tpu_custom_call" | custom-call | flops 2600000000 | bytes 1024 | tf_op jit(solution)/shard_map/attn_bwd_13/pallas_call | solution.py:135
  99.7 9.0 %attn_bwd_2.1 = (bf16[512,512]{1,0:T(8,128)(2,1)}, f32[16,128]{1,0:T(8,128)}, f32[704,512]{1,0:T(8,128)}) custom-call(bf16[704,512]{1,0:T(8,128)(2,1)} %get-tuple-element.136.dhb, bf16[704,512]{1,0:T(8,128)(2,1)} %get-tuple-element.119.z1, bf16[704,128]{1,0:T(8,128)(2,1)} %get-tuple-element.131.refs_0_, bf16[3,704,128]{2,1,0:T(8,128)(2,1)} %get-tuple-element.132.refs_1_, ...), custom_call_target="tpu_custom_call" | custom-call | flops 1800000000 | bytes 1024 | tf_op jit(solution)/shard_map/attn_bwd_2/pallas_call | solution.py:135
  108.8 1.1 collective-permute-start.35
  110.3 1.6 collective-permute-start.18
  111.9 2.1 collective-permute-start.37
  114.0 10.5 %attn_bwd_0.1 = (bf16[512,512]{1,0:T(8,128)(2,1)}, bf16[640,512]{1,0:T(8,128)(2,1)}, f32[120,128]{1,0:T(8,128)}) custom-call(bf16[704,512]{1,0:T(8,128)(2,1)} %get-tuple-element.136.dhb, bf16[704,512]{1,0:T(8,128)(2,1)} %get-tuple-element.119.z1, bf16[704,128]{1,0:T(8,128)(2,1)} %get-tuple-element.137.refs_0_, ...), custom_call_target="tpu_custom_call" | custom-call | flops 2200000000 | bytes 1024 | tf_op jit(solution)/shard_map/attn_bwd_0/pallas_call | solution.py:135
  124.5 1.2 fusion
  126.0 1.5 collective-permute-done.18
  127.8 0.9 collective-permute-start.36
  128.7 1.0 collective-permute-start.21
  129.8 1.1 collective-permute-done.29
  131.0 2.5 %collective-permute-start.38 = (bf16[128,512]{1,0:T(8,128)(2,1)S(1)}, bf16[128,512]{1,0:T(8,128)(2,1)S(1)}, u32[]{:S(2)}, u32[]{:S(2)}) collective-permute-start(bf16[128,512]{1,0:T(8,128)(2,1)S(1)} %get-tuple-element.176), channel_id=1, source_target_pairs={{0,8},{4,12},{8,0},{12,4},{16,24},{20,28},{24,16},{28,20},{1,9},{5... | collective-permute-start | bytes 393224 | tf_op jit(solution)/shard_map/ppermute | solution.py:612
  133.5 9.5 %collective-permute-done.21 = bf16[256,512]{1,0:T(8,128)(2,1)S(1)} collective-permute-done((bf16[256,512]{1,0:T(8,128)(2,1)S(1)}, bf16[256,512]{1,0:T(8,128)(2,1)S(1)}, u32[]{:S(2)}, u32[]{:S(2)}) %collective-permute-start.21) | collective-permute-done | bytes 262176 | tf_op jit(solution)/shard_map/ppermute | solution.py:612
  143.5 0.9 collective-permute-start.30
  144.5 1.1 collective-permute-start.23
  145.6 2.6 %collective-permute-done.30 = f32[120,128]{1,0:T(8,128)S(1)} collective-permute-done((f32[120,128]{1,0:T(8,128)S(1)}, f32[120,128]{1,0:T(8,128)S(1)}, u32[]{:S(2)}, u32[]{:S(2)}) %collective-permute-start.30) | collective-permute-done | bytes 61472 | tf_op jit(solution)/shard_map/ppermute | solution.py:608
  148.3 1.4 collective-permute-done.24
  149.7 1.5 collective-permute-start.25
  151.3 4.2 %collective-permute-done.31 = f32[120,128]{1,0:T(8,128)S(1)} collective-permute-done((f32[120,128]{1,0:T(8,128)S(1)}, f32[120,128]{1,0:T(8,128)S(1)}, u32[]{:S(2)}, u32[]{:S(2)}) %collective-permute-start.31) | collective-permute-done | bytes 61472 | tf_op jit(solution)/shard_map/ppermute | solution.py:612
  155.5 0.6 add.92
  156.1 1.5 collective-permute-start.26
  157.7 1.0 collective-permute-start.32
  158.7 0.7 pad_maximum_fusion.6
  159.3 2.5 %collective-permute-start.40 = (bf16[128,512]{1,0:T(8,128)(2,1)}, bf16[128,512]{1,0:T(8,128)(2,1)}, u32[]{:S(2)}, u32[]{:S(2)}) collective-permute-start(bf16[128,512]{1,0:T(8,128)(2,1)} %pad_maximum_fusion.6), channel_id=1, source_target_pairs={{0,16},{4,20},{8,24},{12,28},{16,0},{20,4},{24,8},{28,12},{1,17},{... | collective-permute-start | bytes 393224 | tf_op jit(solution)/shard_map/ppermute | solution.py:612
  161.9 1.0 collective-permute-done.32
  162.9 0.9 add.93
  163.8 0.7 pad_maximum_fusion.5
  165.0 1.9 collective-permute-done.40
  166.9 1.2 collective-permute-start.33
  168.1 1.6 pad_maximum_fusion.4
  169.7 3.7 %collective-permute-done.33 = f32[120,128]{1,0:T(8,128)S(1)} collective-permute-done((f32[120,128]{1,0:T(8,128)S(1)}, f32[120,128]{1,0:T(8,128)S(1)}, u32[]{:S(2)}, u32[]{:S(2)}) %collective-permute-start.33) | collective-permute-done | bytes 61472 | tf_op jit(solution)/shard_map/ppermute | solution.py:612
  174.5 1.3 constant_dynamic-slice_fusion.1
  175.8 0.9 pad_maximum_fusion.3.refs_0_
  177.3 3.2 %collective-permute-done.41 = bf16[256,512]{1,0:T(8,128)(2,1)} collective-permute-done((bf16[256,512]{1,0:T(8,128)(2,1)}, bf16[256,512]{1,0:T(8,128)(2,1)}, u32[]{:S(2)}, u32[]{:S(2)}) %collective-permute-start.41) | collective-permute-done | bytes 262176 | tf_op jit(solution)/shard_map/ppermute | solution.py:612
  180.5 1.0 pad_maximum_fusion.2.refs_0_
  181.6 1.5 slice_bitcast_fusion.1
  183.1 2.0 collective-permute-start.34
  185.7 4.0 %page_y.1 = bf16[10,240,512]{2,1,0:T(8,128)(2,1)} custom-call(bf16[640,512]{1,0:T(8,128)(2,1)} %copy-done.1, bf16[640,512]{1,0:T(8,128)(2,1)} %copy-done.7, bf16[640,512]{1,0:T(8,128)(2,1)} %copy-done.5, bf16[640,512]{1,0:T(8,128)(2,1)} %collective-permute-done.19.refs_3_), custom_call_target="tpu_custom_call" | custom-call | flops 800000000 | bytes 1024 | tf_op jit(solution)/shard_map/page_y/pallas_call | solution.py:135
  189.7 9.6 %collective-permute-done.34.refs_1_ = bf16[256,512]{1,0:T(8,128)(2,1)S(1)} collective-permute-done((bf16[256,512]{1,0:T(8,128)(2,1)S(1)}, bf16[256,512]{1,0:T(8,128)(2,1)S(1)}, u32[]{:S(2)}, u32[]{:S(2)}) %collective-permute-start.34) | collective-permute-done | bytes 262176 | tf_op jit(solution)/shard_map/ppermute | solution.py:612
  199.2 0.7 copy-done.33
  199.9 2.2 %finish_attn.1 = (f32[3,512,128]{2,1,0:T(8,128)}, f32[128,512]{1,0:T(8,128)}) custom-call(bf16[256,512]{1,0:T(8,128)(2,1)} %copy-done.16, bf16[256,512]{1,0:T(8,128)(2,1)} %copy-done.33), custom_call_target="tpu_custom_call" | custom-call | flops 400000000 | bytes 1024 | tf_op jit(solution)/shard_map/finish_attn/pallas_call | solution.py:135
  202.1 0.8 copy-done.30
  202.9 2.7 %finish_mlp.1 = (f32[512,512]{1,0:T(8,128)}, f32[512,512]{1,0:T(8,128)}) custom-call(bf16[512,512]{1,0:T(8,128)(2,1)} %copy-done.13, bf16[512,512]{1,0:T(8,128)(2,1)} %copy-done.30), custom_call_target="tpu_custom_call" | custom-call | flops 400000000 | bytes 1024 | tf_op jit(solution)/shard_map/finish_mlp/pallas_call | solution.py:135
  205.6 0.8 copy-done.8
  206.4 0.8 copy-done.9
  207.3 4.0 %page_g.1 = bf16[10,240,512]{2,1,0:T(8,128)(2,1)} custom-call(bf16[640,512]{1,0:T(8,128)(2,1)} %copy-done.2, bf16[640,512]{1,0:T(8,128)(2,1)} %copy-done.8, bf16[640,512]{1,0:T(8,128)(2,1)} %copy-done.6, bf16[640,512]{1,0:T(8,128)(2,1)} %copy-done.9), custom_call_target="tpu_custom_call" | custom-call | flops 800000000 | bytes 1024 | tf_op jit(solution)/shard_map/page_g/pallas_call | solution.py:135
  (157 shorter events, 9.4 us)
Async XLA Ops:
  0.6 10.3 %copy-start.19 = (bf16[512]{0:T(512)(128)(2,1)S(1)}, bf16[512]{0:T(512)(128)(2,1)}, u32[]{:S(2)}) copy-start(bf16[512]{0:T(512)(128)(2,1)} %param.39) | copy-start | bytes 3076
  3.5 15.2 %collective-permute-start = (bf16[2080,128]{1,0:T(8,128)(2,1)}, bf16[2080,128]{1,0:T(8,128)(2,1)S(1)}, u32[]{:S(2)}, u32[]{:S(2)}) collective-permute-start(bf16[2080,128]{1,0:T(8,128)(2,1)} %get-tuple-element.95.refs_0_.refs_3_), channel_id=1, source_target_pairs={{0,2},{1,3},{2,0},{3,1},{4,6},{5,7},{6,4},{7,5},{8,10},{9,11},{10,... | collective-permute-start | bytes 1597448 | tf_op jit(solution)/shard_map/ppermute | solution.py:608
  6.4 14.3 %collective-permute-start.3 = (bf16[320,512]{1,0:T(8,128)(2,1)}, bf16[320,512]{1,0:T(8,128)(2,1)S(1)}, u32[]{:S(2)}, u32[]{:S(2)}) collective-permute-start(bf16[320,512]{1,0:T(8,128)(2,1)} %get-tuple-element.92), channel_id=1, source_target_pairs={{0,28},{4,0},{8,4},{12,8},{16,12},{20,16},{24,20},{28,24},{1,29},{... | collective-permute-start | bytes 983048 | tf_op jit(solution)/shard_map/ppermute | solution.py:617
  11.5 8.9 %copy-start.27 = (bf16[2080,128]{1,0:T(8,128)(2,1)S(1)}, bf16[2080,128]{1,0:T(8,128)(2,1)}, u32[]{:S(2)}) copy-start(bf16[2080,128]{1,0:T(8,128)(2,1)} %get-tuple-element.95.refs_0_.refs_3_) | copy-start | bytes 1597444
  11.5 14.0 %copy-start.20 = (bf16[512]{0:T(512)(128)(2,1)S(1)}, bf16[512]{0:T(512)(128)(2,1)}, u32[]{:S(2)}) copy-start(bf16[512]{0:T(512)(128)(2,1)} %param.29) | copy-start | bytes 3076
  11.6 14.0 %copy-start.21 = (bf16[512]{0:T(512)(128)(2,1)S(1)}, bf16[512]{0:T(512)(128)(2,1)}, u32[]{:S(2)}) copy-start(bf16[512]{0:T(512)(128)(2,1)} %param.30) | copy-start | bytes 3076
  11.6 14.0 %copy-start.22 = (bf16[512]{0:T(512)(128)(2,1)S(1)}, bf16[512]{0:T(512)(128)(2,1)}, u32[]{:S(2)}) copy-start(bf16[512]{0:T(512)(128)(2,1)} %param.36) | copy-start | bytes 3076
  11.6 14.0 %copy-start.23 = (bf16[512]{0:T(512)(128)(2,1)S(1)}, bf16[512]{0:T(512)(128)(2,1)}, u32[]{:S(2)}) copy-start(bf16[512]{0:T(512)(128)(2,1)} %param.37) | copy-start | bytes 3076
  11.6 14.0 %copy-start.24 = (bf16[512]{0:T(512)(128)(2,1)S(1)}, bf16[512]{0:T(512)(128)(2,1)}, u32[]{:S(2)}) copy-start(bf16[512]{0:T(512)(128)(2,1)} %param.35) | copy-start | bytes 3076
  11.6 14.1 %copy-start.25 = (bf16[512]{0:T(512)(128)(2,1)S(1)}, bf16[512]{0:T(512)(128)(2,1)}, u32[]{:S(2)}) copy-start(bf16[512]{0:T(512)(128)(2,1)} %param.41) | copy-start | bytes 3076
  18.7 7.6 %copy-start.28 = (bf16[2080,128]{1,0:T(8,128)(2,1)}, bf16[2080,128]{1,0:T(8,128)(2,1)S(1)}, u32[]{:S(2)}) copy-start(bf16[2080,128]{1,0:T(8,128)(2,1)S(1)} %collective-permute-done.refs_2_.refs_3_) | copy-start | bytes 1597444
  18.7 22.1 %collective-permute-start.2 = (bf16[1040,512]{1,0:T(8,128)(2,1)}, bf16[1040,512]{1,0:T(8,128)(2,1)S(1)}, u32[]{:S(2)}, u32[]{:S(2)}) collective-permute-start(bf16[1040,512]{1,0:T(8,128)(2,1)} %get-tuple-element.96.refs_0_), channel_id=1, source_target_pairs={{0,1},{1,0},{2,3},{3,2},{4,5},{5,4},{6,7},{7,6},{8,9},{9,8},{10,11... | collective-permute-start | bytes 3194888 | tf_op jit(solution)/shard_map/ppermute | solution.py:608
  18.7 31.0 %collective-permute-start.1 = (bf16[1040,512]{1,0:T(8,128)(2,1)}, bf16[1040,512]{1,0:T(8,128)(2,1)S(1)}, u32[]{:S(2)}, u32[]{:S(2)}) collective-permute-start(bf16[1040,512]{1,0:T(8,128)(2,1)} %get-tuple-element.96.refs_0_), channel_id=1, source_target_pairs={{0,2},{1,3},{2,0},{3,1},{4,6},{5,7},{6,4},{7,5},{8,10},{9,11},{10,... | collective-permute-start | bytes 3194888 | tf_op jit(solution)/shard_map/ppermute | solution.py:608
  20.5 5.8 %collective-permute-start.4 = (bf16[2080,128]{1,0:T(8,128)(2,1)S(1)}, bf16[2080,128]{1,0:T(8,128)(2,1)}, u32[]{:S(2)}, u32[]{:S(2)}) collective-permute-start(bf16[2080,128]{1,0:T(8,128)(2,1)S(1)} %copy-done.27), channel_id=1, source_target_pairs={{0,1},{1,0},{2,3},{3,2},{4,5},{5,4},{6,7},{7,6},{8,9},{9,8},{10,11... | collective-permute-start | bytes 1597448 | tf_op jit(solution)/shard_map/ppermute | solution.py:608
  20.7 4.9 %copy-start.32 = (bf16[320,512]{1,0:T(8,128)(2,1)}, bf16[320,512]{1,0:T(8,128)(2,1)S(1)}, u32[]{:S(2)}) copy-start(bf16[320,512]{1,0:T(8,128)(2,1)S(1)} %collective-permute-done.3.recv) | copy-start | bytes 983044
  20.7 5.6 %collective-permute-start.5 = (bf16[2080,128]{1,0:T(8,128)(2,1)S(1)}, bf16[2080,128]{1,0:T(8,128)(2,1)}, u32[]{:S(2)}, u32[]{:S(2)}) collective-permute-start(bf16[2080,128]{1,0:T(8,128)(2,1)S(1)} %collective-permute-done.refs_2_.refs_3_), channel_id=1, source_target_pairs={{0,1},{1,0},{2,3},{3,2},{4,5},{5,4},{6,7},{7,6},{8,9},{9,8},{10,11... | collective-permute-start | bytes 1597448 | tf_op jit(solution)/shard_map/ppermute | solution.py:608
  21.0 19.8 %collective-permute-start.6 = (bf16[320,512]{1,0:T(8,128)(2,1)}, bf16[320,512]{1,0:T(8,128)(2,1)}, u32[]{:S(2)}, u32[]{:S(2)}) collective-permute-start(bf16[320,512]{1,0:T(8,128)(2,1)} %get-tuple-element.98), channel_id=1, source_target_pairs={{0,28},{4,0},{8,4},{12,8},{16,12},{20,16},{24,20},{28,24},{1,29},{... | collective-permute-start | bytes 983048 | tf_op jit(solution)/shard_map/ppermute | solution.py:617
  49.7 2.7 %collective-permute-start.7 = (bf16[1040,512]{1,0:T(8,128)(2,1)S(1)}, bf16[1040,512]{1,0:T(8,128)(2,1)S(1)}, u32[]{:S(2)}, u32[]{:S(2)}) collective-permute-start(bf16[1040,512]{1,0:T(8,128)(2,1)S(1)} %collective-permute-done.1.refs_0_.refs_1_), channel_id=1, source_target_pairs={{0,1},{1,0},{2,3},{3,2},{4,5},{5,4},{6,7},{7,6},{8,9},{9,8},{10,11... | collective-permute-start | bytes 3194888 | tf_op jit(solution)/shard_map/ppermute | solution.py:608
  61.7 8.0 %copy-start.31 = (bf16[512,512]{1,0:T(8,128)(2,1)S(1)}, bf16[512,512]{1,0:T(8,128)(2,1)}, u32[]{:S(2)}) copy-start(bf16[512,512]{1,0:T(8,128)(2,1)} %get-tuple-element.108) | copy-start | bytes 1572868
  61.7 8.4 %copy-start.29 = (bf16[512,512]{1,0:T(8,128)(2,1)S(1)}, bf16[512,512]{1,0:T(8,128)(2,1)}, u32[]{:S(2)}) copy-start(bf16[512,512]{1,0:T(8,128)(2,1)} %get-tuple-element.129) | copy-start | bytes 1572868
  61.7 8.5 %copy-start.10 = (bf16[640,512]{1,0:T(8,128)(2,1)S(1)}, bf16[640,512]{1,0:T(8,128)(2,1)}, u32[]{:S(2)}) copy-start(bf16[640,512]{1,0:T(8,128)(2,1)} %get-tuple-element.127) | copy-start | bytes 1966084
  61.7 11.3 %copy-start.12 = (bf16[512,512]{1,0:T(8,128)(2,1)S(1)}, bf16[512,512]{1,0:T(8,128)(2,1)}, u32[]{:S(2)}) copy-start(bf16[512,512]{1,0:T(8,128)(2,1)} %get-tuple-element.107) | copy-start | bytes 1572868
  69.5 13.3 %collective-permute-start.9 = (bf16[1024,512]{1,0:T(8,128)(2,1)}, bf16[1024,512]{1,0:T(8,128)(2,1)S(1)}, u32[]{:S(2)}, u32[]{:S(2)}) collective-permute-start(bf16[1024,512]{1,0:T(8,128)(2,1)} %get-tuple-element.117), channel_id=1, source_target_pairs={{0,1},{1,0},{2,3},{3,2},{4,5},{5,4},{6,7},{7,6},{8,9},{9,8},{10,11... | collective-permute-start | bytes 3145736 | tf_op jit(solution)/shard_map/ppermute | solution.py:608
  69.7 3.3 %collective-permute-start.8 = (bf16[512,512]{1,0:T(8,128)(2,1)S(1)}, bf16[512,512]{1,0:T(8,128)(2,1)S(1)}, u32[]{:S(2)}, u32[]{:S(2)}) collective-permute-start(bf16[512,512]{1,0:T(8,128)(2,1)S(1)} %copy-done.31), channel_id=1, source_target_pairs={{0,1},{1,0},{2,3},{3,2},{4,5},{5,4},{6,7},{7,6},{8,9},{9,8},{10,11... | collective-permute-start | bytes 1572872 | tf_op jit(solution)/shard_map/ppermute | solution.py:608
  70.1 28.6 %collective-permute-start.13 = (bf16[512,512]{1,0:T(8,128)(2,1)S(1)}, bf16[512,512]{1,0:T(8,128)(2,1)S(1)}, u32[]{:S(2)}, u32[]{:S(2)}) collective-permute-start(bf16[512,512]{1,0:T(8,128)(2,1)S(1)} %copy-done.29), channel_id=1, source_target_pairs={{0,1},{1,0},{2,3},{3,2},{4,5},{5,4},{6,7},{7,6},{8,9},{9,8},{10,11... | collective-permute-start | bytes 1572872 | tf_op jit(solution)/shard_map/ppermute | solution.py:608
  70.2 28.8 %collective-permute-start.10 = (bf16[320,512]{1,0:T(8,128)(2,1)S(1)}, bf16[320,512]{1,0:T(8,128)(2,1)S(1)}, u32[]{:S(2)}, u32[]{:S(2)}) collective-permute-start(bf16[320,512]{1,0:T(8,128)(2,1)S(1)} %slice.130), channel_id=1, source_target_pairs={{0,4},{4,8},{8,12},{12,16},{16,20},{20,24},{24,28},{28,0},{1,5},{5... | collective-permute-start | bytes 983048 | tf_op jit(solution)/shard_map/ppermute | solution.py:617
  73.1 25.6 %collective-permute-start.14 = (bf16[512,512]{1,0:T(8,128)(2,1)S(1)}, bf16[512,512]{1,0:T(8,128)(2,1)S(1)}, u32[]{:S(2)}, u32[]{:S(2)}) collective-permute-start(bf16[512,512]{1,0:T(8,128)(2,1)S(1)} %add_convert_fusion.5), channel_id=1, source_target_pairs={{0,2},{1,3},{2,0},{3,1},{4,6},{5,7},{6,4},{7,5},{8,10},{9,11},{10,... | collective-permute-start | bytes 1572872 | tf_op jit(solution)/shard_map/ppermute | solution.py:608
  84.0 25.9 %collective-permute-start.16 = (bf16[512,512]{1,0:T(8,128)(2,1)S(1)}, bf16[512,512]{1,0:T(8,128)(2,1)S(1)}, u32[]{:S(2)}, u32[]{:S(2)}) collective-permute-start(bf16[512,512]{1,0:T(8,128)(2,1)S(1)} %add_convert_fusion.4), channel_id=1, source_target_pairs={{0,2},{1,3},{2,0},{3,1},{4,6},{5,7},{6,4},{7,5},{8,10},{9,11},{10,... | collective-permute-start | bytes 1572872 | tf_op jit(solution)/shard_map/ppermute | solution.py:608
  85.6 13.1 %copy-start.14 = (bf16[512,512]{1,0:T(8,128)(2,1)S(1)}, bf16[512,512]{1,0:T(8,128)(2,1)}, u32[]{:S(2)}) copy-start(bf16[512,512]{1,0:T(8,128)(2,1)} %get-tuple-element.128) | copy-start | bytes 1572868
  98.7 11.5 %collective-permute-start.15 = (bf16[1024,512]{1,0:T(8,128)(2,1)}, bf16[1024,512]{1,0:T(8,128)(2,1)S(1)}, u32[]{:S(2)}, u32[]{:S(2)}) collective-permute-start(bf16[1024,512]{1,0:T(8,128)(2,1)} %get-tuple-element.126), channel_id=1, source_target_pairs={{0,1},{1,0},{2,3},{3,2},{4,5},{5,4},{6,7},{7,6},{8,9},{9,8},{10,11... | collective-permute-start | bytes 3145736 | tf_op jit(solution)/shard_map/ppermute | solution.py:608
  98.9 9.8 %collective-permute-start.17 = (bf16[256,512]{1,0:T(8,128)(2,1)S(1)}, bf16[256,512]{1,0:T(8,128)(2,1)S(1)}, u32[]{:S(2)}, u32[]{:S(2)}) collective-permute-start(bf16[256,512]{1,0:T(8,128)(2,1)S(1)} %slice.170), channel_id=1, source_target_pairs={{0,4},{4,0},{8,12},{12,8},{16,20},{20,16},{24,28},{28,24},{1,5},{5... | collective-permute-start | bytes 786440 | tf_op jit(solution)/shard_map/ppermute | solution.py:612
  99.1 62.7 %copy-start.1 = (bf16[640,512]{1,0:T(8,128)(2,1)}, bf16[640,512]{1,0:T(8,128)(2,1)S(1)}, u32[]{:S(2)}) copy-start(bf16[640,512]{1,0:T(8,128)(2,1)S(1)} %pad_maximum_fusion.refs_0_) | copy-start | bytes 1966084
  99.1 62.7 %collective-permute-start.12 = (bf16[640,512]{1,0:T(8,128)(2,1)S(1)}, bf16[640,512]{1,0:T(8,128)(2,1)S(1)}, u32[]{:S(2)}, u32[]{:S(2)}) collective-permute-start(bf16[640,512]{1,0:T(8,128)(2,1)S(1)} %pad_maximum_fusion.refs_0_), channel_id=1, source_target_pairs={{0,2},{1,3},{2,0},{3,1},{4,6},{5,7},{6,4},{7,5},{8,10},{9,11},{10,... | collective-permute-start | bytes 1966088 | tf_op jit(solution)/shard_map/ppermute | solution.py:608
  108.8 18.9 %collective-permute-start.35 = (bf16[128,512]{1,0:T(8,128)(2,1)S(1)}, bf16[128,512]{1,0:T(8,128)(2,1)S(1)}, u32[]{:S(2)}, u32[]{:S(2)}) collective-permute-start(bf16[128,512]{1,0:T(8,128)(2,1)S(1)} %get-tuple-element.173), channel_id=1, source_target_pairs={{0,8},{4,12},{8,0},{12,4},{16,24},{20,28},{24,16},{28,20},{1,9},{5... | collective-permute-start | bytes 393224 | tf_op jit(solution)/shard_map/ppermute | solution.py:612
  110.3 17.2 %collective-permute-start.18 = (bf16[512,512]{1,0:T(8,128)(2,1)S(1)}, bf16[512,512]{1,0:T(8,128)(2,1)S(1)}, u32[]{:S(2)}, u32[]{:S(2)}) collective-permute-start(bf16[512,512]{1,0:T(8,128)(2,1)S(1)} %add_convert_fusion.2), channel_id=1, source_target_pairs={{0,2},{1,3},{2,0},{3,1},{4,6},{5,7},{6,4},{7,5},{8,10},{9,11},{10,... | collective-permute-start | bytes 1572872 | tf_op jit(solution)/shard_map/ppermute | solution.py:608
  111.9 17.8 %collective-permute-start.37 = (bf16[256,512]{1,0:T(8,128)(2,1)S(1)}, bf16[256,512]{1,0:T(8,128)(2,1)S(1)}, u32[]{:S(2)}, u32[]{:S(2)}) collective-permute-start(bf16[256,512]{1,0:T(8,128)(2,1)S(1)} %get-tuple-element.171), channel_id=1, source_target_pairs={{0,4},{4,0},{8,12},{12,8},{16,20},{20,16},{24,28},{28,24},{1,5},{5... | collective-permute-start | bytes 786440 | tf_op jit(solution)/shard_map/ppermute | solution.py:612
  125.7 18.7 %collective-permute-start.20 = (bf16[320,512]{1,0:T(8,128)(2,1)S(1)}, bf16[320,512]{1,0:T(8,128)(2,1)S(1)}, u32[]{:S(2)}, u32[]{:S(2)}) collective-permute-start(bf16[320,512]{1,0:T(8,128)(2,1)S(1)} %get-tuple-element.170), channel_id=1, source_target_pairs={{0,4},{4,8},{8,12},{12,16},{16,20},{20,24},{24,28},{28,0},{1,5},{5... | collective-permute-start | bytes 983048 | tf_op jit(solution)/shard_map/ppermute | solution.py:617
  127.8 5.7 %collective-permute-start.36 = (bf16[64,512]{1,0:T(8,128)(2,1)S(1)}, bf16[64,512]{1,0:T(8,128)(2,1)S(1)}, u32[]{:S(2)}, u32[]{:S(2)}) collective-permute-start(bf16[64,512]{1,0:T(8,128)(2,1)S(1)} %slice.187), channel_id=1, source_target_pairs={{0,16},{4,20},{8,24},{12,28},{16,0},{20,4},{24,8},{28,12},{1,17},{... | collective-permute-start | bytes 196616 | tf_op jit(solution)/shard_map/ppermute | solution.py:612
  128.7 14.3 %collective-permute-start.21 = (bf16[256,512]{1,0:T(8,128)(2,1)S(1)}, bf16[256,512]{1,0:T(8,128)(2,1)S(1)}, u32[]{:S(2)}, u32[]{:S(2)}) collective-permute-start(bf16[256,512]{1,0:T(8,128)(2,1)S(1)} %slice.174), channel_id=1, source_target_pairs={{0,4},{4,0},{8,12},{12,8},{16,20},{20,16},{24,28},{28,24},{1,5},{5... | collective-permute-start | bytes 786440 | tf_op jit(solution)/shard_map/ppermute | solution.py:612
  129.7 1.2 collective-permute-start.29
  131.0 12.2 %collective-permute-start.38 = (bf16[128,512]{1,0:T(8,128)(2,1)S(1)}, bf16[128,512]{1,0:T(8,128)(2,1)S(1)}, u32[]{:S(2)}, u32[]{:S(2)}) collective-permute-start(bf16[128,512]{1,0:T(8,128)(2,1)S(1)} %get-tuple-element.176), channel_id=1, source_target_pairs={{0,8},{4,12},{8,0},{12,4},{16,24},{20,28},{24,16},{28,20},{1,9},{5... | collective-permute-start | bytes 393224 | tf_op jit(solution)/shard_map/ppermute | solution.py:612
  143.1 6.5 %collective-permute-start.24 = (bf16[128,512]{1,0:T(8,128)(2,1)S(1)}, bf16[128,512]{1,0:T(8,128)(2,1)S(1)}, u32[]{:S(2)}, u32[]{:S(2)}) collective-permute-start(bf16[128,512]{1,0:T(8,128)(2,1)S(1)} %slice.176), channel_id=1, source_target_pairs={{0,8},{4,12},{8,0},{12,4},{16,24},{20,28},{24,16},{28,20},{1,9},{5... | collective-permute-start | bytes 393224 | tf_op jit(solution)/shard_map/ppermute | solution.py:612
  143.3 8.0 %collective-permute-start.39 = (bf16[64,512]{1,0:T(8,128)(2,1)S(1)}, bf16[64,512]{1,0:T(8,128)(2,1)S(1)}, u32[]{:S(2)}, u32[]{:S(2)}) collective-permute-start(bf16[64,512]{1,0:T(8,128)(2,1)S(1)} %slice.192), channel_id=1, source_target_pairs={{0,16},{4,20},{8,24},{12,28},{16,0},{20,4},{24,8},{28,12},{1,17},{... | collective-permute-start | bytes 196616 | tf_op jit(solution)/shard_map/ppermute | solution.py:612
  143.5 4.8 %collective-permute-start.30 = (f32[120,128]{1,0:T(8,128)S(1)}, f32[120,128]{1,0:T(8,128)S(1)}, u32[]{:S(2)}, u32[]{:S(2)}) collective-permute-start(f32[120,128]{1,0:T(8,128)S(1)} %add.90), channel_id=1, source_target_pairs={{0,2},{1,3},{2,0},{3,1},{4,6},{5,7},{6,4},{7,5},{8,10},{9,11},{10,... | collective-permute-start | bytes 184328 | tf_op jit(solution)/shard_map/ppermute | solution.py:608
  144.5 32.2 %copy-start.2 = (bf16[640,512]{1,0:T(8,128)(2,1)}, bf16[640,512]{1,0:T(8,128)(2,1)S(1)}, u32[]{:S(2)}) copy-start(bf16[640,512]{1,0:T(8,128)(2,1)S(1)} %pad_maximum_fusion.1.refs_0_) | copy-start | bytes 1966084
  144.5 32.2 %collective-permute-start.23 = (bf16[640,512]{1,0:T(8,128)(2,1)S(1)}, bf16[640,512]{1,0:T(8,128)(2,1)S(1)}, u32[]{:S(2)}, u32[]{:S(2)}) collective-permute-start(bf16[640,512]{1,0:T(8,128)(2,1)S(1)} %pad_maximum_fusion.1.refs_0_), channel_id=1, source_target_pairs={{0,2},{1,3},{2,0},{3,1},{4,6},{5,7},{6,4},{7,5},{8,10},{9,11},{10,... | collective-permute-start | bytes 1966088 | tf_op jit(solution)/shard_map/ppermute | solution.py:608
  149.7 6.4 %collective-permute-start.25 = (bf16[64,512]{1,0:T(8,128)(2,1)S(1)}, bf16[64,512]{1,0:T(8,128)(2,1)S(1)}, u32[]{:S(2)}, u32[]{:S(2)}) collective-permute-start(bf16[64,512]{1,0:T(8,128)(2,1)S(1)} %slice.178), channel_id=1, source_target_pairs={{0,16},{4,20},{8,24},{12,28},{16,0},{20,4},{24,8},{28,12},{1,17},{... | collective-permute-start | bytes 196616 | tf_op jit(solution)/shard_map/ppermute | solution.py:612
  151.2 4.2 %collective-permute-start.31 = (f32[120,128]{1,0:T(8,128)S(1)}, f32[120,128]{1,0:T(8,128)S(1)}, u32[]{:S(2)}, u32[]{:S(2)}) collective-permute-start(f32[120,128]{1,0:T(8,128)S(1)} %add.91), channel_id=1, source_target_pairs={{0,4},{4,0},{8,12},{12,8},{16,20},{20,16},{24,28},{28,24},{1,5},{5... | collective-permute-start | bytes 184328 | tf_op jit(solution)/shard_map/ppermute | solution.py:612
  156.1 7.7 %collective-permute-start.26 = (bf16[64,512]{1,0:T(8,128)(2,1)S(1)}, bf16[64,512]{1,0:T(8,128)(2,1)S(1)}, u32[]{:S(2)}, u32[]{:S(2)}) collective-permute-start(bf16[64,512]{1,0:T(8,128)(2,1)S(1)} %add_convert_fusion.14), channel_id=1, source_target_pairs={{0,16},{4,20},{8,24},{12,28},{16,0},{20,4},{24,8},{28,12},{1,17},{... | collective-permute-start | bytes 196616 | tf_op jit(solution)/shard_map/ppermute | solution.py:612
  157.7 5.2 %collective-permute-start.32 = (f32[120,128]{1,0:T(8,128)}, f32[120,128]{1,0:T(8,128)}, u32[]{:S(2)}, u32[]{:S(2)}) collective-permute-start(f32[120,128]{1,0:T(8,128)} %add.92), channel_id=1, source_target_pairs={{0,8},{4,12},{8,0},{12,4},{16,24},{20,28},{24,16},{28,20},{1,9},{5... | collective-permute-start | bytes 184328 | tf_op jit(solution)/shard_map/ppermute | solution.py:612
  159.3 7.6 %collective-permute-start.40 = (bf16[128,512]{1,0:T(8,128)(2,1)}, bf16[128,512]{1,0:T(8,128)(2,1)}, u32[]{:S(2)}, u32[]{:S(2)}) collective-permute-start(bf16[128,512]{1,0:T(8,128)(2,1)} %pad_maximum_fusion.6), channel_id=1, source_target_pairs={{0,16},{4,20},{8,24},{12,28},{16,0},{20,4},{24,8},{28,12},{1,17},{... | collective-permute-start | bytes 393224 | tf_op jit(solution)/shard_map/ppermute | solution.py:612
  161.8 23.8 %copy-start.5 = (bf16[640,512]{1,0:T(8,128)(2,1)}, bf16[640,512]{1,0:T(8,128)(2,1)S(1)}, u32[]{:S(2)}) copy-start(bf16[640,512]{1,0:T(8,128)(2,1)S(1)} %collective-permute-done.12.refs_2_) | copy-start | bytes 1966084
  161.8 21.3 %collective-permute-start.11 = (bf16[640,512]{1,0:T(8,128)(2,1)S(1)}, bf16[640,512]{1,0:T(8,128)(2,1)S(1)}, u32[]{:S(2)}, u32[]{:S(2)}) collective-permute-start(bf16[640,512]{1,0:T(8,128)(2,1)S(1)} %pad_maximum_fusion.refs_0_), channel_id=1, source_target_pairs={{0,1},{1,0},{2,3},{3,2},{4,5},{5,4},{6,7},{7,6},{8,9},{9,8},{10,11... | collective-permute-start | bytes 1966088 | tf_op jit(solution)/shard_map/ppermute | solution.py:608
  162.9 22.8 %collective-permute-start.19 = (bf16[640,512]{1,0:T(8,128)(2,1)S(1)}, bf16[640,512]{1,0:T(8,128)(2,1)}, u32[]{:S(2)}, u32[]{:S(2)}) collective-permute-start(bf16[640,512]{1,0:T(8,128)(2,1)S(1)} %collective-permute-done.12.refs_2_), channel_id=1, source_target_pairs={{0,1},{1,0},{2,3},{3,2},{4,5},{5,4},{6,7},{7,6},{8,9},{9,8},{10,11... | collective-permute-start | bytes 1966088 | tf_op jit(solution)/shard_map/ppermute | solution.py:608
  164.4 11.3 %collective-permute-start.27 = (bf16[128,512]{1,0:T(8,128)(2,1)}, bf16[128,512]{1,0:T(8,128)(2,1)}, u32[]{:S(2)}, u32[]{:S(2)}) collective-permute-start(bf16[128,512]{1,0:T(8,128)(2,1)} %pad_maximum_fusion.5), channel_id=1, source_target_pairs={{0,8},{4,12},{8,0},{12,4},{16,24},{20,28},{24,16},{28,20},{1,9},{5... | collective-permute-start | bytes 393224 | tf_op jit(solution)/shard_map/ppermute | solution.py:612
  166.9 6.4 %collective-permute-start.33 = (f32[120,128]{1,0:T(8,128)S(1)}, f32[120,128]{1,0:T(8,128)S(1)}, u32[]{:S(2)}, u32[]{:S(2)}) collective-permute-start(f32[120,128]{1,0:T(8,128)S(1)} %add.93), channel_id=1, source_target_pairs={{0,16},{4,20},{8,24},{12,28},{16,0},{20,4},{24,8},{28,12},{1,17},{... | collective-permute-start | bytes 184328 | tf_op jit(solution)/shard_map/ppermute | solution.py:612
  173.3 7.1 %collective-permute-start.41 = (bf16[256,512]{1,0:T(8,128)(2,1)}, bf16[256,512]{1,0:T(8,128)(2,1)}, u32[]{:S(2)}, u32[]{:S(2)}) collective-permute-start(bf16[256,512]{1,0:T(8,128)(2,1)} %pad_maximum_fusion.4), channel_id=1, source_target_pairs={{0,8},{4,12},{8,0},{12,4},{16,24},{20,28},{24,16},{28,20},{1,9},{5... | collective-permute-start | bytes 786440 | tf_op jit(solution)/shard_map/ppermute | solution.py:612
  175.8 29.8 %collective-permute-start.22 = (bf16[640,512]{1,0:T(8,128)(2,1)S(1)}, bf16[640,512]{1,0:T(8,128)(2,1)S(1)}, u32[]{:S(2)}, u32[]{:S(2)}) collective-permute-start(bf16[640,512]{1,0:T(8,128)(2,1)S(1)} %pad_maximum_fusion.1.refs_0_), channel_id=1, source_target_pairs={{0,1},{1,0},{2,3},{3,2},{4,5},{5,4},{6,7},{7,6},{8,9},{9,8},{10,11... | collective-permute-start | bytes 1966088 | tf_op jit(solution)/shard_map/ppermute | solution.py:608
  176.7 13.0 %copy-start.16 = (bf16[256,512]{1,0:T(8,128)(2,1)}, bf16[256,512]{1,0:T(8,128)(2,1)S(1)}, u32[]{:S(2)}) copy-start(bf16[256,512]{1,0:T(8,128)(2,1)S(1)} %pad_maximum_fusion.3.refs_0_) | copy-start | bytes 786436
  176.7 12.9 %copy-start.6 = (bf16[640,512]{1,0:T(8,128)(2,1)}, bf16[640,512]{1,0:T(8,128)(2,1)S(1)}, u32[]{:S(2)}) copy-start(bf16[640,512]{1,0:T(8,128)(2,1)S(1)} %collective-permute-done.23.refs_2_) | copy-start | bytes 1966084
  176.7 28.8 %collective-permute-start.28 = (bf16[640,512]{1,0:T(8,128)(2,1)S(1)}, bf16[640,512]{1,0:T(8,128)(2,1)S(1)}, u32[]{:S(2)}, u32[]{:S(2)}) collective-permute-start(bf16[640,512]{1,0:T(8,128)(2,1)S(1)} %collective-permute-done.23.refs_2_), channel_id=1, source_target_pairs={{0,1},{1,0},{2,3},{3,2},{4,5},{5,4},{6,7},{7,6},{8,9},{9,8},{10,11... | collective-permute-start | bytes 1966088 | tf_op jit(solution)/shard_map/ppermute | solution.py:608
  181.5 20.6 %copy-start.13 = (bf16[512,512]{1,0:T(8,128)(2,1)}, bf16[512,512]{1,0:T(8,128)(2,1)S(1)}, u32[]{:S(2)}) copy-start(bf16[512,512]{1,0:T(8,128)(2,1)S(1)} %pad_maximum_fusion.2.refs_0_) | copy-start | bytes 1572868
  181.5 20.6 %collective-permute-start.42 = (bf16[512,512]{1,0:T(8,128)(2,1)S(1)}, bf16[512,512]{1,0:T(8,128)(2,1)S(1)}, u32[]{:S(2)}, u32[]{:S(2)}) collective-permute-start(bf16[512,512]{1,0:T(8,128)(2,1)S(1)} %pad_maximum_fusion.2.refs_0_), channel_id=1, source_target_pairs={{0,4},{4,0},{8,12},{12,8},{16,20},{20,16},{24,28},{28,24},{1,5},{5... | collective-permute-start | bytes 1572872 | tf_op jit(solution)/shard_map/ppermute | solution.py:612
  183.1 16.1 %collective-permute-start.34 = (bf16[256,512]{1,0:T(8,128)(2,1)S(1)}, bf16[256,512]{1,0:T(8,128)(2,1)S(1)}, u32[]{:S(2)}, u32[]{:S(2)}) collective-permute-start(bf16[256,512]{1,0:T(8,128)(2,1)S(1)} %pad_maximum_fusion.3.refs_0_), channel_id=1, source_target_pairs={{0,4},{4,0},{8,12},{12,8},{16,20},{20,16},{24,28},{28,24},{1,5},{5... | collective-permute-start | bytes 786440 | tf_op jit(solution)/shard_map/ppermute | solution.py:612
  (13 other events, 18.9 us)
where the time goes:
time: 212 us; the launch traced here: 211 us
  Pallas kernels  101 us (48%)
  waiting for transfers between devices  47.1 us (22%)
  starting transfers between devices  41.4 us (20%)
  local copies, waits for them, and re-layouts  11.3 us (5%)
  other arithmetic  9.53 us (4%)
    pallas_call x12, Pallas kernels, call(): pl.pallas_call(kernel, out_shape=[jax.ShapeDtypeStruct(s, d) for s, d in...  93 us
    ppermute x18, waiting for transfers between devices, swap_rows(): lax.ppermute(x, 'rows', [(i, i ^ bit) for i in range(lax.axis_size('rows'...  34.4 us
    ppermute x18, starting transfers between devices, swap_rows(): lax.ppermute(x, 'rows', [(i, i ^ bit) for i in range(lax.axis_size('rows'...  18.7 us
    ppermute x21, starting transfers between devices, swap_tp(): return lax.ppermute(x, 'tp', [(i, i ^ bit) for i in range(TP)])  13 us
    ppermute x21, waiting for transfers between devices, swap_tp(): return lax.ppermute(x, 'tp', [(i, i ^ bit) for i in range(TP)])  12.7 us
    ppermute x4, starting transfers between devices, shift_rows(): return lax.ppermute(x, 'rows', [(i, (i + distance) % n) for i in range(n)])  9.73 us
    pallas_call x2, Pallas kernels, windowed_call(): pl.pallas_call(kernel, grid=(1,), in_specs=specs, out_specs=[pl.BlockSpec...  7.7 us
    unnamed x68, local copies, waits for them, and re-layouts  5.9 us
  transfers between devices with their start and end apart: 43, of which 14 were waited for; matrix products, arithmetic and copies ran while one was open for 7% of the time, Pallas kernels for 37%

commit v1 on v0

v1 whole, which is shorter than its diff:
```python
import functools

import jax
import jax.numpy as jnp
import numpy as np
from jax import lax
from jax.experimental import pallas as pl
from jax.experimental.pallas import tpu as pltpu
from jax.sharding import PartitionSpec as P

D = 512
HD = 32
WIN = 10
SHIFT = 5
TABLE = 361
TABLE_PAD = 384
NORM_EPS = 1e-05
MASKED = -1000000000.0
HIDDEN_KEY = -1e30

TP = 4
HEADS_HERE = 4
LANES = 128
TOKENS = WIN * WIN
WROW = 112
SEG = 64
STRIP = SHIFT * SEG
COLBLK = 16
NBLK = 5
SLAB = SHIFT * NBLK * COLBLK
STACK = HEADS_HERE * WROW
SPAN = 2 * WIN - 1
REACH = SPAN * (WIN - 1) + WIN - 1
PACK1 = 4 * D + 32
SMALL_SHARD = 24
SMALL_ROWS = 32
PACK2 = 2 * D + 16

F32 = jnp.float32
BF = jnp.bfloat16
VMEM_LIMIT = 24
VMEM_OF = {"head": 56, "rest": 56, "attn_fwd": 56}
COST_RATE = 2e8


def dot(a, b):
    return lax.dot_general(a, b, (((1,), (0,)), ((), ())), preferred_element_type=F32)


def dot_nt(a, b):
    return lax.dot_general(a, b, (((1,), (1,)), ((), ())), preferred_element_type=F32)


def dot_tn(a, b):
    return lax.dot_general(a, b, (((0,), (0,)), ((), ())), preferred_element_type=F32)


def onehot(idx, width):
    lanes = lax.broadcasted_iota(jnp.int32, (idx.shape[0], width), 1)
    return jnp.where(idx == lanes, 1.0, 0.0).astype(BF)


def rows_of(nwl):
    return -(-(nwl * WROW + 16) // 64) * 64


def tens(v):
    return sum((v >= WIN * m).astype(jnp.int32) for m in range(1, WIN))


def column(n):
    return lax.broadcasted_iota(jnp.int32, (n, 1), 0)


def lane_row(n):
    return lax.broadcasted_iota(jnp.int32, (1, n), 1)


def strip_places():
    d = column(STRIP)
    a = sum((d >= SEG * m).astype(jnp.int32) for m in range(1, SHIFT))
    return a, d - SEG * a


def window_places(rows, nwl):
    r = column(rows)
    j = sum((r >= WROW * m).astype(jnp.int32) for m in range(1, nwl + 1))
    return j, r - WROW * j


def strip_from_slab(nwl):
    a, c = strip_places()
    return jnp.where(c < nwl * WIN, a * (NBLK * COLBLK) + c, -1000)


def window_from(rows, nwl, low, row_width):
    j, i = window_places(rows, nwl)
    a = tens(i)
    found = (a - (SHIFT if low else 0)) * row_width + WIN * j + i - WIN * a
    first = TOKENS // 2 if low else 0
    ok = (i >= first) & (i < first + TOKENS // 2) & (j < nwl)
    return jnp.where(ok, found, -1000)


def strip_from_window(nwl, low):
    a, c = strip_places()
    j = tens(c)
    found = j * WROW + (a + (SHIFT if low else 0)) * WIN + c - WIN * j
    return jnp.where(c < nwl * WIN, found, -1000)


def pick_rows(places, source):
    return dot(onehot(places, source.shape[0]), source).astype(BF)


KERNEL_US = {
    "head": 3.0,
    "rest": 5.0,
    "attn_fwd": 14.0,
    "mlp_first": 9.0,
    "mlp_mid": 5.0,
    "mlp_last": 5.0,
    "attn_bwd_3": 7.0,
    "attn_bwd_2": 7.0,
    "attn_bwd_01": 11.0,
    "final": 1.0,
}


def cost(name):
    return pl.CostEstimate(
        flops=int(KERNEL_US.get(name, 0.01) * COST_RATE), bytes_accessed=1024, transcendentals=0
    )


def vspec():
    return pl.BlockSpec(memory_space=pltpu.VMEM)


def after(x, *others):
    return lax.optimization_barrier((x, *others))[0]


def call(kernel, args, outs, scratch=(), scalars=(), hbm=0, name=None):
    in_hbm = pl.BlockSpec(memory_space=pltpu.HBM)
    return pl.pallas_call(
        kernel,
        out_shape=[jax.ShapeDtypeStruct(s, d) for s, d in outs],
        in_specs=[pl.BlockSpec(memory_space=pltpu.SMEM) for _ in scalars]
        + [in_hbm if i < hbm else vspec() for i in range(len(args))],
        out_specs=[vspec() for _ in outs],
        scratch_shapes=list(scratch),
        compiler_params=pltpu.CompilerParams(vmem_limit_bytes=VMEM_OF.get(name, VMEM_LIMIT) * 2**20),
        cost_estimate=cost(name),
        name=name,
    )(*scalars, *[pltpu.with_memory_space_constraint(a, pltpu.HBM) for a in args[:hbm]], *args[hbm:])


def first_column(width):
    c = lax.axis_index("tp") * width + SHIFT
    off = lax.rem(c, COLBLK)
    return c - off, off


def slab_copies(field, half, start, slab, sems, k):
    main = (NBLK - 1) * COLBLK
    last = lax.rem(start + main, field.shape[1])
    rows = pl.ds(half * SHIFT, SHIFT)
    return [
        pltpu.make_async_copy(
            field.at[rows, pl.ds(pl.multiple_of(start, COLBLK), main), :],
            slab.at[:, :main, :],
            sems.at[k],
        ),
        pltpu.make_async_copy(
            field.at[rows, pl.ds(pl.multiple_of(last, COLBLK), COLBLK), :],
            slab.at[:, main:, :],
            sems.at[k + 1],
        ),
    ]


def head_kernel(width, x, wqkv, wproj, table, bias, strip, pack, slab, sems):
    start, off = first_column(width)
    rows = slab_copies(x, 0, start, slab, sems, 0)
    copies = [pltpu.make_async_copy(wqkv, pack.at[: 3 * D, :], sems.at[2])]
    for c in range(D // LANES):
        at = 3 * D + c * LANES
        copies.append(
            pltpu.make_async_copy(
                wproj.at[:, c * LANES : (c + 1) * LANES], pack.at[at : at + LANES, :], sems.at[3 + c]
            )
        )
    for copy in rows + copies:
        copy.start()
    row = lax.broadcasted_iota(jnp.int32, (TABLE, TABLE_PAD), 0)
    lane = lax.broadcasted_iota(jnp.int32, (TABLE, TABLE_PAD), 1)
    flip = jnp.where(row + lane == TABLE - 1, 1.0, 0.0).astype(BF)
    rev = dot(table[...], flip)
    lines = [rev[:, c * LANES : (c + 1) * LANES] for c in range(TABLE_PAD // LANES)]
    lines += [bias[...].astype(F32), jnp.zeros((PACK1 - 4 * D - 14, LANES), F32)]
    pack[4 * D :, :] = jnp.concatenate(lines, axis=0).astype(BF)
    hot = onehot(strip_from_slab(width // WIN) + off, SLAB)
    for copy in rows:
        copy.wait()
    strip[...] = dot(hot, slab[...].reshape(SLAB, D)).astype(BF)
    for copy in copies:
        copy.wait()


def rest_kernel(width, x, g, up, down, ubias, strip_g, win_x, win_g, pack, slabs, sems):
    start, off = first_column(width)
    rows = []
    for k, (field, half) in enumerate(((g, 0), (x, 1), (g, 1))):
        rows.append(slab_copies(field, half, start, slabs.at[k], sems, 2 * k))
    copies = [
        pltpu.make_async_copy(up, pack.at[:D, :], sems.at[6]),
        pltpu.make_async_copy(down, pack.at[D : 2 * D, :], sems.at[7]),
    ]
    for copy in sum(rows, []) + copies:
        copy.start()
    pack[2 * D :, :] = jnp.broadcast_to(ubias[...], (PACK2 - 2 * D, D))
    nwl = width // WIN
    wide = window_from(win_x.shape[0], nwl, False, NBLK * COLBLK)
    hots = [onehot(strip_from_slab(nwl) + off, SLAB), onehot(wide + off, SLAB)]
    for k, out in enumerate((strip_g, win_x, win_g)):
        for copy in rows[k]:
            copy.wait()
        out[...] = dot(hots[min(k, 1)], slabs[k].reshape(SLAB, D)).astype(BF)
    for copy in copies:
        copy.wait()


def norm_stats(x):
    mean = jnp.mean(x, axis=-1, keepdims=True)
    center = x - mean
    spread = jnp.mean(center * center, axis=-1, keepdims=True)
    inv = lax.rsqrt(spread + NORM_EPS)
    return center * inv, inv


def norm_back(dz, n, inv, gain):
    gz = dz * gain
    m1 = jnp.mean(gz, axis=-1, keepdims=True)
    m2 = jnp.mean(gz * n, axis=-1, keepdims=True)
    return (gz - m1 - n * m2) * inv


def row_chunks(rows, count):
    size = rows // count
    return [(c * size, size) for c in range(count)]


def head_masks():
    lane = lax.broadcasted_iota(jnp.int32, (1, LANES), 1)
    return [(lane >= h * HD) & (lane < (h + 1) * HD) for h in range(HEADS_HERE)]


def stacked(x, masks):
    return jnp.concatenate([jnp.where(m, x, jnp.zeros_like(x)) for m in masks], axis=0)


def unstacked(y, masks):
    total = jnp.where(masks[0], y[:WROW], 0.0)
    for h in range(1, HEADS_HERE):
        total = jnp.where(masks[h], y[h * WROW : (h + 1) * WROW], total)
    return total


def attn_fwd_kernel(nwl, bounds, *refs):
    packs, (upx, recv, vecs) = refs[:TP], refs[TP : TP + 3]
    refs = refs[TP + 3 :]
    qkv, probs, o_out = refs[:TP], refs[TP : 2 * TP], refs[2 * TP : 3 * TP]
    x_out, z1_out, hs_out, z2_out, bias_sc, roll_sc, row_sc, w_sc, small_sc, fm, sems = refs[3 * TP :]
    rows = x_out.shape[0]
    smalls, weights, projs = [], [], []
    for s in range(TP):
        lanes = slice(s * LANES, (s + 1) * LANES)
        smalls.append(
            pltpu.make_async_copy(packs[s].at[4 * D :, :], small_sc.at[s], sems.at[8 * s])
        )
        for m in range(3):
            weights.append(
                pltpu.make_async_copy(
                    packs[s].at[m * D : (m + 1) * D, :], w_sc.at[m, :, lanes], sems.at[8 * s + 1 + m]
                )
            )
        for c in range(D // LANES):
            projs.append(
                pltpu.make_async_copy(
                    packs[s].at[3 * D + c * LANES : 3 * D + (c + 1) * LANES, :],
                    w_sc.at[3, lanes, c * LANES : (c + 1) * LANES],
                    sems.at[8 * s + 4 + c],
                )
            )
    for copy in smalls + weights + projs:
        copy.start()
    is_end = jnp.where(bounds[0, 1] == lax.axis_index("rows"), 1.0, 0.0)
    last = jnp.where(lax.axis_index("tp") == TP - 1, 1.0, 0.0)
    g1, b1, g2, b2, bp = (vecs[i : i + 1, :] for i in range(5))

    for copy in smalls:
        copy.wait()
    table = jnp.concatenate(
        [
            jnp.concatenate(
                [small_sc[s, 4 * c : 4 * c + 4, :].astype(F32) for c in range(TABLE_PAD // LANES)],
                axis=1,
            )
            for s in range(TP)
        ],
        axis=0,
    )
    for i in range(TOKENS):
        shift = TABLE_PAD - REACH + SPAN * (i // WIN) + i % WIN
        rolled = pltpu.roll(table, shift, 1)
        roll_sc[i * TP * HEADS_HERE : (i + 1) * TP * HEADS_HERE, :] = rolled[:, : 2 * LANES].astype(BF)
    n16 = TOKENS * TP * HEADS_HERE
    lane = lane_row(LANES)
    at_lane = jnp.where(lane < TOKENS, lane + (SPAN - WIN) * tens(lane), -1000)
    spread = jnp.where(column(2 * LANES) == at_lane, 1.0, 0.0).astype(BF)
    row_sc[:n16, :] = dot(roll_sc[...], spread)
    row_sc[n16:, :] = jnp.zeros((WROW * TP * HEADS_HERE - n16, LANES), F32)
    row = column(WROW)
    real = (row < TOKENS) & (lane < TOKENS)
    low_differ = ((row >= TOKENS // 2) != (lane >= TOKENS // 2)) & real
    right_differ = ((row - WIN * tens(row) >= SHIFT) != (lane - WIN * tens(lane) >= SHIFT)) & real
    extra = jnp.where(lane < TOKENS, 0.0, HIDDEN_KEY) + jnp.where(low_differ, MASKED * is_end, 0.0)
    fm[...] = jnp.where(right_differ, MASKED * last, 0.0)
    for s in range(TP):
        for h in range(HEADS_HERE):
            rows_h = row_sc[pl.ds(s * HEADS_HERE + h, WROW, TP * HEADS_HERE), :]
            bias_sc[s, h * WROW : (h + 1) * WROW, :] = rows_h + extra

    places = window_from(rows, nwl, True, SEG)
    for r0, n in row_chunks(rows, 4):
        x = upx[r0 : r0 + n, :].astype(F32) + dot(onehot(places[r0 : r0 + n, :], STRIP), recv[...])
        x_out[r0 : r0 + n, :] = x.astype(BF)
        z, _ = norm_stats(x)
        z1_out[r0 : r0 + n, :] = (z * g1 + b1).astype(BF)
    scale = HD ** (-0.5)
    for copy in weights:
        copy.wait()
    for m in range(3):
        for r0, n in row_chunks(rows, 2):
            y = dot(z1_out[r0 : r0 + n, :], w_sc[m])
            for s in range(TP):
                part = y[:, s * LANES : (s + 1) * LANES]
                if m == 0:
                    part = (part + small_sc[s, 12:13, :].astype(F32)) * scale
                if m == 2:
                    part = part + small_sc[s, 13:14, :].astype(F32)
                qkv[s][m, r0 : r0 + n, :] = part.astype(BF)
    for s in range(TP):
        o_out[s][nwl * WROW :, :] = jnp.zeros((rows - nwl * WROW, LANES), BF)

    def window(j, carry):
        masks = head_masks()
        base = pl.multiple_of(j * WROW, 16)
        flag = jnp.where(j == nwl - 1, 1.0, 0.0)
        fm4 = jnp.concatenate([fm[...] * flag] * HEADS_HERE, axis=0)
        for s in range(TP):
            q = qkv[s][0, pl.ds(base, WROW), :]
            k = qkv[s][1, pl.ds(base, LANES), :]
            v = qkv[s][2, pl.ds(base, LANES), :]
            sco = dot_nt(stacked(q, masks), k) + bias_sc[s] + fm4
            top = jnp.max(sco, axis=-1, keepdims=True)
            e = jnp.exp(sco - top)
            total = jnp.sum(e, axis=-1, keepdims=True)
            p = (e / total).astype(BF)
            probs[s][j] = p
            o = unstacked(dot(p, v), masks)
            o_out[s][pl.ds(base, WROW), :] = o.astype(BF)
        return carry

    lax.fori_loop(0, nwl, window, 0)
    for copy in projs:
        copy.wait()
    for r0, n in row_chunks(rows, 2):
        o = jnp.concatenate([o_out[s][r0 : r0 + n, :] for s in range(TP)], axis=1)
        acc = x_out[r0 : r0 + n, :].astype(F32) + bp + dot(o, w_sc[3])
        hs_out[r0 : r0 + n, :] = acc
        z, _ = norm_stats(acc)
        z2_out[r0 : r0 + n, :] = (z * g2 + b2).astype(BF)


def my_block(blocks):
    w = lax.axis_index("rows")
    mine = 0
    size = blocks
    while size > 1:
        size //= 2
        mine = mine * 2 + lax.rem(w, 2)
        w = lax.div(w, 2)
    return mine


def store_blocks(out, r0, value, blocks, cols=None):
    size = value.shape[0] // blocks
    mine = my_block(blocks)
    for b in range(blocks):
        at = pl.multiple_of(r0 + jnp.bitwise_xor(mine, b) * size, size)
        part = value[b * size : (b + 1) * size, :]
        if cols is None:
            out[pl.ds(at, size), :] = part
        else:
            out[pl.ds(at, size), cols[0] : cols[1]] = part


def mlp_kernel(ns, first, last, nwl, blocks, *refs):
    refs = list(refs)
    packs = refs[:ns]
    if first:
        held, sems = refs[-1 - ns : -1], refs[-1]
        copies = loads(packs, held, sems)
        packs, refs = held, refs[: -1 - ns]
    z2 = refs[ns]
    refs = refs[ns + 1 :]
    if first:
        gup, grecv = refs[:2]
        refs = refs[2:]
    else:
        gs, y_in, z_in = refs[:3]
        refs = refs[3:]
    if last:
        hs, vecs = refs[:2]
        refs = refs[2:]
    grads, dub = refs[:ns], refs[ns]
    refs = refs[ns + 1 :]
    if first:
        gs = refs.pop(0)
    if last:
        out_up, out_low, dh_out, dhb_out, vec_out = refs[:5]
        refs = refs[5:]
    acc_y, acc_z, act_sc, du_sc = refs
    rows = z2.shape[0]
    if first:
        places = window_from(rows, nwl, True, SEG)
        for r0, n in row_chunks(rows, 4):
            gs[r0 : r0 + n, :] = (
                gup[r0 : r0 + n, :].astype(F32)
                + dot(onehot(places[r0 : r0 + n, :], STRIP), grecv[...])
            ).astype(BF)
    for k in range(ns):
        if first:
            copies[k].wait()
        ub = packs[k][2 * D : 2 * D + 1, :].astype(F32)
        dub_total = jnp.zeros((1, D), F32)
        for r0, n in row_chunks(rows, 2):
            sl = slice(r0, r0 + n)
            u = dot(z2[sl, :], packs[k][:D, :]) + ub
            phi = 0.5 * (1.0 + lax.erf(u * np.float32(np.sqrt(0.5))))
            act = (u * phi).astype(BF)
            slope = phi + u * (jnp.exp(-0.5 * u * u) * np.float32(1 / np.sqrt(2 * np.pi)))
            act_sc[sl, :] = act
            ga = dot_nt(gs[sl, :], packs[k][D : 2 * D, :])
            du = (slope * ga).astype(BF)
            du_sc[sl, :] = du
            dub_total += jnp.sum(du.astype(F32), axis=0, keepdims=True)
            y = dot(act, packs[k][D : 2 * D, :])
            z = dot_nt(du, packs[k][:D, :])
            if k > 0:
                acc_y[sl, :] += y
                acc_z[sl, :] += z
            elif first:
                acc_y[sl, :] = y
                acc_z[sl, :] = z
            else:
                acc_y[sl, :] = y + y_in[sl, :]
                acc_z[sl, :] = z + z_in[sl, :]
        for c in range(D // LANES):
            line = k * (D // LANES) + c
            dub[line : line + 1, :] = dub_total[:, c * LANES : (c + 1) * LANES]
        store_blocks(grads[k], 0, dot_tn(act_sc[...], gs[...]).astype(BF), blocks)
        store_blocks(grads[k], D, dot_tn(z2[...], du_sc[...]).astype(BF), blocks)
    if not last:
        return
    g2, bd = vecs[2:3, :], vecs[5:6, :]
    sums = [jnp.zeros((1, D), F32) for _ in range(4)]
    for r0, n in row_chunks(rows, 4):
        sl = slice(r0, r0 + n)
        dz = acc_z[sl, :]
        g = gs[sl, :].astype(F32)
        h = hs[sl, :]
        nrm, inv = norm_stats(h)
        dh = g + norm_back(dz, nrm, inv, g2)
        dh_out[sl, :] = dh
        dhb_out[sl, :] = dh.astype(BF)
        act_sc[sl, :] = (h + acc_y[sl, :] + bd).astype(BF)
        for i, term in enumerate((dz * nrm, dz, g, dh)):
            sums[i] = sums[i] + jnp.sum(term, axis=0, keepdims=True)
    vec_out[...] = jnp.concatenate(sums, axis=0)
    out_up[...] = pick_rows(strip_from_window(nwl, False), act_sc[...])
    out_low[...] = pick_rows(strip_from_window(nwl, True), act_sc[...])


def loads(sources, targets, sems, at=0):
    copies = [
        pltpu.make_async_copy(x, y, sems.at[at + i]) for i, (x, y) in enumerate(zip(sources, targets))
    ]
    for copy in copies:
        copy.start()
    return copies


def attn_bwd_kernel(ns, nwl, blocks, *refs):
    refs = list(refs)

    def take(n):
        found = refs[:n]
        del refs[:n]
        return found

    n_in = 4 * ns
    sources = take(n_in)
    dhb, z1 = take(2)
    grads = take(ns)
    dpos, *dx_sc = take(1 + ns)
    dsum, do_sc = take(2)
    held = take(n_in)
    (sems,) = refs
    copies = loads(sources, held, sems)
    packs, o, qkv, probs = (held[i * ns : (i + 1) * ns] for i in range(4))
    rows = dhb.shape[0]
    scale = HD ** (-0.5)
    masks = head_masks()
    lin = column(LANES)
    lin = jnp.where(lin < TOKENS, REACH - lin - (SPAN - WIN) * tens(lin), -1000)
    back = onehot(lin, TABLE_PAD)
    place = lane_row(STACK)
    head = sum((place >= WROW * m).astype(jnp.int32) for m in range(1, HEADS_HERE))
    place = place - WROW * head
    line = jnp.where(place < TOKENS, tens(place) * 8 + head, -1000)
    groups = jnp.where(column(WIN * 8) == line, 1.0, 0.0).astype(BF)
    for k in range(ns):
        copies[k].wait()
        total = None
        for c in range(D // LANES):
            w = packs[k][3 * D + c * LANES : 3 * D + (c + 1) * LANES, :]
            term = dot_nt(dhb[:, c * LANES : (c + 1) * LANES], w)
            total = term if total is None else total + term
        do_sc[k] = total.astype(BF)
        copies[ns + k].wait()
        gp = dot_tn(o[k][...], dhb[...]).astype(BF)
        gp = jnp.concatenate([gp[:, c * LANES : (c + 1) * LANES] for c in range(D // LANES)], axis=0)
        store_blocks(grads[k], 0, gp, blocks, (3 * LANES, 4 * LANES))
        dx_sc[k][nwl * WROW :, :] = jnp.zeros((rows - nwl * WROW, 3 * LANES), BF)
        dsum[k] = jnp.zeros(dsum.shape[1:], F32)
        copies[2 * ns + k].wait()
        copies[3 * ns + k].wait()

        def window(j, carry, k=k):
            base = pl.multiple_of(j * WROW, 16)
            q = stacked(qkv[k][0, pl.ds(base, WROW), :], masks)
            key = qkv[k][1, pl.ds(base, LANES), :]
            v = qkv[k][2, pl.ds(base, LANES), :]
            do = stacked(do_sc[k, pl.ds(base, WROW), :], masks)
            p = probs[k][j]
            p32 = p.astype(F32)
            pdp = p32 * dot_nt(do, v)
            ds = (pdp - p32 * jnp.sum(pdp, axis=-1, keepdims=True)).astype(BF)
            dsum[k] += ds.astype(F32)
            dv = dot_tn(p, do)
            dk = dot_tn(ds, q)
            dq = unstacked(dot(ds, key), masks) * scale
            dx_sc[k][pl.ds(base, WROW), :LANES] = dq.astype(BF)
            dx_sc[k][pl.ds(base, WROW), LANES : 2 * LANES] = dk[:WROW].astype(BF)
            dx_sc[k][pl.ds(base, WROW), 2 * LANES :] = dv[:WROW].astype(BF)
            return carry

        lax.fori_loop(0, nwl, window, 0)
    for k in range(ns):
        store_blocks(grads[k], 0, dot_tn(z1[...], dx_sc[k][...]).astype(BF), blocks, (0, 3 * LANES))
        high = dsum[k].astype(BF)
        low = (dsum[k] - high.astype(F32)).astype(BF)
        lanes = dot(high, back) + dot(low, back)
        turned = jnp.concatenate(
            [
                pltpu.roll(lanes[h * WROW : (h + 1) * WROW, :], 0, 1, stride=1, stride_axis=0)
                for h in range(HEADS_HERE)
            ],
            axis=0,
        )
        high = turned.astype(BF)
        low = (turned - high.astype(F32)).astype(BF)
        summed = dot(groups, high) + dot(groups, low)
        total = summed[:8, :]
        for a in range(1, WIN):
            total = total + pltpu.roll(summed[a * 8 : (a + 1) * 8, :], (SPAN - WIN) * a, 1)
        per = 16
        for h in range(HEADS_HERE):
            for c in range(TABLE_PAD // LANES):
                line = k * per + h * (TABLE_PAD // LANES) + c
                dpos[line : line + 1, :] = total[h : h + 1, c * LANES : (c + 1) * LANES]
        for i, m in enumerate((0, 2)):
            part = dx_sc[k][:, m * LANES : (m + 1) * LANES].astype(F32)
            line = k * per + 12 + i
            dpos[line : line + 1, :] = jnp.sum(part, axis=0, keepdims=True)
        dpos[k * per + 14 : (k + 1) * per, :] = jnp.zeros((2, LANES), F32)


def final_kernel(nwl, *refs):
    refs = list(refs)
    sources, refs = refs[: 2 * TP + 2], refs[2 * TP + 2 :]
    vecs, vec_mlp, small3, small2, small01, dub01, dub2, dub3 = refs[:8]
    out_up, out_low, small_out, small_f32, dz = refs[8:13]
    held, sems = refs[13:-1], refs[-1]
    copies = loads(sources, held, sems)
    x_ref, dh = held[2 * TP :]
    rows = x_ref.shape[0]
    for copy in copies:
        copy.wait()
    parts = list(zip(held[:TP], held[TP : 2 * TP]))
    weights = [
        jnp.concatenate([pack[m * D : (m + 1) * D, :] for m in range(3)], axis=1) for _, pack in parts
    ]
    sums = [jnp.zeros((1, D), F32) for _ in range(2)]
    for r0, n in row_chunks(rows, 4):
        sl = slice(r0, r0 + n)
        total = None
        for (dx, _), weight in zip(parts, weights):
            term = dot_nt(dx[sl, :], weight)
            total = term if total is None else total + term
        nrm, inv = norm_stats(x_ref[sl, :].astype(F32))
        dz[sl, :] = (dh[sl, :] + norm_back(total, nrm, inv, vecs[0:1, :])).astype(BF)
        sums[0] = sums[0] + jnp.sum(total * nrm, axis=0, keepdims=True)
        sums[1] = sums[1] + jnp.sum(total, axis=0, keepdims=True)
    t = lax.axis_index("tp")
    pieces = [
        (small01[:16, :], dub01[:4, :]),
        (small01[16:, :], dub01[4:, :]),
        (small2[...], dub2[...]),
        (small3[...], dub3[...]),
    ]
    for s, (lines, dub) in enumerate(pieces):
        at = pl.multiple_of(jnp.bitwise_xor(t, s) * LANES, LANES)
        both = jnp.concatenate([lines, dub, jnp.zeros((4, LANES), F32)], axis=0)
        small_f32[: SMALL_SHARD, pl.ds(at, LANES)] = both
    small_f32[SMALL_SHARD:, :] = jnp.concatenate(
        [vec_mlp[...]] + sums + [jnp.zeros((SMALL_ROWS - SMALL_SHARD - 6, D), F32)], axis=0
    )
    small_out[...] = small_f32[...].astype(BF)
    out_up[...] = pick_rows(strip_from_window(nwl, False), dz[...])
    out_low[...] = pick_rows(strip_from_window(nwl, True), dz[...])


def page_kernel(*refs):
    out = refs[TP]
    pw = out.shape[1]
    t = lax.axis_index("tp")
    width = pw // TP
    col = lax.broadcasted_iota(jnp.int32, (pw, 1), 0)
    hots = []
    for s in range(TP):
        v = col - width * jnp.bitwise_xor(t, s) - SHIFT
        v = jnp.where(v < 0, v + pw, v)
        v = jnp.where(v < width, v, -1000)
        hots.append(onehot(v, SEG))
    hot = jnp.concatenate(hots, axis=1)
    for r in range(WIN):
        off = STRIP + r * SEG if r < SHIFT else (r - SHIFT) * SEG
        parts = [ul[off : off + SEG, :] for ul in refs[:TP]]
        out[r] = dot(hot, jnp.concatenate(parts, axis=0)).astype(BF)


def swap_tp(x, bit):
    return lax.ppermute(x, "tp", [(i, i ^ bit) for i in range(TP)])


def swap_rows(x, bit):
    return lax.ppermute(x, "rows", [(i, i ^ bit) for i in range(lax.axis_size("rows"))])


def shift_rows(x, distance):
    n = lax.axis_size("rows")
    return lax.ppermute(x, "rows", [(i, (i + distance) % n) for i in range(n)])


def row_bits():
    n = lax.axis_size("rows")
    bits = []
    while 1 << len(bits) < n:
        bits.append(1 << len(bits))
    return bits


def blocks_for(rows):
    blocks = 1
    while 2 * blocks <= lax.axis_size("rows") and rows % (2 * blocks) == 0 and rows // (2 * blocks) >= 16:
        blocks *= 2
    return blocks


def added(arrays):
    total = arrays[0].astype(F32)
    for extra in arrays[1:]:
        total = total + extra.astype(F32)
    return total.astype(BF)


def scatter_step(arrays, bit, blocks):
    total = added(arrays)
    if bit < blocks:
        half = total.shape[0] // 2
        return [total[:half], swap_rows(total[half:], bit)]
    return [total, swap_rows(total, bit)]


def finish_kernel(blocks, order, n_in, *refs):
    ins, outs = refs[:n_in], refs[n_in:]
    part = ins[0].shape[0] * n_in // blocks
    each = blocks // n_in
    mine = my_block(blocks)
    both = len(outs) == 2
    half = part // 2
    for p in range(blocks):
        b = jnp.bitwise_xor(mine, sum(((p >> k) & 1) << to for k, to in enumerate(order)))
        piece = ins[p // each][(p % each) * part : (p % each + 1) * part, :].astype(F32)
        if both:
            at = pl.ds(pl.multiple_of(b * half, half), half)
            outs[0][at, :] = piece[:half]
            outs[1][at, :] = piece[half:]
        else:
            outs[2][pl.ds(pl.multiple_of(b * part, part), part), :] = piece
    if both:
        return
    qkv, proj, whole = outs
    for c in range(D // LANES):
        if c < 3:
            qkv[c] = whole[:, c * LANES : (c + 1) * LANES]
        proj[:, c * LANES : (c + 1) * LANES] = whole[c * LANES : (c + 1) * LANES, 3 * LANES :]


def finish(pieces, blocks, gathered, name):
    attn = name == "finish_attn"
    order = [len(gathered) - bit.bit_length() for bit in gathered]
    return call(
        functools.partial(finish_kernel, blocks, order, len(pieces)),
        pieces,
        [((3, D, LANES), F32), ((LANES, D), F32)] if attn else [((D, D), F32)] * 2,
        scratch=[pltpu.VMEM((D, D), F32)] if attn else [],
        name=name,
    )


def interleaved(parts, blocks):
    n = blocks
    cut = [p.reshape(n, 1, p.shape[0] // n, p.shape[1]) for p in parts]
    return jnp.concatenate(cut, axis=1).reshape(-1, parts[0].shape[1])


def riding_step(arrays, small, bit, blocks):
    total = added(arrays)
    small = added(small)
    half = total.shape[0] // 2 if bit < blocks else total.shape[0]
    got = swap_rows(jnp.concatenate([total[-half:], small], axis=0), bit)
    return [total[:half], got[:half]], [small, got[half:]]


def small_kernel(*refs):
    ins, vecs, shard = refs[:TP], refs[TP : TP + 6], refs[TP + 6]
    total = ins[0][...].astype(F32)
    for r in ins[1:]:
        total += r[...].astype(F32)
    for i in range(6):
        vecs[i][...] = total[SMALL_SHARD + i : SMALL_SHARD + i + 1, :]
    t = lax.axis_index("tp")
    mine = jnp.zeros(shard.shape, F32)
    for a in range(TP):
        mine = jnp.where(t == a, total[:SMALL_SHARD, a * LANES : (a + 1) * LANES], mine)
    shard[...] = mine


def page(pieces, page_shape, name):
    return call(page_kernel, pieces, [(page_shape, BF)], name=name)[0]


def per_device(
    patches,
    cotangent,
    page_bounds,
    attn_gain,
    attn_shift,
    qkv_weight,
    qv_bias,
    pos_table,
    proj_weight,
    proj_bias,
    mlp_gain,
    mlp_shift,
    up_weight,
    up_bias,
    down_weight,
    down_bias,
):
    t = lax.axis_index("tp")
    pw = patches.shape[1]
    nwl = pw // WIN // TP
    width = nwl * WIN
    rows = rows_of(nwl)
    bits = row_bits()
    blocks = blocks_for(D)

    slab = (SHIFT, NBLK * COLBLK, D)
    strip_x, pack1 = call(
        functools.partial(head_kernel, width),
        [patches, qkv_weight.reshape(3 * D, LANES), proj_weight, pos_table.T, qv_bias],
        [((STRIP, D), BF), ((PACK1, LANES), BF)],
        scratch=[
            pltpu.VMEM(slab, BF),
            pltpu.SemaphoreType.DMA((7,)),
        ],
        hbm=3,
        name="head",
    )
    recv_x = shift_rows(strip_x, -1)
    pack1_x = swap_tp(pack1, 2)
    pack1_c = swap_tp(pack1, 1)
    strip_g, up_x, up_g, pack2 = call(
        functools.partial(rest_kernel, width),
        [patches, after(cotangent, strip_x), up_weight, down_weight, up_bias[None]],
        [((STRIP, D), BF), ((rows, D), BF), ((rows, D), BF), ((PACK2, D), BF)],
        scratch=[
            pltpu.VMEM((3,) + slab, BF),
            pltpu.SemaphoreType.DMA((8,)),
        ],
        hbm=4,
        name="rest",
    )
    recv_g = shift_rows(strip_g, -1)
    vecs = jnp.stack([attn_gain, attn_shift, mlp_gain, mlp_shift, proj_bias, down_bias]).astype(F32)
    pack1_cx = swap_tp(after(pack1_x, strip_g, recv_x), 1)
    packs1 = [pack1, pack1_c, pack1_x, pack1_cx]
    pack2 = after(pack2, pack1_cx)
    pack2_x = swap_tp(pack2, 2)
    pack2_c = swap_tp(pack2, 1)

    outs = call(
        functools.partial(attn_fwd_kernel, nwl),
        packs1 + [up_x, recv_x, vecs],
        [((3, rows, LANES), BF)] * TP
        + [((nwl, STACK, LANES), BF)] * TP
        + [((rows, LANES), BF)] * TP
        + [((rows, D), BF), ((rows, D), BF), ((rows, D), F32), ((rows, D), BF)],
        scratch=[
            pltpu.VMEM((TP, STACK, LANES), F32),
            pltpu.VMEM((TOKENS * TP * HEADS_HERE, 2 * LANES), BF),
            pltpu.VMEM((WROW * TP * HEADS_HERE, LANES), F32),
            pltpu.VMEM((4, D, D), BF),
            pltpu.VMEM((TP, PACK1 - 4 * D, LANES), BF),
            pltpu.VMEM((WROW, LANES), F32),
            pltpu.SemaphoreType.DMA((8 * TP,)),
        ],
        scalars=[page_bounds],
        hbm=TP,
        name="attn_fwd",
    )
    qkv, probs, o = outs[:TP], outs[TP : 2 * TP], outs[2 * TP : 3 * TP]
    x_win, z1, hs, z2 = outs[3 * TP :]

    def mlp(packs, extra, first, last):
        ns = len(packs)
        outs = [((2 * D, D), BF)] * ns + [((ns * D // LANES, LANES), F32)]
        if first:
            outs += [((rows, D), BF)]
        if last:
            outs += [((STRIP, D), BF)] * 2 + [((rows, D), F32), ((rows, D), BF), ((4, D), F32)]
        accs = [((rows, D), F32)] * 2
        return call(
            functools.partial(mlp_kernel, ns, first, last, nwl, blocks),
            packs + [z2] + extra,
            outs if last else outs + accs,
            scratch=([pltpu.VMEM(*a) for a in accs] if last else [])
            + [pltpu.VMEM((rows, D), BF)] * 2
            + ([pltpu.VMEM((PACK2, D), BF)] * ns + [pltpu.SemaphoreType.DMA((ns,))] if first else []),
            hbm=ns if first else 0,
            name="mlp_last" if last else "mlp_first" if first else "mlp_mid",
        )

    g0, g1, dub01, gs, acc_y, acc_z = mlp([pack2, pack2_c], [up_g, recv_g], True, False)
    got_g1 = swap_tp(g1, 1)
    pack2_cx = swap_tp(after(pack2_x, acc_y), 1)
    g2, dub2, acc_y, acc_z = mlp([pack2_x], [gs, acc_y, acc_z], False, False)
    g3, dub3, up_y, low_y, dh, dhb, vec_mlp = mlp(
        [pack2_cx],
        [gs, acc_y, acc_z, hs, vecs],
        False,
        True,
    )
    got_g3 = swap_tp(g3, 1)
    lower_y = shift_rows(low_y, 1)

    def attn_bwd(shards, dhb):
        ns = len(shards)
        loaded = [a[s] for a in (packs1, o, qkv, probs) for s in shards]
        return call(
            functools.partial(attn_bwd_kernel, ns, nwl, blocks),
            loaded + [dhb, z1],
            [((D, D), BF)] * ns + [((ns * 16, LANES), F32)] + [((rows, 3 * LANES), BF)] * ns,
            scratch=[pltpu.VMEM((ns, STACK, LANES), F32), pltpu.VMEM((ns, rows, LANES), BF)]
            + [pltpu.VMEM(a.shape, a.dtype) for a in loaded]
            + [pltpu.SemaphoreType.DMA((len(loaded),))],
            hbm=len(loaded),
            name="attn_bwd_" + "".join(map(str, shards)),
        )

    a3, small3, dx3 = attn_bwd((3,), dhb)
    got_a3 = swap_tp(a3, 1)
    across_d = added([g2[:D], after(got_g3, a3)[:D]])
    got_dx = swap_tp(across_d, 2)
    up0 = added([after(g0, across_d)[D:], got_g1[D:]])
    up2 = added([g2[D:], got_g3[D:]])
    half = D // 2
    up_got = swap_rows(jnp.concatenate([up0[half:], up2[half:]], axis=0), bits[0])
    a2, small2, dx2 = attn_bwd((2,), after(dhb, across_d, up0, up2))
    across_a = added([a2, got_a3])
    got_ax = swap_tp(across_a, 2)
    a0, a1, small01, dx0, dx1 = attn_bwd((0, 1), after(dhb, across_a))
    got_a1 = swap_tp(a1, 1)
    page_own = jnp.concatenate([after(up_y, a2), lower_y], axis=0)
    from_c = swap_tp(page_own, 1)

    down = scatter_step([after(g0, a0)[:D], after(got_g1, a0)[:D], got_dx], bits[0], blocks)
    up_got = after(up_got, down[0])
    up0 = added([up0[:half], up_got[:half]])
    up2 = added([up2[:half], up_got[half:]])
    up_x = swap_tp(up2, 2)
    attn = [after(a0, up0, up2, down[0]), got_a1, got_ax]
    mlp = None
    gather_a = [b for b in reversed(bits) if b < blocks]
    gather_m = gather_a[:-2] + gather_a[:-3:-1]
    steps = len(bits) + len(gather_a)
    for i in range(steps):
        if i == 0:
            mark = added(attn)
            attn = scatter_step([mark], bits[i], blocks)
            loaded = [after(dx0, mark), dx1, dx2, dx3] + packs1 + [x_win, dh]
            up_g, low_g, small = call(
                functools.partial(final_kernel, nwl),
                loaded + [vecs, vec_mlp, small3, small2, small01, dub01, dub2, dub3],
                [((STRIP, D), BF)] * 2 + [((SMALL_ROWS, D), BF)],
                scratch=[pltpu.VMEM((SMALL_ROWS, D), F32), pltpu.VMEM((rows, D), BF)]
                + [pltpu.VMEM(a.shape, a.dtype) for a in loaded]
                + [pltpu.SemaphoreType.DMA((len(loaded),))],
                hbm=len(loaded),
                name="final",
            )
            small = [small]
            lower_g = shift_rows(low_g, 1)
        elif i < len(bits):
            mark = added(attn)
            attn, small = riding_step([mark], small, bits[i], blocks)
        else:
            mark = added(attn) if i == len(bits) else jnp.concatenate(attn, axis=0)
            attn = [mark, swap_rows(mark, gather_a[i - len(bits)])]
        if i == 0:
            down = added([after(down[0], mark), down[1]])
            up = added([up0, up_x])
            mlp = scatter_step([interleaved([down, up], blocks // 2)], bits[1], blocks)
            from_x = swap_tp(after(page_own, mark), 2)
        elif i + 1 < steps:
            kept = after(mlp[0], mark)
            if i + 1 < len(bits):
                mlp = scatter_step([kept, mlp[1]], bits[i + 1], blocks)
            else:
                first = i + 1 == len(bits)
                total = added([kept, mlp[1]]) if first else jnp.concatenate([kept, mlp[1]], axis=0)
                mlp = [total, swap_rows(total, gather_m[i + 1 - len(bits)])]
        if i == 2:
            own_g = jnp.concatenate([after(up_g, mark), lower_g], axis=0)
            g_x = swap_tp(own_g, 2)
            g_c = swap_tp(own_g, 1)
        if i == len(bits):
            small = added([after(small[0], mark), small[1]])
            small = [small, swap_rows(small, bits[0])]
            from_cx = swap_tp(after(from_x, mark), 1)
        if i == len(bits) + 1:
            small = added([after(small[0], mark), small[1]])
            s_x = swap_tp(small, 2)
            s_c = swap_tp(small, 1)
    g_cx = swap_tp(after(g_x, mark), 1)
    s_cx = swap_tp(after(s_x, mark), 1)
    block_out = page([after(page_own, mark), from_c, from_x, from_cx], patches.shape, "page_y")
    grad_patches = page([after(own_g, mark), g_c, g_x, g_cx], patches.shape, "page_g")
    *v, mine = call(
        small_kernel,
        [small, s_c, s_x, s_cx],
        [((1, D), F32)] * 6 + [((SMALL_SHARD, LANES), F32)],
        name="small",
    )
    attn[0] = after(attn[0], block_out, grad_patches, mine)
    grad_qkv, grad_proj = finish(attn, blocks, gather_a, "finish_attn")
    grad_down, grad_up = finish([after(mlp[0], grad_qkv), mlp[1]], blocks, gather_m, "finish_mlp")

    v = [line.reshape(D) for line in v]
    grad_pos_table = mine[:12].reshape(HEADS_HERE, TABLE_PAD)[:, :TABLE].T

    return (
        block_out,
        grad_patches,
        v[4],
        v[5],
        grad_qkv,
        mine[12:14],
        grad_pos_table,
        grad_proj,
        v[3],
        v[0],
        v[1],
        grad_up,
        mine[16:20].reshape(D),
        grad_down,
        v[2],
    )


def solution(mesh):
    placed = (
        P("rows", None, None),
        P("rows", None, None),
        P("rows", None),
        P(),
        P(),
        P(None, None, "tp"),
        P(None, "tp"),
        P(None, "tp"),
        P("tp", None),
        P(),
        P(),
        P(),
        P(None, "tp"),
        P("tp"),
        P("tp", None),
        P(),
    )
    return jax.shard_map(
        per_device,
        mesh=mesh,
        in_specs=placed,
        out_specs=(
            P("rows", None, None),
            P("rows", None, None),
            P(),
            P(),
            P(None, None, "tp"),
            P(None, "tp"),
            P(None, "tp"),
            P("tp", None),
            P(),
            P(),
            P(),
            P(None, "tp"),
            P("tp"),
            P("tp", None),
            P(),
        ),
        check_vma=False,
    )
```

time: 212 us -> 169 us (0.80)
  Pallas kernels: 101 us -> 80.1 us
  waiting for transfers between devices: 47.1 us -> 31.4 us
  other arithmetic: 9.53 us -> 2.19 us
  starting transfers between devices: 41.4 us -> 47.5 us
  local copies, waits for them, and re-layouts: 11.3 us -> 6.41 us
    ppermute x18 -> x14, waiting for transfers between devices: 34.4 us -> 18.5 us  [swap_rows(): lax.ppermute(x, 'rows', [(i, i ^ bit) for i in range(lax.axis_size('rows'...]
    pallas_call x12 -> x15, Pallas kernels: 93 us -> 80.1 us  [call(): pl.pallas_call(kernel, out_shape=[jax.ShapeDtypeStruct(s, d) for s, d in...]
    pallas_call x2 -> x0, Pallas kernels: 7.7 us -> none  [windowed_call(): pl.pallas_call(kernel, grid=(1,), in_specs=specs, out_specs=[pl.BlockSpec...]
    concatenate x7 -> x6, other arithmetic: 4.98 us -> 0.13 us  [the longest x1 0.05 us: interleaved(): return jnp.concatenate(cut, axis=1).reshape(-1, parts[0].shape[1])]
    ppermute x18 -> x14, starting transfers between devices: 18.7 us -> 23.5 us  [swap_rows(): lax.ppermute(x, 'rows', [(i, i ^ bit) for i in range(lax.axis_size('rows'...]
    unnamed x68 -> x52, local copies, waits for them, and re-layouts: 5.9 us -> 3.83 us
    ppermute x21 -> x22, waiting for transfers between devices: 12.7 us -> 11.3 us  [swap_tp(): return lax.ppermute(x, 'tp', [(i, i ^ bit) for i in range(TP)])]
    ppermute x21 -> x22, starting transfers between devices: 13 us -> 13.7 us  [swap_tp(): return lax.ppermute(x, 'tp', [(i, i ^ bit) for i in range(TP)])]
  transfers between devices with their start and end apart: 43 -> 40, of which waited for: 14 -> 13; matrix products, arithmetic and copies ran while one was open for 7% -> 3% of each run, Pallas kernels for 37% -> 42%
where the time goes in v1:
time: 169 us
  Pallas kernels  80.1 us (47%)
  starting transfers between devices  47.5 us (28%)
  waiting for transfers between devices  31.4 us (19%)
  local copies, waits for them, and re-layouts  6.41 us (4%)
  other arithmetic  2.19 us (1%)
    pallas_call x15, Pallas kernels, call(): pl.pallas_call(kernel, out_shape=[jax.ShapeDtypeStruct(s, d) for s, d in...  80.1 us
    ppermute x14, starting transfers between devices, swap_rows(): lax.ppermute(x, 'rows', [(i, i ^ bit) for i in range(lax.axis_size('rows'...  23.5 us
    ppermute x14, waiting for transfers between devices, swap_rows(): lax.ppermute(x, 'rows', [(i, i ^ bit) for i in range(lax.axis_size('rows'...  18.5 us
    ppermute x22, starting transfers between devices, swap_tp(): return lax.ppermute(x, 'tp', [(i, i ^ bit) for i in range(TP)])  13.7 us
    ppermute x22, waiting for transfers between devices, swap_tp(): return lax.ppermute(x, 'tp', [(i, i ^ bit) for i in range(TP)])  11.3 us
    ppermute x4, starting transfers between devices, shift_rows(): return lax.ppermute(x, 'rows', [(i, (i + distance) % n) for i in range(n)])  10.3 us
    unnamed x52, local copies, waits for them, and re-layouts  3.83 us
  transfers between devices with their start and end apart: 40, of which 13 were waited for; matrix products, arithmetic and copies ran while one was open for 3% of the time, Pallas kernels for 42%

profile of v1, /device:TPU:0, one launch (start us, length us, event | category | flops | bytes accessed | tf_op | source)
XLA Modules:
  0.0 169.0 jit_solution(2064928414197090934)
XLA Ops:
  0.7 3.1 %head.1 = (bf16[320,512]{1,0:T(8,128)(2,1)}, bf16[2080,128]{1,0:T(8,128)(2,1)}) custom-call(bf16[10,240,512]{2,1,0:T(8,128)(2,1)} %x.3, bf16[1536,128]{1,0:T(8,128)(2,1)} %bitcast.23, bf16[128,512]{1,0:T(8,128)(2,1)} %wproj.1, bf16[4,361]{1,0:T(4,128)(2,1)} %bitcast.25, bf16[2,128]{1,0:T(2,128)(2,1)} %bias.1), custom_call_target="tpu_custom_call" | custom-call | flops 600000000 | bytes 1024 | tf_op jit(solution)/shard_map/head/pallas_call | solution.py:146
  3.7 3.0 %collective-permute-start = (bf16[2080,128]{1,0:T(8,128)(2,1)}, bf16[2080,128]{1,0:T(8,128)(2,1)S(1)}, u32[]{:S(2)}, u32[]{:S(2)}) collective-permute-start(bf16[2080,128]{1,0:T(8,128)(2,1)} %get-tuple-element.112.refs_0_.refs_4_), channel_id=1, source_target_pairs={{0,2},{1,3},{2,0},{3,1},{4,6},{5,7},{6,4},{7,5},{8,10},{9,11},{10,... | collective-permute-start | bytes 1597448 | tf_op jit(solution)/shard_map/ppermute | solution.py:667
  6.7 4.6 %collective-permute-start.1 = (bf16[320,512]{1,0:T(8,128)(2,1)}, bf16[320,512]{1,0:T(8,128)(2,1)S(1)}, u32[]{:S(2)}, u32[]{:S(2)}) collective-permute-start(bf16[320,512]{1,0:T(8,128)(2,1)} %get-tuple-element.109), channel_id=1, source_target_pairs={{0,28},{4,0},{8,4},{12,8},{16,12},{20,16},{24,20},{28,24},{1,29},{... | collective-permute-start | bytes 983048 | tf_op jit(solution)/shard_map/ppermute | solution.py:676
  11.3 0.6 broadcast_in_dim.3.ubias
  11.9 4.8 %rest.1 = (bf16[320,512]{1,0:T(8,128)(2,1)}, bf16[704,512]{1,0:T(8,128)(2,1)}, bf16[704,512]{1,0:T(8,128)(2,1)}, bf16[1040,512]{1,0:T(8,128)(2,1)}) custom-call(bf16[10,240,512]{2,1,0:T(8,128)(2,1)} %x.3, bf16[10,240,512]{2,1,0:T(8,128)(2,1)} %g, bf16[512,512]{1,0:T(8,128)(2,1)} %up.1, bf16[512,512]{1,0:T(8,128)(2,1)} %down.1, ...), custom_call_target="tpu_custom_call" | custom-call | flops 1000000000 | bytes 1024 | tf_op jit(solution)/shard_map/rest/pallas_call | solution.py:146
  16.7 1.6 collective-permute-done.1.refs_5_
  18.3 0.7 collective-permute-done.refs_2_.refs_0_.refs_6_
  19.1 1.9 %collective-permute-done.2.refs_3_.refs_0_.refs_7_ = bf16[2080,128]{1,0:T(8,128)(2,1)S(1)} collective-permute-done((bf16[2080,128]{1,0:T(8,128)(2,1)S(1)}, bf16[2080,128]{1,0:T(8,128)(2,1)S(1)}, u32[]{:S(2)}, u32[]{:S(2)}) %collective-permute-start.2) | collective-permute-done | bytes 532512 | tf_op jit(solution)/shard_map/ppermute | solution.py:667
  21.1 1.8 %collective-permute-start.3 = (bf16[1040,512]{1,0:T(8,128)(2,1)}, bf16[1040,512]{1,0:T(8,128)(2,1)S(1)}, u32[]{:S(2)}, u32[]{:S(2)}) collective-permute-start(bf16[1040,512]{1,0:T(8,128)(2,1)} %get-tuple-element.115.refs_0_), channel_id=1, source_target_pairs={{0,2},{1,3},{2,0},{3,1},{4,6},{5,7},{6,4},{7,5},{8,10},{9,11},{10,... | collective-permute-start | bytes 3194888 | tf_op jit(solution)/shard_map/ppermute | solution.py:667
  23.0 4.6 %collective-permute-start.6 = (bf16[320,512]{1,0:T(8,128)(2,1)}, bf16[320,512]{1,0:T(8,128)(2,1)S(1)}, u32[]{:S(2)}, u32[]{:S(2)}) collective-permute-start(bf16[320,512]{1,0:T(8,128)(2,1)} %get-tuple-element.113), channel_id=1, source_target_pairs={{0,28},{4,0},{8,4},{12,8},{16,12},{20,16},{24,20},{28,24},{1,29},{... | collective-permute-start | bytes 983048 | tf_op jit(solution)/shard_map/ppermute | solution.py:676
  27.7 0.6 convert_element_type.181.refs_6_.refs_10_
  28.3 15.3 %attn_fwd.1 = (bf16[3,704,128]{2,1,0:T(8,128)(2,1)}, bf16[3,704,128]{2,1,0:T(8,128)(2,1)}, bf16[3,704,128]{2,1,0:T(8,128)(2,1)}, bf16[3,704,128]{2,1,0:T(8,128)(...) custom-call(s32[1,2]{1,0:T(1,128)} %bounds.1, ...), custom_call_target="tpu_custom_call" | custom-call | flops 2800000000 | bytes 1024 | tf_op jit(solution)/shard_map/attn_fwd/pallas_call | solution.py:146
  43.6 1.1 copy-done
  44.7 7.0 %mlp_first.1 = (bf16[1024,512]{1,0:T(8,128)(2,1)S(1)}, bf16[1024,512]{1,0:T(8,128)(2,1)S(1)}, f32[8,128]{1,0:T(8,128)S(1)}, bf16[704,512]{1,0:T(8,128)(2,1)S(1)}...) custom-call(bf16[1040,512]{1,0:T(8,128)(2,1)} %get-tuple-element.115.refs_0_, ...), custom_call_target="tpu_custom_call" | custom-call | flops 1800000000 | bytes 1024 | tf_op jit(solution)/shard_map/mlp_first/pallas_call | solution.py:146
  51.8 0.2 collective-permute-start.7
  52.0 2.8 %mlp_mid.1 = (bf16[1024,512]{1,0:T(8,128)(2,1)S(1)}, f32[4,128]{1,0:T(4,128)S(1)}, f32[704,512]{1,0:T(8,128)S(1)}, f32[704,512]{1,0:T(8,128)S(1)}) custom-call(bf16[1040,512]{1,0:T(8,128)(2,1)S(1)} %collective-permute-done.3.refs_0_, bf16[704,512]{1,0:T(8,128)(2,1)S(1)} %copy-done.1, bf16[704,512]{1,0:T(8,128)(2,1)S(1)} %get-tuple-element.121.refs_2_, ...), custom_call_target="tpu_custom_call" | custom-call | flops 1000000000 | bytes 1024 | tf_op jit(solution)/shard_map/mlp_mid/pallas_call | solution.py:146
  54.8 4.2 %mlp_last.1 = (bf16[1024,512]{1,0:T(8,128)(2,1)S(1)}, f32[4,128]{1,0:T(4,128)S(1)}, bf16[320,512]{1,0:T(8,128)(2,1)S(1)}, bf16[320,512]{1,0:T(8,128)(2,1)S(1)}, ...) custom-call(bf16[1040,512]{1,0:T(8,128)(2,1)S(1)} %collective-permute-done.7.refs_0_, ...), custom_call_target="tpu_custom_call" | custom-call | flops 1000000000 | bytes 1024 | tf_op jit(solution)/shard_map/mlp_last/pallas_call | solution.py:146
  59.1 1.1 copy-done.2
  60.2 0.3 collective-permute-start.8
  60.7 6.6 %attn_bwd_3.1 = (bf16[512,512]{1,0:T(8,128)(2,1)S(1)}, f32[16,128]{1,0:T(8,128)S(1)}, bf16[704,384]{1,0:T(8,128)(2,1)S(1)}) custom-call(bf16[2080,128]{1,0:T(8,128)(2,1)} %copy-done.15, bf16[704,128]{1,0:T(8,128)(2,1)} %get-tuple-element.133.refs_1_, bf16[3,704,128]{2,1,0:T(8,128)(2,1)} %get-tuple-element.134.refs_2_, ...), custom_call_target="tpu_custom_call" | custom-call | flops 1400000000 | bytes 1024 | tf_op jit(solution)/shard_map/attn_bwd_3/pallas_call | solution.py:146
  67.3 0.4 collective-permute-start.11
  67.7 0.3 add_convert_fusion.3
  68.1 0.8 collective-permute-start.13
  69.1 6.6 %attn_bwd_2.1 = (bf16[512,512]{1,0:T(8,128)(2,1)S(1)}, f32[16,128]{1,0:T(8,128)S(1)}, bf16[704,384]{1,0:T(8,128)(2,1)S(1)}) custom-call(bf16[2080,128]{1,0:T(8,128)(2,1)} %copy-done.14, bf16[704,128]{1,0:T(8,128)(2,1)} %get-tuple-element.127.refs_1_, bf16[3,704,128]{2,1,0:T(8,128)(2,1)} %get-tuple-element.128.refs_2_, ...), custom_call_target="tpu_custom_call" | custom-call | flops 1400000000 | bytes 1024 | tf_op jit(solution)/shard_map/attn_bwd_2/pallas_call | solution.py:146
  75.7 0.8 copy-done.5
  76.6 1.3 collective-permute-start.15
  78.0 11.3 %attn_bwd_01.1 = (bf16[512,512]{1,0:T(8,128)(2,1)S(1)}, bf16[512,512]{1,0:T(8,128)(2,1)S(1)}, f32[32,128]{1,0:T(8,128)S(1)}, bf16[704,384]{1,0:T(8,128)(2,1)S(1)}, bf16[704,384]{1,0:T(8,128)(2,1)S(1)}) custom-call(bf16[2080,128]{1,0:T(8,128)(2,1)} %get-tuple-element.112.refs_0_.refs_4_, bf16[2080,128]{1,0:T(8,128)(2,1)} %collective-permute-done.5.refs_1_.refs_5_, ...), custom_call_target="tpu_custom_call" | custom-call | flops 2200000000 | bytes 1024 | tf_op jit(solution)/shard_map/attn_bwd_01/pallas_call | solution.py:146
  89.5 0.2 add_convert_fusion.1
  89.7 0.4 copy-done.6
  90.3 1.3 collective-permute-done.12
  91.7 1.1 collective-permute-start.34
  93.0 0.5 collective-permute-start.33
  93.5 5.7 %collective-permute-done.34 = bf16[256,512]{1,0:T(8,128)(2,1)S(1)} collective-permute-done((bf16[256,512]{1,0:T(8,128)(2,1)S(1)}, bf16[256,512]{1,0:T(8,128)(2,1)S(1)}, u32[]{:S(2)}, u32[]{:S(2)}) %collective-permute-start.34) | collective-permute-done | bytes 262176 | tf_op jit(solution)/shard_map/ppermute | solution.py:667
  99.5 1.5 collective-permute-start.16
  101.0 1.1 collective-permute-done.33
  102.3 6.1 %final.1 = (bf16[320,512]{1,0:T(8,128)(2,1)S(1)}, bf16[320,512]{1,0:T(8,128)(2,1)S(1)}, bf16[32,512]{1,0:T(8,128)(2,1)S(1)}) custom-call(bf16[704,384]{1,0:T(8,128)(2,1)} %copy-done.6, bf16[704,384]{1,0:T(8,128)(2,1)} %copy-done.7, bf16[704,384]{1,0:T(8,128)(2,1)} %copy-done.5, bf16[704,384]{1,0:T(8,128)(2,1)} %copy-done.4, ...), custom_call_target="tpu_custom_call" | custom-call | flops 200000000 | bytes 1024 | tf_op jit(solution)/shard_map/final/pallas_call | solution.py:146
  108.4 1.2 collective-permute-start.24
  109.6 0.9 collective-permute-start.22
  110.6 1.5 collective-permute-start.17
  112.2 3.2 %collective-permute-start.36 = (bf16[128,512]{1,0:T(8,128)(2,1)S(1)}, bf16[128,512]{1,0:T(8,128)(2,1)S(1)}, u32[]{:S(2)}, u32[]{:S(2)}) collective-permute-start(bf16[128,512]{1,0:T(8,128)(2,1)S(1)} %get-tuple-element.212), channel_id=1, source_target_pairs={{0,16},{4,20},{8,24},{12,28},{16,0},{20,4},{24,8},{28,12},{1,17},{... | collective-permute-start | bytes 393224 | tf_op jit(solution)/shard_map/ppermute | solution.py:671
  115.4 2.5 %collective-permute-done.17 = bf16[160,512]{1,0:T(8,128)(2,1)S(1)} collective-permute-done((bf16[160,512]{1,0:T(8,128)(2,1)S(1)}, bf16[160,512]{1,0:T(8,128)(2,1)S(1)}, u32[]{:S(2)}, u32[]{:S(2)}) %collective-permute-start.17) | collective-permute-done | bytes 163872 | tf_op jit(solution)/shard_map/ppermute | solution.py:671
  118.0 4.3 %collective-permute-start.18 = (bf16[96,512]{1,0:T(8,128)(2,1)S(1)}, bf16[96,512]{1,0:T(8,128)(2,1)S(1)}, u32[]{:S(2)}, u32[]{:S(2)}) collective-permute-start(bf16[96,512]{1,0:T(8,128)(2,1)S(1)} %pad_maximum_fusion.5), channel_id=1, source_target_pairs={{0,16},{4,20},{8,24},{12,28},{16,0},{20,4},{24,8},{28,12},{1,17},{... | collective-permute-start | bytes 294920 | tf_op jit(solution)/shard_map/ppermute | solution.py:671
  122.5 1.0 collective-permute-start.26
  123.5 4.1 %collective-permute-done.18 = bf16[96,512]{1,0:T(8,128)(2,1)S(1)} collective-permute-done((bf16[96,512]{1,0:T(8,128)(2,1)S(1)}, bf16[96,512]{1,0:T(8,128)(2,1)S(1)}, u32[]{:S(2)}, u32[]{:S(2)}) %collective-permute-start.18) | collective-permute-done | bytes 98336 | tf_op jit(solution)/shard_map/ppermute | solution.py:671
  127.6 0.4 collective-permute-start.19
  128.0 4.4 %collective-permute-done.37 = bf16[128,512]{1,0:T(8,128)(2,1)S(1)} collective-permute-done((bf16[128,512]{1,0:T(8,128)(2,1)S(1)}, bf16[128,512]{1,0:T(8,128)(2,1)S(1)}, u32[]{:S(2)}, u32[]{:S(2)}) %collective-permute-start.37) | collective-permute-done | bytes 131104 | tf_op jit(solution)/shard_map/ppermute | solution.py:671
  132.4 7.9 %collective-permute-start.28 = (bf16[32,512]{1,0:T(8,128)(2,1)S(1)}, bf16[32,512]{1,0:T(8,128)(2,1)S(1)}, u32[]{:S(2)}, u32[]{:S(2)}) collective-permute-start(bf16[32,512]{1,0:T(8,128)(2,1)S(1)} %add_convert_fusion.16), channel_id=1, source_target_pairs={{0,4},{4,0},{8,12},{12,8},{16,20},{20,16},{24,28},{28,24},{1,5},{5... | collective-permute-start | bytes 98312 | tf_op jit(solution)/shard_map/ppermute | solution.py:671
  140.3 2.5 %collective-permute-start.38 = (bf16[256,512]{1,0:T(8,128)(2,1)S(1)}, bf16[256,512]{1,0:T(8,128)(2,1)S(1)}, u32[]{:S(2)}, u32[]{:S(2)}) collective-permute-start(bf16[256,512]{1,0:T(8,128)(2,1)S(1)} %constant_dynamic-update-slice_fusion.4), channel_id=1, source_target_pairs={{0,4},{4,0},{8,12},{12,8},{16,20},{20,16},{24,28},{28,24},{1,5},{5... | collective-permute-start | bytes 786440 | tf_op jit(solution)/shard_map/ppermute | solution.py:671
  143.0 1.1 collective-permute-start.30
  144.0 3.9 %collective-permute-done.20 = bf16[128,512]{1,0:T(8,128)(2,1)S(1)} collective-permute-done((bf16[128,512]{1,0:T(8,128)(2,1)S(1)}, bf16[128,512]{1,0:T(8,128)(2,1)S(1)}, u32[]{:S(2)}, u32[]{:S(2)}) %collective-permute-start.20) | collective-permute-done | bytes 131104 | tf_op jit(solution)/shard_map/ppermute | solution.py:671
  147.9 0.6 collective-permute-start.25
  148.6 0.5 collective-permute-done.29.refs_1_
  149.3 0.4 collective-permute-start.31
  149.7 2.4 %collective-permute-done.31.refs_3_ = bf16[32,512]{1,0:T(8,128)(2,1)S(1)} collective-permute-done((bf16[32,512]{1,0:T(8,128)(2,1)S(1)}, bf16[32,512]{1,0:T(8,128)(2,1)S(1)}, u32[]{:S(2)}, u32[]{:S(2)}) %collective-permute-start.31) | collective-permute-done | bytes 32800 | tf_op jit(solution)/shard_map/ppermute | solution.py:667
  152.2 0.6 small.1
  152.8 1.4 collective-permute-start.32
  154.1 0.6 slice_bitcast_fusion.1
  154.7 0.6 slice.133
  155.3 0.6 slice_bitcast_fusion
  155.9 3.4 %page_y.1 = bf16[10,240,512]{2,1,0:T(8,128)(2,1)} custom-call(bf16[640,512]{1,0:T(8,128)(2,1)S(1)} %constant_dynamic-update-slice_fusion.refs_0_, bf16[640,512]{1,0:T(8,128)(2,1)S(1)} %collective-permute-done.21.refs_1_, bf16[640,512]{1,0:T(8,128)(2,1)S(1)} %collective-permute-done.22.refs_2_, bf16[640,512]{1,0:T(8,128)(2,1)} %collective-permute-done.23.refs_3_), custom_call_target="tpu_custom_call" | custom-call | flops 2000000 | bytes 1024 | tf_op jit(solution)/shard_map/page_y/pallas_call | solution.py:146
  159.3 3.8 %page_g.1 = bf16[10,240,512]{2,1,0:T(8,128)(2,1)} custom-call(bf16[640,512]{1,0:T(8,128)(2,1)S(1)} %constant_dynamic-update-slice_fusion.2.refs_0_, bf16[640,512]{1,0:T(8,128)(2,1)} %collective-permute-done.25.refs_1_, bf16[640,512]{1,0:T(8,128)(2,1)} %collective-permute-done.26.refs_2_, bf16[640,512]{1,0:T(8,128)(2,1)} %collective-permute-done.27.refs_3_), custom_call_target="tpu_custom_call" | custom-call | flops 2000000 | bytes 1024 | tf_op jit(solution)/shard_map/page_g/pallas_call | solution.py:146
  163.1 2.1 %finish_attn.1 = (f32[3,512,128]{2,1,0:T(8,128)}, f32[128,512]{1,0:T(8,128)}) custom-call(bf16[256,512]{1,0:T(8,128)(2,1)S(1)} %pad_maximum_fusion.2.refs_0_, bf16[256,512]{1,0:T(8,128)(2,1)} %collective-permute-done.32.refs_1_), custom_call_target="tpu_custom_call" | custom-call | flops 2000000 | bytes 1024 | tf_op jit(solution)/shard_map/finish_attn/pallas_call | solution.py:146
  165.2 1.3 collective-permute-done.39.refs_1_
  166.5 2.5 %finish_mlp.1 = (f32[512,512]{1,0:T(8,128)}, f32[512,512]{1,0:T(8,128)}) custom-call(bf16[512,512]{1,0:T(8,128)(2,1)S(1)} %constant_dynamic-update-slice_fusion.6.refs_0_, bf16[512,512]{1,0:T(8,128)(2,1)} %collective-permute-done.39.refs_1_), custom_call_target="tpu_custom_call" | custom-call | flops 2000000 | bytes 1024 | tf_op jit(solution)/shard_map/finish_mlp/pallas_call | solution.py:146
  (131 shorter events, 2.9 us)
Async XLA Ops:
  0.6 10.6 %copy-start.16 = (bf16[512]{0:T(512)(128)(2,1)S(1)}, bf16[512]{0:T(512)(128)(2,1)}, u32[]{:S(2)}) copy-start(bf16[512]{0:T(512)(128)(2,1)} %param.29) | copy-start | bytes 3076
  3.7 15.3 %collective-permute-start = (bf16[2080,128]{1,0:T(8,128)(2,1)}, bf16[2080,128]{1,0:T(8,128)(2,1)S(1)}, u32[]{:S(2)}, u32[]{:S(2)}) collective-permute-start(bf16[2080,128]{1,0:T(8,128)(2,1)} %get-tuple-element.112.refs_0_.refs_4_), channel_id=1, source_target_pairs={{0,2},{1,3},{2,0},{3,1},{4,6},{5,7},{6,4},{7,5},{8,10},{9,11},{10,... | collective-permute-start | bytes 1597448 | tf_op jit(solution)/shard_map/ppermute | solution.py:667
  6.7 11.6 %collective-permute-start.1 = (bf16[320,512]{1,0:T(8,128)(2,1)}, bf16[320,512]{1,0:T(8,128)(2,1)S(1)}, u32[]{:S(2)}, u32[]{:S(2)}) collective-permute-start(bf16[320,512]{1,0:T(8,128)(2,1)} %get-tuple-element.109), channel_id=1, source_target_pairs={{0,28},{4,0},{8,4},{12,8},{16,12},{20,16},{24,20},{28,24},{1,29},{... | collective-permute-start | bytes 983048 | tf_op jit(solution)/shard_map/ppermute | solution.py:676
  11.9 11.0 %copy-start.13 = (bf16[2080,128]{1,0:T(8,128)(2,1)S(1)}, bf16[2080,128]{1,0:T(8,128)(2,1)}, u32[]{:S(2)}) copy-start(bf16[2080,128]{1,0:T(8,128)(2,1)} %get-tuple-element.112.refs_0_.refs_4_) | copy-start | bytes 1597444
  11.9 15.6 %copy-start.17 = (bf16[512]{0:T(512)(128)(2,1)S(1)}, bf16[512]{0:T(512)(128)(2,1)}, u32[]{:S(2)}) copy-start(bf16[512]{0:T(512)(128)(2,1)} %param.19) | copy-start | bytes 3076
  11.9 15.6 %copy-start.18 = (bf16[512]{0:T(512)(128)(2,1)S(1)}, bf16[512]{0:T(512)(128)(2,1)}, u32[]{:S(2)}) copy-start(bf16[512]{0:T(512)(128)(2,1)} %param.20) | copy-start | bytes 3076
  11.9 15.6 %copy-start.19 = (bf16[512]{0:T(512)(128)(2,1)S(1)}, bf16[512]{0:T(512)(128)(2,1)}, u32[]{:S(2)}) copy-start(bf16[512]{0:T(512)(128)(2,1)} %param.26) | copy-start | bytes 3076
  11.9 15.7 %copy-start.20 = (bf16[512]{0:T(512)(128)(2,1)S(1)}, bf16[512]{0:T(512)(128)(2,1)}, u32[]{:S(2)}) copy-start(bf16[512]{0:T(512)(128)(2,1)} %param.27) | copy-start | bytes 3076
  11.9 15.7 %copy-start.21 = (bf16[512]{0:T(512)(128)(2,1)S(1)}, bf16[512]{0:T(512)(128)(2,1)}, u32[]{:S(2)}) copy-start(bf16[512]{0:T(512)(128)(2,1)} %param.25) | copy-start | bytes 3076
  11.9 15.7 %copy-start.22 = (bf16[512]{0:T(512)(128)(2,1)S(1)}, bf16[512]{0:T(512)(128)(2,1)}, u32[]{:S(2)}) copy-start(bf16[512]{0:T(512)(128)(2,1)} %param.31) | copy-start | bytes 3076
  19.0 9.2 %copy-start.14 = (bf16[2080,128]{1,0:T(8,128)(2,1)}, bf16[2080,128]{1,0:T(8,128)(2,1)S(1)}, u32[]{:S(2)}) copy-start(bf16[2080,128]{1,0:T(8,128)(2,1)S(1)} %collective-permute-done.refs_2_.refs_0_.refs_6_) | copy-start | bytes 1597444
  19.1 1.9 %collective-permute-start.2 = (bf16[2080,128]{1,0:T(8,128)(2,1)S(1)}, bf16[2080,128]{1,0:T(8,128)(2,1)S(1)}, u32[]{:S(2)}, u32[]{:S(2)}) collective-permute-start(bf16[2080,128]{1,0:T(8,128)(2,1)S(1)} %collective-permute-done.refs_2_.refs_0_.refs_6_), channel_id=1, source_target_pairs={{0,1},{1,0},{2,3},{3,2},{4,5},{5,4},{6,7},{7,6},{8,9},{9,8},{10,11... | collective-permute-start | bytes 1597448 | tf_op jit(solution)/shard_map/ppermute | solution.py:667
  21.0 7.3 %copy-start.15 = (bf16[2080,128]{1,0:T(8,128)(2,1)}, bf16[2080,128]{1,0:T(8,128)(2,1)S(1)}, u32[]{:S(2)}) copy-start(bf16[2080,128]{1,0:T(8,128)(2,1)S(1)} %collective-permute-done.2.refs_3_.refs_0_.refs_7_) | copy-start | bytes 1597444
  21.0 22.6 %collective-permute-start.4 = (bf16[1040,512]{1,0:T(8,128)(2,1)}, bf16[1040,512]{1,0:T(8,128)(2,1)}, u32[]{:S(2)}, u32[]{:S(2)}) collective-permute-start(bf16[1040,512]{1,0:T(8,128)(2,1)} %get-tuple-element.115.refs_0_), channel_id=1, source_target_pairs={{0,1},{1,0},{2,3},{3,2},{4,5},{5,4},{6,7},{7,6},{8,9},{9,8},{10,11... | collective-permute-start | bytes 3194888 | tf_op jit(solution)/shard_map/ppermute | solution.py:667
  21.1 30.7 %collective-permute-start.3 = (bf16[1040,512]{1,0:T(8,128)(2,1)}, bf16[1040,512]{1,0:T(8,128)(2,1)S(1)}, u32[]{:S(2)}, u32[]{:S(2)}) collective-permute-start(bf16[1040,512]{1,0:T(8,128)(2,1)} %get-tuple-element.115.refs_0_), channel_id=1, source_target_pairs={{0,2},{1,3},{2,0},{3,1},{4,6},{5,7},{6,4},{7,5},{8,10},{9,11},{10,... | collective-permute-start | bytes 3194888 | tf_op jit(solution)/shard_map/ppermute | solution.py:667
  22.9 5.4 %collective-permute-start.5 = (bf16[2080,128]{1,0:T(8,128)(2,1)S(1)}, bf16[2080,128]{1,0:T(8,128)(2,1)}, u32[]{:S(2)}, u32[]{:S(2)}) collective-permute-start(bf16[2080,128]{1,0:T(8,128)(2,1)S(1)} %copy-done.13), channel_id=1, source_target_pairs={{0,1},{1,0},{2,3},{3,2},{4,5},{5,4},{6,7},{7,6},{8,9},{9,8},{10,11... | collective-permute-start | bytes 1597448 | tf_op jit(solution)/shard_map/ppermute | solution.py:667
  23.0 20.6 %collective-permute-start.6 = (bf16[320,512]{1,0:T(8,128)(2,1)}, bf16[320,512]{1,0:T(8,128)(2,1)S(1)}, u32[]{:S(2)}, u32[]{:S(2)}) collective-permute-start(bf16[320,512]{1,0:T(8,128)(2,1)} %get-tuple-element.113), channel_id=1, source_target_pairs={{0,28},{4,0},{8,4},{12,8},{16,12},{20,16},{24,20},{28,24},{1,29},{... | collective-permute-start | bytes 983048 | tf_op jit(solution)/shard_map/ppermute | solution.py:676
  28.3 15.3 %copy-start.9 = (bf16[704,512]{1,0:T(8,128)(2,1)S(1)}, bf16[704,512]{1,0:T(8,128)(2,1)}, u32[]{:S(2)}) copy-start(bf16[704,512]{1,0:T(8,128)(2,1)} %get-tuple-element.118.refs_3_) | copy-start | bytes 2162692
  43.6 1.1 copy-start
  44.7 7.3 %copy-start.1 = (bf16[704,512]{1,0:T(8,128)(2,1)S(1)}, bf16[704,512]{1,0:T(8,128)(2,1)}, u32[]{:S(2)}) copy-start(bf16[704,512]{1,0:T(8,128)(2,1)} %get-tuple-element.117.refs_2_.refs_1_) | copy-start | bytes 2162692
  51.8 3.0 %collective-permute-start.7 = (bf16[1040,512]{1,0:T(8,128)(2,1)S(1)}, bf16[1040,512]{1,0:T(8,128)(2,1)S(1)}, u32[]{:S(2)}, u32[]{:S(2)}) collective-permute-start(bf16[1040,512]{1,0:T(8,128)(2,1)S(1)} %collective-permute-done.3.refs_0_), channel_id=1, source_target_pairs={{0,1},{1,0},{2,3},{3,2},{4,5},{5,4},{6,7},{7,6},{8,9},{9,8},{10,11... | collective-permute-start | bytes 3194888 | tf_op jit(solution)/shard_map/ppermute | solution.py:667
  52.0 2.8 %copy-start.3 = (f32[704,512]{1,0:T(8,128)S(1)}, f32[704,512]{1,0:T(8,128)}, u32[]{:S(2)}) copy-start(f32[704,512]{1,0:T(8,128)} %get-tuple-element.125.refs_5_) | copy-start | bytes 4325380
  52.0 2.8 %copy-start.8 = (f32[6,512]{1,0:T(8,128)S(1)}, f32[6,512]{1,0:T(8,128)}, u32[]{:S(2)}) copy-start(f32[6,512]{1,0:T(8,128)} %convert_element_type.181.refs_6_.refs_10_) | copy-start | bytes 36868
  54.8 5.9 %copy-start.10 = (bf16[704,512]{1,0:T(8,128)(2,1)S(1)}, bf16[704,512]{1,0:T(8,128)(2,1)}, u32[]{:S(2)}) copy-start(bf16[704,512]{1,0:T(8,128)(2,1)} %get-tuple-element.136.refs_5_.refs_9_) | copy-start | bytes 2162692
  59.1 1.1 copy-start.2
  60.2 7.5 %collective-permute-start.8 = (bf16[1024,512]{1,0:T(8,128)(2,1)S(1)}, bf16[1024,512]{1,0:T(8,128)(2,1)S(1)}, u32[]{:S(2)}, u32[]{:S(2)}) collective-permute-start(bf16[1024,512]{1,0:T(8,128)(2,1)S(1)} %get-tuple-element.132), channel_id=1, source_target_pairs={{0,1},{1,0},{2,3},{3,2},{4,5},{5,4},{6,7},{7,6},{8,9},{9,8},{10,11... | collective-permute-start | bytes 3145736 | tf_op jit(solution)/shard_map/ppermute | solution.py:667
  60.5 8.4 %collective-permute-start.9 = (bf16[1024,512]{1,0:T(8,128)(2,1)S(1)}, bf16[1024,512]{1,0:T(8,128)(2,1)S(1)}, u32[]{:S(2)}, u32[]{:S(2)}) collective-permute-start(bf16[1024,512]{1,0:T(8,128)(2,1)S(1)} %get-tuple-element.141), channel_id=1, source_target_pairs={{0,1},{1,0},{2,3},{3,2},{4,5},{5,4},{6,7},{7,6},{8,9},{9,8},{10,11... | collective-permute-start | bytes 3145736 | tf_op jit(solution)/shard_map/ppermute | solution.py:667
  67.3 0.8 copy-start.4
  67.3 9.2 %collective-permute-start.11 = (bf16[512,512]{1,0:T(8,128)(2,1)S(1)}, bf16[512,512]{1,0:T(8,128)(2,1)S(1)}, u32[]{:S(2)}, u32[]{:S(2)}) collective-permute-start(bf16[512,512]{1,0:T(8,128)(2,1)S(1)} %get-tuple-element.137), channel_id=1, source_target_pairs={{0,1},{1,0},{2,3},{3,2},{4,5},{5,4},{6,7},{7,6},{8,9},{9,8},{10,11... | collective-permute-start | bytes 1572872 | tf_op jit(solution)/shard_map/ppermute | solution.py:667
  67.7 25.1 %collective-permute-start.10 = (bf16[320,512]{1,0:T(8,128)(2,1)S(1)}, bf16[320,512]{1,0:T(8,128)(2,1)S(1)}, u32[]{:S(2)}, u32[]{:S(2)}) collective-permute-start(bf16[320,512]{1,0:T(8,128)(2,1)S(1)} %get-tuple-element.145), channel_id=1, source_target_pairs={{0,4},{4,8},{8,12},{12,16},{16,20},{20,24},{24,28},{28,0},{1,5},{5... | collective-permute-start | bytes 983048 | tf_op jit(solution)/shard_map/ppermute | solution.py:676
  68.1 21.4 %collective-permute-start.13 = (bf16[512,512]{1,0:T(8,128)(2,1)S(1)}, bf16[512,512]{1,0:T(8,128)(2,1)S(1)}, u32[]{:S(2)}, u32[]{:S(2)}) collective-permute-start(bf16[512,512]{1,0:T(8,128)(2,1)S(1)} %get-tuple-element.206), channel_id=1, source_target_pairs={{0,2},{1,3},{2,0},{3,1},{4,6},{5,7},{6,4},{7,5},{8,10},{9,11},{10,... | collective-permute-start | bytes 1572872 | tf_op jit(solution)/shard_map/ppermute | solution.py:667
  69.0 6.6 %copy-start.11 = (bf16[512,512]{1,0:T(8,128)(2,1)}, bf16[512,512]{1,0:T(8,128)(2,1)S(1)}, u32[]{:S(2)}) copy-start(bf16[512,512]{1,0:T(8,128)(2,1)S(1)} %add_convert_fusion.4) | copy-start | bytes 1572868
  75.7 0.8 copy-start.5
  76.5 1.4 slice-start
  76.6 22.7 %collective-permute-start.15 = (bf16[512,512]{1,0:T(8,128)(2,1)S(1)}, bf16[512,512]{1,0:T(8,128)(2,1)S(1)}, u32[]{:S(2)}, u32[]{:S(2)}) collective-permute-start(bf16[512,512]{1,0:T(8,128)(2,1)S(1)} %add_convert_fusion.2), channel_id=1, source_target_pairs={{0,2},{1,3},{2,0},{3,1},{4,6},{5,7},{6,4},{7,5},{8,10},{9,11},{10,... | collective-permute-start | bytes 1572872 | tf_op jit(solution)/shard_map/ppermute | solution.py:667
  77.9 13.7 %collective-permute-start.12 = (bf16[512,512]{1,0:T(8,128)(2,1)S(1)}, bf16[512,512]{1,0:T(8,128)(2,1)S(1)}, u32[]{:S(2)}, u32[]{:S(2)}) collective-permute-start(bf16[512,512]{1,0:T(8,128)(2,1)S(1)} %pad_maximum_fusion), channel_id=1, source_target_pairs={{0,4},{4,0},{8,12},{12,8},{16,20},{20,16},{24,28},{28,24},{1,5},{5... | collective-permute-start | bytes 1572872 | tf_op jit(solution)/shard_map/ppermute | solution.py:671
  89.3 0.8 copy-start.6
  89.4 1.0 copy-start.7
  89.4 9.9 %collective-permute-start.14 = (bf16[512,512]{1,0:T(8,128)(2,1)S(1)}, bf16[512,512]{1,0:T(8,128)(2,1)S(1)}, u32[]{:S(2)}, u32[]{:S(2)}) collective-permute-start(bf16[512,512]{1,0:T(8,128)(2,1)S(1)} %get-tuple-element.158), channel_id=1, source_target_pairs={{0,1},{1,0},{2,3},{3,2},{4,5},{5,4},{6,7},{7,6},{8,9},{9,8},{10,11... | collective-permute-start | bytes 1572872 | tf_op jit(solution)/shard_map/ppermute | solution.py:667
  89.7 9.5 %copy-start.12 = (bf16[512,512]{1,0:T(8,128)(2,1)S(1)}, bf16[512,512]{1,0:T(8,128)(2,1)}, u32[]{:S(2)}) copy-start(bf16[512,512]{1,0:T(8,128)(2,1)} %copy-done.11) | copy-start | bytes 1572868
  91.7 7.4 %collective-permute-start.34 = (bf16[256,512]{1,0:T(8,128)(2,1)S(1)}, bf16[256,512]{1,0:T(8,128)(2,1)S(1)}, u32[]{:S(2)}, u32[]{:S(2)}) collective-permute-start(bf16[256,512]{1,0:T(8,128)(2,1)S(1)} %add_convert_fusion.10), channel_id=1, source_target_pairs={{0,2},{1,3},{2,0},{3,1},{4,6},{5,7},{6,4},{7,5},{8,10},{9,11},{10,... | collective-permute-start | bytes 786440 | tf_op jit(solution)/shard_map/ppermute | solution.py:667
  92.9 59.9 %collective-permute-start.21 = (bf16[640,512]{1,0:T(8,128)(2,1)S(1)}, bf16[640,512]{1,0:T(8,128)(2,1)S(1)}, u32[]{:S(2)}, u32[]{:S(2)}) collective-permute-start(bf16[640,512]{1,0:T(8,128)(2,1)S(1)} %constant_dynamic-update-slice_fusion.refs_0_), channel_id=1, source_target_pairs={{0,1},{1,0},{2,3},{3,2},{4,5},{5,4},{6,7},{7,6},{8,9},{9,8},{10,11... | collective-permute-start | bytes 1966088 | tf_op jit(solution)/shard_map/ppermute | solution.py:667
  93.0 9.2 %collective-permute-start.33 = (bf16[256,512]{1,0:T(8,128)(2,1)S(1)}, bf16[256,512]{1,0:T(8,128)(2,1)S(1)}, u32[]{:S(2)}, u32[]{:S(2)}) collective-permute-start(bf16[256,512]{1,0:T(8,128)(2,1)S(1)} %get-tuple-element.209), channel_id=1, source_target_pairs={{0,4},{4,0},{8,12},{12,8},{16,20},{20,16},{24,28},{28,24},{1,5},{5... | collective-permute-start | bytes 786440 | tf_op jit(solution)/shard_map/ppermute | solution.py:671
  99.5 11.0 %collective-permute-start.16 = (bf16[256,512]{1,0:T(8,128)(2,1)S(1)}, bf16[256,512]{1,0:T(8,128)(2,1)S(1)}, u32[]{:S(2)}, u32[]{:S(2)}) collective-permute-start(bf16[256,512]{1,0:T(8,128)(2,1)S(1)} %slice.152), channel_id=1, source_target_pairs={{0,4},{4,0},{8,12},{12,8},{16,20},{20,16},{24,28},{28,24},{1,5},{5... | collective-permute-start | bytes 786440 | tf_op jit(solution)/shard_map/ppermute | solution.py:671
  102.3 9.9 %collective-permute-start.35 = (bf16[256,512]{1,0:T(8,128)(2,1)S(1)}, bf16[256,512]{1,0:T(8,128)(2,1)S(1)}, u32[]{:S(2)}, u32[]{:S(2)}) collective-permute-start(bf16[256,512]{1,0:T(8,128)(2,1)S(1)} %bitcast.24), channel_id=1, source_target_pairs={{0,8},{4,12},{8,0},{12,4},{16,24},{20,28},{24,16},{28,20},{1,9},{5... | collective-permute-start | bytes 786440 | tf_op jit(solution)/shard_map/ppermute | solution.py:671
  108.4 14.1 %collective-permute-start.24 = (bf16[320,512]{1,0:T(8,128)(2,1)S(1)}, bf16[320,512]{1,0:T(8,128)(2,1)S(1)}, u32[]{:S(2)}, u32[]{:S(2)}) collective-permute-start(bf16[320,512]{1,0:T(8,128)(2,1)S(1)} %get-tuple-element.179), channel_id=1, source_target_pairs={{0,4},{4,8},{8,12},{12,16},{16,20},{20,24},{24,28},{28,0},{1,5},{5... | collective-permute-start | bytes 983048 | tf_op jit(solution)/shard_map/ppermute | solution.py:676
  109.6 33.4 %collective-permute-start.22 = (bf16[640,512]{1,0:T(8,128)(2,1)S(1)}, bf16[640,512]{1,0:T(8,128)(2,1)S(1)}, u32[]{:S(2)}, u32[]{:S(2)}) collective-permute-start(bf16[640,512]{1,0:T(8,128)(2,1)S(1)} %constant_dynamic-update-slice_fusion.refs_0_), channel_id=1, source_target_pairs={{0,2},{1,3},{2,0},{3,1},{4,6},{5,7},{6,4},{7,5},{8,10},{9,11},{10,... | collective-permute-start | bytes 1966088 | tf_op jit(solution)/shard_map/ppermute | solution.py:667
  110.6 7.3 %collective-permute-start.17 = (bf16[160,512]{1,0:T(8,128)(2,1)S(1)}, bf16[160,512]{1,0:T(8,128)(2,1)S(1)}, u32[]{:S(2)}, u32[]{:S(2)}) collective-permute-start(bf16[160,512]{1,0:T(8,128)(2,1)S(1)} %pad_maximum_fusion.3), channel_id=1, source_target_pairs={{0,8},{4,12},{8,0},{12,4},{16,24},{20,28},{24,16},{28,20},{1,9},{5... | collective-permute-start | bytes 491528 | tf_op jit(solution)/shard_map/ppermute | solution.py:671
  112.2 10.1 %collective-permute-start.36 = (bf16[128,512]{1,0:T(8,128)(2,1)S(1)}, bf16[128,512]{1,0:T(8,128)(2,1)S(1)}, u32[]{:S(2)}, u32[]{:S(2)}) collective-permute-start(bf16[128,512]{1,0:T(8,128)(2,1)S(1)} %get-tuple-element.212), channel_id=1, source_target_pairs={{0,16},{4,20},{8,24},{12,28},{16,0},{20,4},{24,8},{28,12},{1,17},{... | collective-permute-start | bytes 393224 | tf_op jit(solution)/shard_map/ppermute | solution.py:671
  118.0 9.6 %collective-permute-start.18 = (bf16[96,512]{1,0:T(8,128)(2,1)S(1)}, bf16[96,512]{1,0:T(8,128)(2,1)S(1)}, u32[]{:S(2)}, u32[]{:S(2)}) collective-permute-start(bf16[96,512]{1,0:T(8,128)(2,1)S(1)} %pad_maximum_fusion.5), channel_id=1, source_target_pairs={{0,16},{4,20},{8,24},{12,28},{16,0},{20,4},{24,8},{28,12},{1,17},{... | collective-permute-start | bytes 294920 | tf_op jit(solution)/shard_map/ppermute | solution.py:671
  122.3 10.1 %collective-permute-start.37 = (bf16[128,512]{1,0:T(8,128)(2,1)S(1)}, bf16[128,512]{1,0:T(8,128)(2,1)S(1)}, u32[]{:S(2)}, u32[]{:S(2)}) collective-permute-start(bf16[128,512]{1,0:T(8,128)(2,1)S(1)} %add_convert_fusion.12), channel_id=1, source_target_pairs={{0,16},{4,20},{8,24},{12,28},{16,0},{20,4},{24,8},{28,12},{1,17},{... | collective-permute-start | bytes 393224 | tf_op jit(solution)/shard_map/ppermute | solution.py:671
  122.5 25.4 %collective-permute-start.26 = (bf16[640,512]{1,0:T(8,128)(2,1)S(1)}, bf16[640,512]{1,0:T(8,128)(2,1)}, u32[]{:S(2)}, u32[]{:S(2)}) collective-permute-start(bf16[640,512]{1,0:T(8,128)(2,1)S(1)} %constant_dynamic-update-slice_fusion.2.refs_0_), channel_id=1, source_target_pairs={{0,2},{1,3},{2,0},{3,1},{4,6},{5,7},{6,4},{7,5},{8,10},{9,11},{10,... | collective-permute-start | bytes 1966088 | tf_op jit(solution)/shard_map/ppermute | solution.py:667
  127.6 12.7 %collective-permute-start.19 = (bf16[64,512]{1,0:T(8,128)(2,1)S(1)}, bf16[64,512]{1,0:T(8,128)(2,1)S(1)}, u32[]{:S(2)}, u32[]{:S(2)}) collective-permute-start(bf16[64,512]{1,0:T(8,128)(2,1)S(1)} %add_convert_fusion.14), channel_id=1, source_target_pairs={{0,16},{4,20},{8,24},{12,28},{16,0},{20,4},{24,8},{28,12},{1,17},{... | collective-permute-start | bytes 196616 | tf_op jit(solution)/shard_map/ppermute | solution.py:671
  132.4 10.5 %collective-permute-start.28 = (bf16[32,512]{1,0:T(8,128)(2,1)S(1)}, bf16[32,512]{1,0:T(8,128)(2,1)S(1)}, u32[]{:S(2)}, u32[]{:S(2)}) collective-permute-start(bf16[32,512]{1,0:T(8,128)(2,1)S(1)} %add_convert_fusion.16), channel_id=1, source_target_pairs={{0,4},{4,0},{8,12},{12,8},{16,20},{20,16},{24,28},{28,24},{1,5},{5... | collective-permute-start | bytes 98312 | tf_op jit(solution)/shard_map/ppermute | solution.py:671
  140.3 9.0 %collective-permute-start.38 = (bf16[256,512]{1,0:T(8,128)(2,1)S(1)}, bf16[256,512]{1,0:T(8,128)(2,1)S(1)}, u32[]{:S(2)}, u32[]{:S(2)}) collective-permute-start(bf16[256,512]{1,0:T(8,128)(2,1)S(1)} %constant_dynamic-update-slice_fusion.4), channel_id=1, source_target_pairs={{0,4},{4,0},{8,12},{12,8},{16,20},{20,16},{24,28},{28,24},{1,5},{5... | collective-permute-start | bytes 786440 | tf_op jit(solution)/shard_map/ppermute | solution.py:671
  142.9 5.0 %collective-permute-start.20 = (bf16[128,512]{1,0:T(8,128)(2,1)S(1)}, bf16[128,512]{1,0:T(8,128)(2,1)S(1)}, u32[]{:S(2)}, u32[]{:S(2)}) collective-permute-start(bf16[128,512]{1,0:T(8,128)(2,1)S(1)} %pad_maximum_fusion.4), channel_id=1, source_target_pairs={{0,8},{4,12},{8,0},{12,4},{16,24},{20,28},{24,16},{28,20},{1,9},{5... | collective-permute-start | bytes 393224 | tf_op jit(solution)/shard_map/ppermute | solution.py:671
  143.0 5.5 %collective-permute-start.30 = (bf16[32,512]{1,0:T(8,128)(2,1)S(1)}, bf16[32,512]{1,0:T(8,128)(2,1)S(1)}, u32[]{:S(2)}, u32[]{:S(2)}) collective-permute-start(bf16[32,512]{1,0:T(8,128)(2,1)S(1)} %add_convert_fusion.15.refs_0_), channel_id=1, source_target_pairs={{0,2},{1,3},{2,0},{3,1},{4,6},{5,7},{6,4},{7,5},{8,10},{9,11},{10,... | collective-permute-start | bytes 98312 | tf_op jit(solution)/shard_map/ppermute | solution.py:667
  147.9 1.2 collective-permute-start.29
  147.9 11.4 %collective-permute-start.25 = (bf16[640,512]{1,0:T(8,128)(2,1)S(1)}, bf16[640,512]{1,0:T(8,128)(2,1)}, u32[]{:S(2)}, u32[]{:S(2)}) collective-permute-start(bf16[640,512]{1,0:T(8,128)(2,1)S(1)} %constant_dynamic-update-slice_fusion.2.refs_0_), channel_id=1, source_target_pairs={{0,1},{1,0},{2,3},{3,2},{4,5},{5,4},{6,7},{7,6},{8,9},{9,8},{10,11... | collective-permute-start | bytes 1966088 | tf_op jit(solution)/shard_map/ppermute | solution.py:667
  148.5 7.4 %collective-permute-start.23 = (bf16[640,512]{1,0:T(8,128)(2,1)S(1)}, bf16[640,512]{1,0:T(8,128)(2,1)}, u32[]{:S(2)}, u32[]{:S(2)}) collective-permute-start(bf16[640,512]{1,0:T(8,128)(2,1)S(1)} %collective-permute-done.22.refs_2_), channel_id=1, source_target_pairs={{0,1},{1,0},{2,3},{3,2},{4,5},{5,4},{6,7},{7,6},{8,9},{9,8},{10,11... | collective-permute-start | bytes 1966088 | tf_op jit(solution)/shard_map/ppermute | solution.py:667
  149.1 10.2 %collective-permute-start.27 = (bf16[640,512]{1,0:T(8,128)(2,1)}, bf16[640,512]{1,0:T(8,128)(2,1)}, u32[]{:S(2)}, u32[]{:S(2)}) collective-permute-start(bf16[640,512]{1,0:T(8,128)(2,1)} %collective-permute-done.26.refs_2_), channel_id=1, source_target_pairs={{0,1},{1,0},{2,3},{3,2},{4,5},{5,4},{6,7},{7,6},{8,9},{9,8},{10,11... | collective-permute-start | bytes 1966088 | tf_op jit(solution)/shard_map/ppermute | solution.py:667
  149.3 2.9 %collective-permute-start.31 = (bf16[32,512]{1,0:T(8,128)(2,1)S(1)}, bf16[32,512]{1,0:T(8,128)(2,1)S(1)}, u32[]{:S(2)}, u32[]{:S(2)}) collective-permute-start(bf16[32,512]{1,0:T(8,128)(2,1)S(1)} %collective-permute-done.30.refs_2_), channel_id=1, source_target_pairs={{0,1},{1,0},{2,3},{3,2},{4,5},{5,4},{6,7},{7,6},{8,9},{9,8},{10,11... | collective-permute-start | bytes 98312 | tf_op jit(solution)/shard_map/ppermute | solution.py:667
  152.1 14.3 %collective-permute-start.39 = (bf16[512,512]{1,0:T(8,128)(2,1)S(1)}, bf16[512,512]{1,0:T(8,128)(2,1)}, u32[]{:S(2)}, u32[]{:S(2)}) collective-permute-start(bf16[512,512]{1,0:T(8,128)(2,1)S(1)} %constant_dynamic-update-slice_fusion.6.refs_0_), channel_id=1, source_target_pairs={{0,8},{4,12},{8,0},{12,4},{16,24},{20,28},{24,16},{28,20},{1,9},{5... | collective-permute-start | bytes 1572872 | tf_op jit(solution)/shard_map/ppermute | solution.py:671
  152.8 10.3 %collective-permute-start.32 = (bf16[256,512]{1,0:T(8,128)(2,1)S(1)}, bf16[256,512]{1,0:T(8,128)(2,1)}, u32[]{:S(2)}, u32[]{:S(2)}) collective-permute-start(bf16[256,512]{1,0:T(8,128)(2,1)S(1)} %pad_maximum_fusion.2.refs_0_), channel_id=1, source_target_pairs={{0,4},{4,0},{8,12},{12,8},{16,20},{20,16},{24,28},{28,24},{1,5},{5... | collective-permute-start | bytes 786440 | tf_op jit(solution)/shard_map/ppermute | solution.py:671
  (1 other events, 0.7 us)

commit v2 on v1

--- a/solution.py
+++ b/solution.py
@@ -41,6 +41,8 @@
 VMEM_LIMIT = 24
 VMEM_OF = {"head": 56, "rest": 56, "attn_fwd": 56}
 COST_RATE = 2e8
+UNROLL = 2
+UNROLL_F = 2
 
 
 def dot(a, b):
@@ -141,14 +143,14 @@
     return lax.optimization_barrier((x, *others))[0]
 
 
-def call(kernel, args, outs, scratch=(), scalars=(), hbm=0, name=None):
+def call(kernel, args, outs, scratch=(), scalars=(), hbm=0, hbm_out=0, name=None):
     in_hbm = pl.BlockSpec(memory_space=pltpu.HBM)
     return pl.pallas_call(
         kernel,
         out_shape=[jax.ShapeDtypeStruct(s, d) for s, d in outs],
         in_specs=[pl.BlockSpec(memory_space=pltpu.SMEM) for _ in scalars]
         + [in_hbm if i < hbm else vspec() for i in range(len(args))],
-        out_specs=[vspec() for _ in outs],
+        out_specs=[in_hbm if i < hbm_out else vspec() for i in range(len(outs))],
         scratch_shapes=list(scratch),
         compiler_params=pltpu.CompilerParams(vmem_limit_bytes=VMEM_OF.get(name, VMEM_LIMIT) * 2**20),
         cost_estimate=cost(name),
@@ -271,7 +273,8 @@
     packs, (upx, recv, vecs) = refs[:TP], refs[TP : TP + 3]
     refs = refs[TP + 3 :]
     qkv, probs, o_out = refs[:TP], refs[TP : 2 * TP], refs[2 * TP : 3 * TP]
-    x_out, z1_out, hs_out, z2_out, bias_sc, roll_sc, row_sc, w_sc, small_sc, fm, sems = refs[3 * TP :]
+    x_out, z1_out, hs_out, z2_out, bias_sc, roll_sc, row_sc, w_sc, small_sc, fm = refs[3 * TP : 3 * TP + 10]
+    x_sc, z1_sc, qkv_sc, p_sc, o_sc, sems = refs[3 * TP + 10 :]
     rows = x_out.shape[0]
     smalls, weights, projs = [], [], []
     for s in range(TP):
@@ -335,24 +338,26 @@
     places = window_from(rows, nwl, True, SEG)
     for r0, n in row_chunks(rows, 4):
         x = upx[r0 : r0 + n, :].astype(F32) + dot(onehot(places[r0 : r0 + n, :], STRIP), recv[...])
-        x_out[r0 : r0 + n, :] = x.astype(BF)
+        x_sc[r0 : r0 + n, :] = x.astype(BF)
         z, _ = norm_stats(x)
-        z1_out[r0 : r0 + n, :] = (z * g1 + b1).astype(BF)
+        z1_sc[r0 : r0 + n, :] = (z * g1 + b1).astype(BF)
+    outgoing = loads([x_sc, z1_sc], [x_out, z1_out], sems, 8 * TP)
     scale = HD ** (-0.5)
     for copy in weights:
         copy.wait()
     for m in range(3):
         for r0, n in row_chunks(rows, 2):
-            y = dot(z1_out[r0 : r0 + n, :], w_sc[m])
+            y = dot(z1_sc[r0 : r0 + n, :], w_sc[m])
             for s in range(TP):
                 part = y[:, s * LANES : (s + 1) * LANES]
                 if m == 0:
                     part = (part + small_sc[s, 12:13, :].astype(F32)) * scale
                 if m == 2:
                     part = part + small_sc[s, 13:14, :].astype(F32)
-                qkv[s][m, r0 : r0 + n, :] = part.astype(BF)
+                qkv_sc[s, m, r0 : r0 + n, :] = part.astype(BF)
+    outgoing += loads([qkv_sc.at[s] for s in range(TP)], qkv, sems, 8 * TP + 2)
     for s in range(TP):
-        o_out[s][nwl * WROW :, :] = jnp.zeros((rows - nwl * WROW, LANES), BF)
+        o_sc[s, nwl * WROW :, :] = jnp.zeros((rows - nwl * WROW, LANES), BF)
 
     def window(j, carry):
         masks = head_masks()
@@ -360,44 +365,50 @@
         flag = jnp.where(j == nwl - 1, 1.0, 0.0)
         fm4 = jnp.concatenate([fm[...] * flag] * HEADS_HERE, axis=0)
         for s in range(TP):
-            q = qkv[s][0, pl.ds(base, WROW), :]
-            k = qkv[s][1, pl.ds(base, LANES), :]
-            v = qkv[s][2, pl.ds(base, LANES), :]
+            q = qkv_sc[s, 0, pl.ds(base, WROW), :]
+            k = qkv_sc[s, 1, pl.ds(base, LANES), :]
+            v = qkv_sc[s, 2, pl.ds(base, LANES), :]
             sco = dot_nt(stacked(q, masks), k) + bias_sc[s] + fm4
             top = jnp.max(sco, axis=-1, keepdims=True)
             e = jnp.exp(sco - top)
             total = jnp.sum(e, axis=-1, keepdims=True)
             p = (e / total).astype(BF)
-            probs[s][j] = p
+            p_sc[s, j] = p
             o = unstacked(dot(p, v), masks)
-            o_out[s][pl.ds(base, WROW), :] = o.astype(BF)
+            o_sc[s, pl.ds(base, WROW), :] = o.astype(BF)
         return carry
 
-    lax.fori_loop(0, nwl, window, 0)
+    lax.fori_loop(0, nwl, window, 0, unroll=UNROLL_F)
+    outgoing += loads([p_sc.at[s] for s in range(TP)], probs, sems, 8 * TP + 6)
+    outgoing += loads([o_sc.at[s] for s in range(TP)], o_out, sems, 8 * TP + 10)
     for copy in projs:
         copy.wait()
     for r0, n in row_chunks(rows, 2):
-        o = jnp.concatenate([o_out[s][r0 : r0 + n, :] for s in range(TP)], axis=1)
-        acc = x_out[r0 : r0 + n, :].astype(F32) + bp + dot(o, w_sc[3])
+        o = jnp.concatenate([o_sc[s, r0 : r0 + n, :] for s in range(TP)], axis=1)
+        acc = x_sc[r0 : r0 + n, :].astype(F32) + bp + dot(o, w_sc[3])
         hs_out[r0 : r0 + n, :] = acc
         z, _ = norm_stats(acc)
         z2_out[r0 : r0 + n, :] = (z * g2 + b2).astype(BF)
-
-
-def my_block(blocks):
+    for copy in outgoing:
+        copy.wait()
+
+
+def bits_in_order(blocks, down):
+    bits = [1 << k for k in range(blocks.bit_length() - 1)]
+    return bits[1::-1] + bits[2:] if down else bits
+
+
+def my_block(blocks, down=False):
     w = lax.axis_index("rows")
     mine = 0
-    size = blocks
-    while size > 1:
-        size //= 2
-        mine = mine * 2 + lax.rem(w, 2)
-        w = lax.div(w, 2)
+    for bit in bits_in_order(blocks, down):
+        mine = mine * 2 + lax.rem(lax.div(w, bit), 2)
     return mine
 
 
-def store_blocks(out, r0, value, blocks, cols=None):
+def store_blocks(out, r0, value, blocks, cols=None, down=False):
     size = value.shape[0] // blocks
-    mine = my_block(blocks)
+    mine = my_block(blocks, down)
     for b in range(blocks):
         at = pl.multiple_of(r0 + jnp.bitwise_xor(mine, b) * size, size)
         part = value[b * size : (b + 1) * size, :]
@@ -471,7 +482,7 @@
         for c in range(D // LANES):
             line = k * (D // LANES) + c
             dub[line : line + 1, :] = dub_total[:, c * LANES : (c + 1) * LANES]
-        store_blocks(grads[k], 0, dot_tn(act_sc[...], gs[...]).astype(BF), blocks)
+        store_blocks(grads[k], 0, dot_tn(act_sc[...], gs[...]).astype(BF), blocks, down=True)
         store_blocks(grads[k], D, dot_tn(z2[...], du_sc[...]).astype(BF), blocks)
     if not last:
         return
@@ -568,7 +579,7 @@
             dx_sc[k][pl.ds(base, WROW), 2 * LANES :] = dv[:WROW].astype(BF)
             return carry
 
-        lax.fori_loop(0, nwl, window, 0)
+        lax.fori_loop(0, nwl, window, 0, unroll=UNROLL)
     for k in range(ns):
         store_blocks(grads[k], 0, dot_tn(z1[...], dx_sc[k][...]).astype(BF), blocks, (0, 3 * LANES))
         high = dsum[k].astype(BF)
@@ -601,21 +612,20 @@
 
 def final_kernel(nwl, *refs):
     refs = list(refs)
-    sources, refs = refs[: 2 * TP + 2], refs[2 * TP + 2 :]
-    vecs, vec_mlp, small3, small2, small01, dub01, dub2, dub3 = refs[:8]
-    out_up, out_low, small_out, small_f32, dz = refs[8:13]
-    held, sems = refs[13:-1], refs[-1]
-    copies = loads(sources, held, sems)
-    x_ref, dh = held[2 * TP :]
+    packs, dxs, refs = refs[:TP], refs[TP : 2 * TP], refs[2 * TP :]
+    x_ref, dh, vecs, vec_mlp, small3, small2, small01, dub01, dub2, dub3 = refs[:10]
+    out_up, out_low, small_out, small_f32, dz = refs[10:15]
+    held, sems = refs[15:-1], refs[-1]
+    copies = loads(packs, held, sems)
     rows = x_ref.shape[0]
     for copy in copies:
         copy.wait()
-    parts = list(zip(held[:TP], held[TP : 2 * TP]))
+    parts = list(zip(dxs, held))
     weights = [
         jnp.concatenate([pack[m * D : (m + 1) * D, :] for m in range(3)], axis=1) for _, pack in parts
     ]
     sums = [jnp.zeros((1, D), F32) for _ in range(2)]
-    for r0, n in row_chunks(rows, 4):
+    for r0, n in row_chunks(rows, 2):
         sl = slice(r0, r0 + n)
         total = None
         for (dx, _), weight in zip(parts, weights):
@@ -706,22 +716,27 @@
     return [total, swap_rows(total, bit)]
 
 
-def finish_kernel(blocks, order, n_in, *refs):
+def finish_kernel(blocks, gathered, n_in, *refs):
     ins, outs = refs[:n_in], refs[n_in:]
     part = ins[0].shape[0] * n_in // blocks
     each = blocks // n_in
-    mine = my_block(blocks)
     both = len(outs) == 2
     half = part // 2
+
+    def place(p, down):
+        order = bits_in_order(blocks, down)
+        moved = sum(
+            ((p >> k) & 1) << (len(order) - 1 - order.index(bit)) for k, bit in enumerate(gathered)
+        )
+        return jnp.bitwise_xor(my_block(blocks, down), moved)
+
     for p in range(blocks):
-        b = jnp.bitwise_xor(mine, sum(((p >> k) & 1) << to for k, to in enumerate(order)))
         piece = ins[p // each][(p % each) * part : (p % each + 1) * part, :].astype(F32)
         if both:
-            at = pl.ds(pl.multiple_of(b * half, half), half)
-            outs[0][at, :] = piece[:half]
-            outs[1][at, :] = piece[half:]
+            for out, value, down in zip(outs, (piece[:half], piece[half:]), (True, False)):
+                out[pl.ds(pl.multiple_of(place(p, down) * half, half), half), :] = value
         else:
-            outs[2][pl.ds(pl.multiple_of(b * part, part), part), :] = piece
+            outs[2][pl.ds(pl.multiple_of(place(p, False) * part, part), part), :] = piece
     if both:
         return
     qkv, proj, whole = outs
@@ -733,9 +748,8 @@
 
 def finish(pieces, blocks, gathered, name):
     attn = name == "finish_attn"
-    order = [len(gathered) - bit.bit_length() for bit in gathered]
     return call(
-        functools.partial(finish_kernel, blocks, order, len(pieces)),
+        functools.partial(finish_kernel, blocks, gathered, len(pieces)),
         pieces,
         [((3, D, LANES), F32), ((LANES, D), F32)] if attn else [((D, D), F32)] * 2,
         scratch=[pltpu.VMEM((D, D), F32)] if attn else [],
@@ -758,17 +772,23 @@
 
 
 def small_kernel(*refs):
-    ins, vecs, shard = refs[:TP], refs[TP : TP + 6], refs[TP + 6]
-    total = ins[0][...].astype(F32)
+    ins, outs = refs[:TP], refs[TP:]
+    total = ins[0][2 * STRIP :, :].astype(F32)
     for r in ins[1:]:
-        total += r[...].astype(F32)
+        total += r[2 * STRIP :, :].astype(F32)
     for i in range(6):
-        vecs[i][...] = total[SMALL_SHARD + i : SMALL_SHARD + i + 1, :]
+        outs[i][...] = total[SMALL_SHARD + i : SMALL_SHARD + i + 1, :]
     t = lax.axis_index("tp")
-    mine = jnp.zeros(shard.shape, F32)
+    mine = jnp.zeros((SMALL_SHARD, LANES), F32)
     for a in range(TP):
         mine = jnp.where(t == a, total[:SMALL_SHARD, a * LANES : (a + 1) * LANES], mine)
-    shard[...] = mine
+    qvb, up, table = outs[6:]
+    qvb[...] = mine[12:14, :]
+    up[...] = mine[16:20, :]
+    per = TABLE_PAD // LANES
+    for h in range(HEADS_HERE):
+        line = jnp.concatenate([mine[h * per + c : h * per + c + 1, :] for c in range(per)], axis=1)
+        table[h : h + 1, :] = line[:, :TABLE]
 
 
 def page(pieces, page_shape, name):
@@ -801,6 +821,7 @@
     bits = row_bits()
     blocks = blocks_for(D)
 
+    vecs = jnp.stack([attn_gain, attn_shift, mlp_gain, mlp_shift, proj_bias, down_bias]).astype(F32)
     slab = (SHIFT, NBLK * COLBLK, D)
     strip_x, pack1 = call(
         functools.partial(head_kernel, width),
@@ -818,7 +839,7 @@
     pack1_c = swap_tp(pack1, 1)
     strip_g, up_x, up_g, pack2 = call(
         functools.partial(rest_kernel, width),
-        [patches, after(cotangent, strip_x), up_weight, down_weight, up_bias[None]],
+        [patches, after(cotangent, strip_x, vecs), up_weight, down_weight, up_bias[None]],
         [((STRIP, D), BF), ((rows, D), BF), ((rows, D), BF), ((PACK2, D), BF)],
         scratch=[
             pltpu.VMEM((3,) + slab, BF),
@@ -828,11 +849,9 @@
         name="rest",
     )
     recv_g = shift_rows(strip_g, -1)
-    vecs = jnp.stack([attn_gain, attn_shift, mlp_gain, mlp_shift, proj_bias, down_bias]).astype(F32)
-    pack1_cx = swap_tp(after(pack1_x, strip_g, recv_x), 1)
+    pack1_cx = swap_tp(after(pack1_x, strip_g, recv_x, pack1_c), 1)
     packs1 = [pack1, pack1_c, pack1_x, pack1_cx]
-    pack2 = after(pack2, pack1_cx)
-    pack2_x = swap_tp(pack2, 2)
+    pack2_x = swap_tp(after(pack2, pack1_x), 2)
     pack2_c = swap_tp(pack2, 1)
 
     outs = call(
@@ -849,10 +868,16 @@
             pltpu.VMEM((4, D, D), BF),
             pltpu.VMEM((TP, PACK1 - 4 * D, LANES), BF),
             pltpu.VMEM((WROW, LANES), F32),
-            pltpu.SemaphoreType.DMA((8 * TP,)),
+            pltpu.VMEM((rows, D), BF),
+            pltpu.VMEM((rows, D), BF),
+            pltpu.VMEM((TP, 3, rows, LANES), BF),
+            pltpu.VMEM((TP, nwl, STACK, LANES), BF),
+            pltpu.VMEM((TP, rows, LANES), BF),
+            pltpu.SemaphoreType.DMA((8 * TP + 2 + 3 * TP,)),
         ],
         scalars=[page_bounds],
         hbm=TP,
+        hbm_out=3 * TP + 2,
         name="attn_fwd",
     )
     qkv, probs, o = outs[:TP], outs[TP : 2 * TP], outs[2 * TP : 3 * TP]
@@ -920,80 +945,73 @@
     page_own = jnp.concatenate([after(up_y, a2), lower_y], axis=0)
     from_c = swap_tp(page_own, 1)
 
-    down = scatter_step([after(g0, a0)[:D], after(got_g1, a0)[:D], got_dx], bits[0], blocks)
+    down = scatter_step([after(g0, a0)[:D], after(got_g1, a0)[:D], got_dx], bits[1], blocks)
     up_got = after(up_got, down[0])
     up0 = added([up0[:half], up_got[:half]])
     up2 = added([up2[:half], up_got[half:]])
     up_x = swap_tp(up2, 2)
-    attn = [after(a0, up0, up2, down[0]), got_a1, got_ax]
+    up_g, low_g, small = call(
+        functools.partial(final_kernel, nwl),
+        packs1
+        + [after(dx0, down[0], up2), dx1, dx2, dx3, x_win, dh, vecs, vec_mlp]
+        + [small3, small2, small01, dub01, dub2, dub3],
+        [((STRIP, D), BF)] * 2 + [((SMALL_ROWS, D), BF)],
+        scratch=[pltpu.VMEM((SMALL_ROWS, D), F32), pltpu.VMEM((rows, D), BF)]
+        + [pltpu.VMEM((PACK1, LANES), BF)] * TP
+        + [pltpu.SemaphoreType.DMA((TP,))],
+        hbm=TP,
+        name="final",
+    )
+    lower_g = shift_rows(low_g, 1)
+
+    attn = [after(a0, low_g), got_a1, got_ax]
+    small = [small]
     mlp = None
     gather_a = [b for b in reversed(bits) if b < blocks]
     gather_m = gather_a[:-2] + gather_a[:-3:-1]
     steps = len(bits) + len(gather_a)
     for i in range(steps):
-        if i == 0:
-            mark = added(attn)
-            attn = scatter_step([mark], bits[i], blocks)
-            loaded = [after(dx0, mark), dx1, dx2, dx3] + packs1 + [x_win, dh]
-            up_g, low_g, small = call(
-                functools.partial(final_kernel, nwl),
-                loaded + [vecs, vec_mlp, small3, small2, small01, dub01, dub2, dub3],
-                [((STRIP, D), BF)] * 2 + [((SMALL_ROWS, D), BF)],
-                scratch=[pltpu.VMEM((SMALL_ROWS, D), F32), pltpu.VMEM((rows, D), BF)]
-                + [pltpu.VMEM(a.shape, a.dtype) for a in loaded]
-                + [pltpu.SemaphoreType.DMA((len(loaded),))],
-                hbm=len(loaded),
-                name="final",
-            )
-            small = [small]
-            lower_g = shift_rows(low_g, 1)
-        elif i < len(bits):
+        if i < len(bits):
             mark = added(attn)
             attn, small = riding_step([mark], small, bits[i], blocks)
         else:
             mark = added(attn) if i == len(bits) else jnp.concatenate(attn, axis=0)
             attn = [mark, swap_rows(mark, gather_a[i - len(bits)])]
         if i == 0:
-            down = added([after(down[0], mark), down[1]])
-            up = added([up0, up_x])
-            mlp = scatter_step([interleaved([down, up], blocks // 2)], bits[1], blocks)
+            down = scatter_step([after(down[0], mark), down[1]], bits[0], blocks)
+            up = scatter_step([after(up0, mark), up_x], bits[1], blocks)
             from_x = swap_tp(after(page_own, mark), 2)
         elif i + 1 < steps:
-            kept = after(mlp[0], mark)
-            if i + 1 < len(bits):
-                mlp = scatter_step([kept, mlp[1]], bits[i + 1], blocks)
+            if i == 1:
+                mlp = [added([after(down[0], mark), down[1]]), added([after(up[0], mark), up[1]])]
+                mlp = scatter_step([interleaved(mlp, blocks // 4)], bits[2], blocks)
+            elif i + 1 < len(bits):
+                mlp = scatter_step([after(mlp[0], mark), mlp[1]], bits[i + 1], blocks)
             else:
+                kept = after(mlp[0], mark)
                 first = i + 1 == len(bits)
                 total = added([kept, mlp[1]]) if first else jnp.concatenate([kept, mlp[1]], axis=0)
                 mlp = [total, swap_rows(total, gather_m[i + 1 - len(bits)])]
-        if i == 2:
-            own_g = jnp.concatenate([after(up_g, mark), lower_g], axis=0)
+        if i == len(bits):
+            small = added([after(small[0], mark), small[1]])
+            own_g = jnp.concatenate([up_g, lower_g, small], axis=0)
             g_x = swap_tp(own_g, 2)
             g_c = swap_tp(own_g, 1)
-        if i == len(bits):
-            small = added([after(small[0], mark), small[1]])
-            small = [small, swap_rows(small, bits[0])]
             from_cx = swap_tp(after(from_x, mark), 1)
-        if i == len(bits) + 1:
-            small = added([after(small[0], mark), small[1]])
-            s_x = swap_tp(small, 2)
-            s_c = swap_tp(small, 1)
     g_cx = swap_tp(after(g_x, mark), 1)
-    s_cx = swap_tp(after(s_x, mark), 1)
     block_out = page([after(page_own, mark), from_c, from_x, from_cx], patches.shape, "page_y")
     grad_patches = page([after(own_g, mark), g_c, g_x, g_cx], patches.shape, "page_g")
-    *v, mine = call(
+    *v, qvb_line, up_line, table = call(
         small_kernel,
-        [small, s_c, s_x, s_cx],
-        [((1, D), F32)] * 6 + [((SMALL_SHARD, LANES), F32)],
+        [own_g, g_c, g_x, g_cx],
+        [((1, D), F32)] * 6 + [((2, LANES), F32), ((D // LANES, LANES), F32), ((HEADS_HERE, TABLE), F32)],
         name="small",
     )
-    attn[0] = after(attn[0], block_out, grad_patches, mine)
+    attn[0] = after(attn[0], block_out, grad_patches, table)
     grad_qkv, grad_proj = finish(attn, blocks, gather_a, "finish_attn")
     grad_down, grad_up = finish([after(mlp[0], grad_qkv), mlp[1]], blocks, gather_m, "finish_mlp")
 
     v = [line.reshape(D) for line in v]
-    grad_pos_table = mine[:12].reshape(HEADS_HERE, TABLE_PAD)[:, :TABLE].T
 
     return (
         block_out,
@@ -1001,14 +1019,14 @@
         v[4],
         v[5],
         grad_qkv,
-        mine[12:14],
-        grad_pos_table,
+        qvb_line,
+        table.T,
         grad_proj,
         v[3],
         v[0],
         v[1],
         grad_up,
-        mine[16:20].reshape(D),
+        up_line.reshape(D),
         grad_down,
         v[2],
     )

time: 169 us -> 160 us (0.947)
  Pallas kernels: 80.1 us -> 69 us
  waiting for transfers between devices: 31.4 us -> 41.2 us
  starting transfers between devices: 47.5 us -> 41.6 us
  local copies, waits for them, and re-layouts: 6.41 us -> 3.87 us
    ppermute x14, waiting for transfers between devices: 18.5 us -> 39.2 us  [swap_rows(): lax.ppermute(x, 'rows', [(i, i ^ bit) for i in range(lax.axis_size('rows'...]
    pallas_call x15, Pallas kernels: 80.1 us -> 69 us  [call(): pl.pallas_call(kernel, out_shape=[jax.ShapeDtypeStruct(s, d) for s, d in...]
    ppermute x22 -> x19, waiting for transfers between devices: 11.3 us -> 1.94 us  [swap_tp(): return lax.ppermute(x, 'tp', [(i, i ^ bit) for i in range(TP)])]
    ppermute x14, starting transfers between devices: 23.5 us -> 19.8 us  [swap_rows(): lax.ppermute(x, 'rows', [(i, i ^ bit) for i in range(lax.axis_size('rows'...]
    ppermute x22 -> x19, starting transfers between devices: 13.7 us -> 12.3 us  [swap_tp(): return lax.ppermute(x, 'tp', [(i, i ^ bit) for i in range(TP)])]
    unnamed x52 -> x45, local copies, waits for them, and re-layouts: 3.83 us -> 3.04 us
  transfers between devices with their start and end apart: 40 -> 37, of which waited for: 13 -> 12; matrix products, arithmetic and copies ran while one was open for 3% -> 2% of each run, Pallas kernels for 42% -> 38%
where the time goes in v2:
time: 160 us; the launch traced here: 159 us
  Pallas kernels  69 us (43%)
  starting transfers between devices  41.6 us (26%)
  waiting for transfers between devices  41.2 us (26%)
  local copies, waits for them, and re-layouts  3.87 us (2%)
  other arithmetic  2.29 us (1%)
    pallas_call x15, Pallas kernels, call(): pl.pallas_call(kernel, out_shape=[jax.ShapeDtypeStruct(s, d) for s, d in...  69 us
    ppermute x14, waiting for transfers between devices, swap_rows(): lax.ppermute(x, 'rows', [(i, i ^ bit) for i in range(lax.axis_size('rows'...  39.2 us
    ppermute x14, starting transfers between devices, swap_rows(): lax.ppermute(x, 'rows', [(i, i ^ bit) for i in range(lax.axis_size('rows'...  19.8 us
    ppermute x19, starting transfers between devices, swap_tp(): return lax.ppermute(x, 'tp', [(i, i ^ bit) for i in range(TP)])  12.3 us
    ppermute x4, starting transfers between devices, shift_rows(): return lax.ppermute(x, 'rows', [(i, (i + distance) % n) for i in range(n)])  9.49 us
  transfers between devices with their start and end apart: 37, of which 12 were waited for; matrix products, arithmetic and copies ran while one was open for 2% of the time, Pallas kernels for 38%

profile of v2, /device:TPU:0, one launch (start us, length us, event | category | flops | bytes accessed | tf_op | source)
XLA Modules:
  0.0 159.3 jit_solution(8453729088173102945)
XLA Ops:
  0.7 3.1 %head.1 = (bf16[320,512]{1,0:T(8,128)(2,1)}, bf16[2080,128]{1,0:T(8,128)(2,1)}) custom-call(bf16[10,240,512]{2,1,0:T(8,128)(2,1)} %x.3, bf16[1536,128]{1,0:T(8,128)(2,1)} %bitcast.21, bf16[128,512]{1,0:T(8,128)(2,1)} %wproj.1, bf16[4,361]{1,0:T(4,128)(2,1)} %bitcast.23, bf16[2,128]{1,0:T(2,128)(2,1)} %bias.1), custom_call_target="tpu_custom_call" | custom-call | flops 600000000 | bytes 1024 | tf_op jit(solution)/shard_map/head/pallas_call | solution.py:148
  3.8 3.0 %collective-permute-start = (bf16[2080,128]{1,0:T(8,128)(2,1)}, bf16[2080,128]{1,0:T(8,128)(2,1)S(1)}, u32[]{:S(2)}, u32[]{:S(2)}) collective-permute-start(bf16[2080,128]{1,0:T(8,128)(2,1)} %get-tuple-element.113.refs_0_), channel_id=1, source_target_pairs={{0,2},{1,3},{2,0},{3,1},{4,6},{5,7},{6,4},{7,5},{8,10},{9,11},{10,... | collective-permute-start | bytes 1597448 | tf_op jit(solution)/shard_map/ppermute | solution.py:677
  6.8 4.6 %collective-permute-start.4 = (bf16[320,512]{1,0:T(8,128)(2,1)}, bf16[320,512]{1,0:T(8,128)(2,1)S(1)}, u32[]{:S(2)}, u32[]{:S(2)}) collective-permute-start(bf16[320,512]{1,0:T(8,128)(2,1)} %get-tuple-element.110), channel_id=1, source_target_pairs={{0,28},{4,0},{8,4},{12,8},{16,12},{20,16},{24,20},{28,24},{1,29},{... | collective-permute-start | bytes 983048 | tf_op jit(solution)/shard_map/ppermute | solution.py:686
  11.5 0.6 convert_element_type.190.refs_6_.refs_10_
  12.1 0.6 broadcast_in_dim.3.ubias
  12.7 4.7 %rest.1 = (bf16[320,512]{1,0:T(8,128)(2,1)}, bf16[704,512]{1,0:T(8,128)(2,1)}, bf16[704,512]{1,0:T(8,128)(2,1)}, bf16[1040,512]{1,0:T(8,128)(2,1)}) custom-call(bf16[10,240,512]{2,1,0:T(8,128)(2,1)} %x.3, bf16[10,240,512]{2,1,0:T(8,128)(2,1)} %g, bf16[512,512]{1,0:T(8,128)(2,1)} %up.1, bf16[512,512]{1,0:T(8,128)(2,1)} %down.1, ...), custom_call_target="tpu_custom_call" | custom-call | flops 1000000000 | bytes 1024 | tf_op jit(solution)/shard_map/rest/pallas_call | solution.py:148
  17.4 0.3 collective-permute-start.2
  17.7 1.4 collective-permute-done.refs_2_.refs_0_
  19.1 1.7 %collective-permute-start.1 = (bf16[1040,512]{1,0:T(8,128)(2,1)}, bf16[1040,512]{1,0:T(8,128)(2,1)S(1)}, u32[]{:S(2)}, u32[]{:S(2)}) collective-permute-start(bf16[1040,512]{1,0:T(8,128)(2,1)} %get-tuple-element.114.refs_0_), channel_id=1, source_target_pairs={{0,2},{1,3},{2,0},{3,1},{4,6},{5,7},{6,4},{7,5},{8,10},{9,11},{10,... | collective-permute-start | bytes 3194888 | tf_op jit(solution)/shard_map/ppermute | solution.py:677
  21.0 4.6 %collective-permute-start.6 = (bf16[320,512]{1,0:T(8,128)(2,1)}, bf16[320,512]{1,0:T(8,128)(2,1)S(1)}, u32[]{:S(2)}, u32[]{:S(2)}) collective-permute-start(bf16[320,512]{1,0:T(8,128)(2,1)} %get-tuple-element.115), channel_id=1, source_target_pairs={{0,28},{4,0},{8,4},{12,8},{16,12},{20,16},{24,20},{28,24},{1,29},{... | collective-permute-start | bytes 983048 | tf_op jit(solution)/shard_map/ppermute | solution.py:686
  25.6 0.8 copy-done.11
  26.4 12.7 %attn_fwd.1 = (bf16[3,704,128]{2,1,0:T(8,128)(2,1)}, bf16[3,704,128]{2,1,0:T(8,128)(2,1)}, bf16[3,704,128]{2,1,0:T(8,128)(2,1)}, bf16[3,704,128]{2,1,0:T(8,128)(...) custom-call(s32[1,2]{1,0:T(1,128)} %bounds.1, ...), custom_call_target="tpu_custom_call" | custom-call | flops 2800000000 | bytes 1024 | tf_op jit(solution)/shard_map/attn_fwd/pallas_call | solution.py:148
  39.1 1.0 copy-done.19
  40.1 1.1 copy-done
  41.2 7.0 %mlp_first.1 = (bf16[1024,512]{1,0:T(8,128)(2,1)S(1)}, bf16[1024,512]{1,0:T(8,128)(2,1)S(1)}, f32[8,128]{1,0:T(8,128)S(1)}, bf16[704,512]{1,0:T(8,128)(2,1)S(1)}...) custom-call(bf16[1040,512]{1,0:T(8,128)(2,1)} %get-tuple-element.114.refs_0_, bf16[1040,512]{1,0:T(8,128)(2,1)} %copy-done.19, ...), custom_call_target="tpu_custom_call" | custom-call | flops 1800000000 | bytes 1024 | tf_op jit(solution)/shard_map/mlp_first/pallas_call | solution.py:148
  48.3 0.2 collective-permute-start.7
  48.5 2.8 %mlp_mid.1 = (bf16[1024,512]{1,0:T(8,128)(2,1)S(1)}, f32[4,128]{1,0:T(4,128)S(1)}, f32[704,512]{1,0:T(8,128)S(1)}, f32[704,512]{1,0:T(8,128)S(1)}) custom-call(bf16[1040,512]{1,0:T(8,128)(2,1)S(1)} %collective-permute-done.1.refs_0_, bf16[704,512]{1,0:T(8,128)(2,1)S(1)} %copy-done.1, bf16[704,512]{1,0:T(8,128)(2,1)S(1)} %get-tuple-element.122.refs_2_, ...), custom_call_target="tpu_custom_call" | custom-call | flops 1000000000 | bytes 1024 | tf_op jit(solution)/shard_map/mlp_mid/pallas_call | solution.py:148
  51.3 4.2 %mlp_last.1 = (bf16[1024,512]{1,0:T(8,128)(2,1)S(1)}, f32[4,128]{1,0:T(4,128)S(1)}, bf16[320,512]{1,0:T(8,128)(2,1)S(1)}, bf16[320,512]{1,0:T(8,128)(2,1)S(1)}, ...) custom-call(bf16[1040,512]{1,0:T(8,128)(2,1)S(1)} %collective-permute-done.7.refs_0_, ...), custom_call_target="tpu_custom_call" | custom-call | flops 1000000000 | bytes 1024 | tf_op jit(solution)/shard_map/mlp_last/pallas_call | solution.py:148
  55.5 0.4 collective-permute-start.8
  55.9 0.2 collective-permute-start.9
  56.1 6.1 %attn_bwd_3.1 = (bf16[512,512]{1,0:T(8,128)(2,1)S(1)}, f32[16,128]{1,0:T(8,128)S(1)}, bf16[704,384]{1,0:T(8,128)(2,1)S(1)}) custom-call(bf16[2080,128]{1,0:T(8,128)(2,1)} %copy-done.11, bf16[704,128]{1,0:T(8,128)(2,1)} %get-tuple-element.134.refs_1_, bf16[3,704,128]{2,1,0:T(8,128)(2,1)} %get-tuple-element.135.refs_2_, ...), custom_call_target="tpu_custom_call" | custom-call | flops 1400000000 | bytes 1024 | tf_op jit(solution)/shard_map/attn_bwd_3/pallas_call | solution.py:148
  62.2 0.4 collective-permute-start.11
  62.6 0.3 add_convert_fusion.3
  63.1 0.6 collective-permute-start.12
  63.7 5.9 %attn_bwd_2.1 = (bf16[512,512]{1,0:T(8,128)(2,1)S(1)}, f32[16,128]{1,0:T(8,128)S(1)}, bf16[704,384]{1,0:T(8,128)(2,1)S(1)}) custom-call(bf16[2080,128]{1,0:T(8,128)(2,1)} %copy-done.9, bf16[704,128]{1,0:T(8,128)(2,1)} %get-tuple-element.128.refs_1_, bf16[3,704,128]{2,1,0:T(8,128)(2,1)} %get-tuple-element.129.refs_2_, ...), custom_call_target="tpu_custom_call" | custom-call | flops 1400000000 | bytes 1024 | tf_op jit(solution)/shard_map/attn_bwd_2/pallas_call | solution.py:148
  69.7 1.6 collective-permute-start.15
  71.3 0.4 collective-permute-start.13
  71.7 10.3 %attn_bwd_01.1 = (bf16[512,512]{1,0:T(8,128)(2,1)S(1)}, bf16[512,512]{1,0:T(8,128)(2,1)S(1)}, f32[32,128]{1,0:T(8,128)S(1)}, bf16[704,384]{1,0:T(8,128)(2,1)S(1)}, bf16[704,384]{1,0:T(8,128)(2,1)S(1)}) custom-call(bf16[2080,128]{1,0:T(8,128)(2,1)} %get-tuple-element.113.refs_0_, bf16[2080,128]{1,0:T(8,128)(2,1)} %copy-done.10, ...), custom_call_target="tpu_custom_call" | custom-call | flops 2200000000 | bytes 1024 | tf_op jit(solution)/shard_map/attn_bwd_01/pallas_call | solution.py:148
  82.2 0.6 collective-permute-start.21
  82.8 0.2 add_convert_fusion.1
  83.0 3.3 %collective-permute-done.13 = bf16[512,512]{1,0:T(8,128)(2,1)S(1)} collective-permute-done((bf16[512,512]{1,0:T(8,128)(2,1)S(1)}, bf16[512,512]{1,0:T(8,128)(2,1)S(1)}, u32[]{:S(2)}, u32[]{:S(2)}) %collective-permute-start.13) | collective-permute-done | bytes 524320 | tf_op jit(solution)/shard_map/ppermute | solution.py:681
  86.4 0.6 collective-permute-start.31
  87.0 4.4 %final.1 = (bf16[320,512]{1,0:T(8,128)(2,1)S(1)}, bf16[320,512]{1,0:T(8,128)(2,1)S(1)}, bf16[32,512]{1,0:T(8,128)(2,1)S(1)}) custom-call(bf16[2080,128]{1,0:T(8,128)(2,1)} %get-tuple-element.113.refs_0_, bf16[2080,128]{1,0:T(8,128)(2,1)} %copy-done.10, bf16[2080,128]{1,0:T(8,128)(2,1)} %copy-done.9, bf16[2080,128]{1,0:T(8,128)(2,1)} %copy-done.11, ...), custom_call_target="tpu_custom_call" | custom-call | flops 200000000 | bytes 1024 | tf_op jit(solution)/shard_map/final/pallas_call | solution.py:148
  91.5 0.2 add_convert_fusion
  91.7 0.3 collective-permute-start.24
  92.1 0.6 collective-permute-start.16
  92.6 1.6 collective-permute-start.29
  94.2 0.5 collective-permute-done.31
  94.7 0.5 collective-permute-start.22
  95.4 4.8 %collective-permute-done.29 = bf16[256,512]{1,0:T(8,128)(2,1)S(1)} collective-permute-done((bf16[256,512]{1,0:T(8,128)(2,1)S(1)}, bf16[256,512]{1,0:T(8,128)(2,1)S(1)}, u32[]{:S(2)}, u32[]{:S(2)}) %collective-permute-start.29) | collective-permute-done | bytes 262176 | tf_op jit(solution)/shard_map/ppermute | solution.py:681
  100.2 1.6 collective-permute-start.32
  101.8 6.0 %collective-permute-done.16 = bf16[288,512]{1,0:T(8,128)(2,1)S(1)} collective-permute-done((bf16[288,512]{1,0:T(8,128)(2,1)S(1)}, bf16[288,512]{1,0:T(8,128)(2,1)S(1)}, u32[]{:S(2)}, u32[]{:S(2)}) %collective-permute-start.16) | collective-permute-done | bytes 294944 | tf_op jit(solution)/shard_map/ppermute | solution.py:681
  107.8 1.2 collective-permute-start.30
  109.2 2.1 %collective-permute-start.17 = (bf16[160,512]{1,0:T(8,128)(2,1)S(1)}, bf16[160,512]{1,0:T(8,128)(2,1)S(1)}, u32[]{:S(2)}, u32[]{:S(2)}) collective-permute-start(bf16[160,512]{1,0:T(8,128)(2,1)S(1)} %pad_maximum_fusion.4), channel_id=1, source_target_pairs={{0,8},{4,12},{8,0},{12,4},{16,24},{20,28},{24,16},{28,20},{1,9},{5... | collective-permute-start | bytes 491528 | tf_op jit(solution)/shard_map/ppermute | solution.py:681
  111.3 1.5 collective-permute-done.30
  112.8 1.7 %collective-permute-done.17 = bf16[160,512]{1,0:T(8,128)(2,1)S(1)} collective-permute-done((bf16[160,512]{1,0:T(8,128)(2,1)S(1)}, bf16[160,512]{1,0:T(8,128)(2,1)S(1)}, u32[]{:S(2)}, u32[]{:S(2)}) %collective-permute-start.17) | collective-permute-done | bytes 163872 | tf_op jit(solution)/shard_map/ppermute | solution.py:681
  114.6 2.8 %collective-permute-start.18 = (bf16[96,512]{1,0:T(8,128)(2,1)S(1)}, bf16[96,512]{1,0:T(8,128)(2,1)S(1)}, u32[]{:S(2)}, u32[]{:S(2)}) collective-permute-start(bf16[96,512]{1,0:T(8,128)(2,1)S(1)} %pad_maximum_fusion.7), channel_id=1, source_target_pairs={{0,16},{4,20},{8,24},{12,28},{16,0},{20,4},{24,8},{28,12},{1,17},{... | collective-permute-start | bytes 294920 | tf_op jit(solution)/shard_map/ppermute | solution.py:681
  117.5 0.2 collective-permute-start.33
  117.7 6.9 %collective-permute-done.18 = bf16[96,512]{1,0:T(8,128)(2,1)S(1)} collective-permute-done((bf16[96,512]{1,0:T(8,128)(2,1)S(1)}, bf16[96,512]{1,0:T(8,128)(2,1)S(1)}, u32[]{:S(2)}, u32[]{:S(2)}) %collective-permute-start.18) | collective-permute-done | bytes 98336 | tf_op jit(solution)/shard_map/ppermute | solution.py:681
  124.7 1.5 collective-permute-start.26
  126.4 2.9 %collective-permute-start.19 = (bf16[64,512]{1,0:T(8,128)(2,1)S(1)}, bf16[64,512]{1,0:T(8,128)(2,1)S(1)}, u32[]{:S(2)}, u32[]{:S(2)}) collective-permute-start(bf16[64,512]{1,0:T(8,128)(2,1)S(1)} %add_convert_fusion.15), channel_id=1, source_target_pairs={{0,16},{4,20},{8,24},{12,28},{16,0},{20,4},{24,8},{28,12},{1,17},{... | collective-permute-start | bytes 196616 | tf_op jit(solution)/shard_map/ppermute | solution.py:681
  129.3 7.8 %collective-permute-done.19 = bf16[64,512]{1,0:T(8,128)(2,1)S(1)} collective-permute-done((bf16[64,512]{1,0:T(8,128)(2,1)S(1)}, bf16[64,512]{1,0:T(8,128)(2,1)S(1)}, u32[]{:S(2)}, u32[]{:S(2)}) %collective-permute-start.19) | collective-permute-done | bytes 65568 | tf_op jit(solution)/shard_map/ppermute | solution.py:681
  137.3 2.7 %collective-permute-start.35 = (bf16[256,512]{1,0:T(8,128)(2,1)S(1)}, bf16[256,512]{1,0:T(8,128)(2,1)S(1)}, u32[]{:S(2)}, u32[]{:S(2)}) collective-permute-start(bf16[256,512]{1,0:T(8,128)(2,1)S(1)} %constant_dynamic-update-slice_fusion.2), channel_id=1, source_target_pairs={{0,4},{4,0},{8,12},{12,8},{16,20},{20,16},{24,28},{28,24},{1,5},{5... | collective-permute-start | bytes 786440 | tf_op jit(solution)/shard_map/ppermute | solution.py:681
  140.0 2.2 %collective-permute-done.20 = bf16[128,512]{1,0:T(8,128)(2,1)S(1)} collective-permute-done((bf16[128,512]{1,0:T(8,128)(2,1)S(1)}, bf16[128,512]{1,0:T(8,128)(2,1)S(1)}, u32[]{:S(2)}, u32[]{:S(2)}) %collective-permute-start.20) | collective-permute-done | bytes 131104 | tf_op jit(solution)/shard_map/ppermute | solution.py:681
  142.2 0.6 collective-permute-start.27
  142.8 2.7 %collective-permute-done.35 = bf16[256,512]{1,0:T(8,128)(2,1)S(1)} collective-permute-done((bf16[256,512]{1,0:T(8,128)(2,1)S(1)}, bf16[256,512]{1,0:T(8,128)(2,1)S(1)}, u32[]{:S(2)}, u32[]{:S(2)}) %collective-permute-start.35) | collective-permute-done | bytes 262176 | tf_op jit(solution)/shard_map/ppermute | solution.py:681
  145.5 1.8 %collective-permute-start.36 = (bf16[512,512]{1,0:T(8,128)(2,1)S(1)}, bf16[512,512]{1,0:T(8,128)(2,1)S(1)}, u32[]{:S(2)}, u32[]{:S(2)}) collective-permute-start(bf16[512,512]{1,0:T(8,128)(2,1)S(1)} %constant_dynamic-update-slice_fusion.4.refs_0_), channel_id=1, source_target_pairs={{0,8},{4,12},{8,0},{12,4},{16,24},{20,28},{24,16},{28,20},{1,9},{5... | collective-permute-start | bytes 1572872 | tf_op jit(solution)/shard_map/ppermute | solution.py:681
  147.3 1.7 %collective-permute-start.28 = (bf16[256,512]{1,0:T(8,128)(2,1)S(1)}, bf16[256,512]{1,0:T(8,128)(2,1)S(1)}, u32[]{:S(2)}, u32[]{:S(2)}) collective-permute-start(bf16[256,512]{1,0:T(8,128)(2,1)S(1)} %pad_maximum_fusion.3.refs_0_), channel_id=1, source_target_pairs={{0,4},{4,0},{8,12},{12,8},{16,20},{20,16},{24,28},{28,24},{1,5},{5... | collective-permute-start | bytes 786440 | tf_op jit(solution)/shard_map/ppermute | solution.py:681
  149.0 2.3 %page_y.1 = bf16[10,240,512]{2,1,0:T(8,128)(2,1)} custom-call(bf16[640,512]{1,0:T(8,128)(2,1)S(1)} %constant_dynamic-update-slice_fusion.refs_0_, bf16[640,512]{1,0:T(8,128)(2,1)S(1)} %collective-permute-done.21.refs_1_, bf16[640,512]{1,0:T(8,128)(2,1)S(1)} %collective-permute-done.22.refs_2_, bf16[640,512]{1,0:T(8,128)(2,1)S(1)} %collective-permute-done.23.refs_3_), custom_call_target="tpu_custom_call" | custom-call | flops 2000000 | bytes 1024 | tf_op jit(solution)/shard_map/page_y/pallas_call | solution.py:148
  151.4 0.6 small.1
  152.0 2.3 %page_g.1 = bf16[10,240,512]{2,1,0:T(8,128)(2,1)} custom-call(bf16[672,512]{1,0:T(8,128)(2,1)S(1)} %pad_maximum_fusion.refs_0_, bf16[672,512]{1,0:T(8,128)(2,1)S(1)} %collective-permute-done.25.refs_1_, bf16[672,512]{1,0:T(8,128)(2,1)S(1)} %collective-permute-done.26.refs_2_, bf16[672,512]{1,0:T(8,128)(2,1)S(1)} %collective-permute-done.27.refs_3_), custom_call_target="tpu_custom_call" | custom-call | flops 2000000 | bytes 1024 | tf_op jit(solution)/shard_map/page_g/pallas_call | solution.py:148
  154.3 1.1 finish_attn.1
  155.5 2.3 %collective-permute-done.36.refs_1_ = bf16[512,512]{1,0:T(8,128)(2,1)S(1)} collective-permute-done((bf16[512,512]{1,0:T(8,128)(2,1)S(1)}, bf16[512,512]{1,0:T(8,128)(2,1)S(1)}, u32[]{:S(2)}, u32[]{:S(2)}) %collective-permute-start.36) | collective-permute-done | bytes 524320 | tf_op jit(solution)/shard_map/ppermute | solution.py:681
  157.8 1.5 finish_mlp.1
  (116 shorter events, 1.8 us)
Async XLA Ops:
  0.7 10.7 %copy-start.12 = (bf16[512]{0:T(512)(128)(2,1)S(1)}, bf16[512]{0:T(512)(128)(2,1)}, u32[]{:S(2)}) copy-start(bf16[512]{0:T(512)(128)(2,1)} %param.19) | copy-start | bytes 3076
  0.7 10.7 %copy-start.13 = (bf16[512]{0:T(512)(128)(2,1)S(1)}, bf16[512]{0:T(512)(128)(2,1)}, u32[]{:S(2)}) copy-start(bf16[512]{0:T(512)(128)(2,1)} %param.20) | copy-start | bytes 3076
  0.7 10.7 %copy-start.14 = (bf16[512]{0:T(512)(128)(2,1)S(1)}, bf16[512]{0:T(512)(128)(2,1)}, u32[]{:S(2)}) copy-start(bf16[512]{0:T(512)(128)(2,1)} %param.26) | copy-start | bytes 3076
  0.7 10.7 %copy-start.15 = (bf16[512]{0:T(512)(128)(2,1)S(1)}, bf16[512]{0:T(512)(128)(2,1)}, u32[]{:S(2)}) copy-start(bf16[512]{0:T(512)(128)(2,1)} %param.27) | copy-start | bytes 3076
  0.7 10.7 %copy-start.16 = (bf16[512]{0:T(512)(128)(2,1)S(1)}, bf16[512]{0:T(512)(128)(2,1)}, u32[]{:S(2)}) copy-start(bf16[512]{0:T(512)(128)(2,1)} %param.25) | copy-start | bytes 3076
  0.7 10.8 %copy-start.17 = (bf16[512]{0:T(512)(128)(2,1)S(1)}, bf16[512]{0:T(512)(128)(2,1)}, u32[]{:S(2)}) copy-start(bf16[512]{0:T(512)(128)(2,1)} %param.31) | copy-start | bytes 3076
  0.7 11.4 %copy-start.18 = (bf16[512]{0:T(512)(128)(2,1)S(1)}, bf16[512]{0:T(512)(128)(2,1)}, u32[]{:S(2)}) copy-start(bf16[512]{0:T(512)(128)(2,1)} %param.29) | copy-start | bytes 3076
  3.8 15.3 %collective-permute-start = (bf16[2080,128]{1,0:T(8,128)(2,1)}, bf16[2080,128]{1,0:T(8,128)(2,1)S(1)}, u32[]{:S(2)}, u32[]{:S(2)}) collective-permute-start(bf16[2080,128]{1,0:T(8,128)(2,1)} %get-tuple-element.113.refs_0_), channel_id=1, source_target_pairs={{0,2},{1,3},{2,0},{3,1},{4,6},{5,7},{6,4},{7,5},{8,10},{9,11},{10,... | collective-permute-start | bytes 1597448 | tf_op jit(solution)/shard_map/ppermute | solution.py:677
  6.8 14.1 %collective-permute-start.3 = (bf16[2080,128]{1,0:T(8,128)(2,1)}, bf16[2080,128]{1,0:T(8,128)(2,1)S(1)}, u32[]{:S(2)}, u32[]{:S(2)}) collective-permute-start(bf16[2080,128]{1,0:T(8,128)(2,1)} %get-tuple-element.113.refs_0_), channel_id=1, source_target_pairs={{0,1},{1,0},{2,3},{3,2},{4,5},{5,4},{6,7},{7,6},{8,9},{9,8},{10,11... | collective-permute-start | bytes 1597448 | tf_op jit(solution)/shard_map/ppermute | solution.py:677
  6.8 14.1 %collective-permute-start.4 = (bf16[320,512]{1,0:T(8,128)(2,1)}, bf16[320,512]{1,0:T(8,128)(2,1)S(1)}, u32[]{:S(2)}, u32[]{:S(2)}) collective-permute-start(bf16[320,512]{1,0:T(8,128)(2,1)} %get-tuple-element.110), channel_id=1, source_target_pairs={{0,28},{4,0},{8,4},{12,8},{16,12},{20,16},{24,20},{28,24},{1,29},{... | collective-permute-start | bytes 983048 | tf_op jit(solution)/shard_map/ppermute | solution.py:686
  17.4 21.7 %collective-permute-start.2 = (bf16[1040,512]{1,0:T(8,128)(2,1)}, bf16[1040,512]{1,0:T(8,128)(2,1)S(1)}, u32[]{:S(2)}, u32[]{:S(2)}) collective-permute-start(bf16[1040,512]{1,0:T(8,128)(2,1)} %get-tuple-element.114.refs_0_), channel_id=1, source_target_pairs={{0,1},{1,0},{2,3},{3,2},{4,5},{5,4},{6,7},{7,6},{8,9},{9,8},{10,11... | collective-permute-start | bytes 3194888 | tf_op jit(solution)/shard_map/ppermute | solution.py:677
  19.1 6.5 %copy-start.9 = (bf16[2080,128]{1,0:T(8,128)(2,1)}, bf16[2080,128]{1,0:T(8,128)(2,1)S(1)}, u32[]{:S(2)}) copy-start(bf16[2080,128]{1,0:T(8,128)(2,1)S(1)} %collective-permute-done.refs_2_.refs_0_) | copy-start | bytes 1597444
  19.1 29.2 %collective-permute-start.1 = (bf16[1040,512]{1,0:T(8,128)(2,1)}, bf16[1040,512]{1,0:T(8,128)(2,1)S(1)}, u32[]{:S(2)}, u32[]{:S(2)}) collective-permute-start(bf16[1040,512]{1,0:T(8,128)(2,1)} %get-tuple-element.114.refs_0_), channel_id=1, source_target_pairs={{0,2},{1,3},{2,0},{3,1},{4,6},{5,7},{6,4},{7,5},{8,10},{9,11},{10,... | collective-permute-start | bytes 3194888 | tf_op jit(solution)/shard_map/ppermute | solution.py:677
  20.9 4.7 %copy-start.20 = (bf16[320,512]{1,0:T(8,128)(2,1)}, bf16[320,512]{1,0:T(8,128)(2,1)S(1)}, u32[]{:S(2)}) copy-start(bf16[320,512]{1,0:T(8,128)(2,1)S(1)} %collective-permute-done.4.refs_5_) | copy-start | bytes 983044
  20.9 4.7 %copy-start.10 = (bf16[2080,128]{1,0:T(8,128)(2,1)}, bf16[2080,128]{1,0:T(8,128)(2,1)S(1)}, u32[]{:S(2)}) copy-start(bf16[2080,128]{1,0:T(8,128)(2,1)S(1)} %collective-permute-done.3.refs_1_) | copy-start | bytes 1597444
  20.9 4.7 %collective-permute-start.5 = (bf16[2080,128]{1,0:T(8,128)(2,1)S(1)}, bf16[2080,128]{1,0:T(8,128)(2,1)S(1)}, u32[]{:S(2)}, u32[]{:S(2)}) collective-permute-start(bf16[2080,128]{1,0:T(8,128)(2,1)S(1)} %collective-permute-done.refs_2_.refs_0_), channel_id=1, source_target_pairs={{0,1},{1,0},{2,3},{3,2},{4,5},{5,4},{6,7},{7,6},{8,9},{9,8},{10,11... | collective-permute-start | bytes 1597448 | tf_op jit(solution)/shard_map/ppermute | solution.py:677
  21.0 18.1 %collective-permute-start.6 = (bf16[320,512]{1,0:T(8,128)(2,1)}, bf16[320,512]{1,0:T(8,128)(2,1)S(1)}, u32[]{:S(2)}, u32[]{:S(2)}) collective-permute-start(bf16[320,512]{1,0:T(8,128)(2,1)} %get-tuple-element.115), channel_id=1, source_target_pairs={{0,28},{4,0},{8,4},{12,8},{16,12},{20,16},{24,20},{28,24},{1,29},{... | collective-permute-start | bytes 983048 | tf_op jit(solution)/shard_map/ppermute | solution.py:686
  25.6 0.8 copy-start.11
  26.4 13.7 %copy-start.5 = (bf16[704,512]{1,0:T(8,128)(2,1)S(1)}, bf16[704,512]{1,0:T(8,128)(2,1)}, u32[]{:S(2)}) copy-start(bf16[704,512]{1,0:T(8,128)(2,1)} %get-tuple-element.119.refs_3_) | copy-start | bytes 2162692
  39.1 1.0 copy-start.19
  40.1 1.1 copy-start
  41.2 7.3 %copy-start.1 = (bf16[704,512]{1,0:T(8,128)(2,1)S(1)}, bf16[704,512]{1,0:T(8,128)(2,1)}, u32[]{:S(2)}) copy-start(bf16[704,512]{1,0:T(8,128)(2,1)} %get-tuple-element.118.refs_2_.refs_1_) | copy-start | bytes 2162692
  48.3 3.0 %collective-permute-start.7 = (bf16[1040,512]{1,0:T(8,128)(2,1)S(1)}, bf16[1040,512]{1,0:T(8,128)(2,1)S(1)}, u32[]{:S(2)}, u32[]{:S(2)}) collective-permute-start(bf16[1040,512]{1,0:T(8,128)(2,1)S(1)} %collective-permute-done.1.refs_0_), channel_id=1, source_target_pairs={{0,1},{1,0},{2,3},{3,2},{4,5},{5,4},{6,7},{7,6},{8,9},{9,8},{10,11... | collective-permute-start | bytes 3194888 | tf_op jit(solution)/shard_map/ppermute | solution.py:677
  48.5 2.8 %copy-start.2 = (f32[704,512]{1,0:T(8,128)S(1)}, f32[704,512]{1,0:T(8,128)}, u32[]{:S(2)}) copy-start(f32[704,512]{1,0:T(8,128)} %get-tuple-element.126.refs_5_) | copy-start | bytes 4325380
  48.5 2.8 %copy-start.4 = (f32[6,512]{1,0:T(8,128)S(1)}, f32[6,512]{1,0:T(8,128)}, u32[]{:S(2)}) copy-start(f32[6,512]{1,0:T(8,128)} %convert_element_type.190.refs_6_.refs_10_) | copy-start | bytes 36868
  51.3 4.8 %copy-start.6 = (bf16[704,512]{1,0:T(8,128)(2,1)S(1)}, bf16[704,512]{1,0:T(8,128)(2,1)}, u32[]{:S(2)}) copy-start(bf16[704,512]{1,0:T(8,128)(2,1)} %get-tuple-element.137.refs_5_.refs_9_) | copy-start | bytes 2162692
  55.5 7.1 %collective-permute-start.8 = (bf16[1024,512]{1,0:T(8,128)(2,1)S(1)}, bf16[1024,512]{1,0:T(8,128)(2,1)S(1)}, u32[]{:S(2)}, u32[]{:S(2)}) collective-permute-start(bf16[1024,512]{1,0:T(8,128)(2,1)S(1)} %get-tuple-element.133), channel_id=1, source_target_pairs={{0,1},{1,0},{2,3},{3,2},{4,5},{5,4},{6,7},{7,6},{8,9},{9,8},{10,11... | collective-permute-start | bytes 3145736 | tf_op jit(solution)/shard_map/ppermute | solution.py:677
  55.9 7.0 %collective-permute-start.9 = (bf16[1024,512]{1,0:T(8,128)(2,1)S(1)}, bf16[1024,512]{1,0:T(8,128)(2,1)S(1)}, u32[]{:S(2)}, u32[]{:S(2)}) collective-permute-start(bf16[1024,512]{1,0:T(8,128)(2,1)S(1)} %get-tuple-element.142), channel_id=1, source_target_pairs={{0,1},{1,0},{2,3},{3,2},{4,5},{5,4},{6,7},{7,6},{8,9},{9,8},{10,11... | collective-permute-start | bytes 3145736 | tf_op jit(solution)/shard_map/ppermute | solution.py:677
  62.2 7.4 %collective-permute-start.11 = (bf16[512,512]{1,0:T(8,128)(2,1)S(1)}, bf16[512,512]{1,0:T(8,128)(2,1)S(1)}, u32[]{:S(2)}, u32[]{:S(2)}) collective-permute-start(bf16[512,512]{1,0:T(8,128)(2,1)S(1)} %get-tuple-element.138), channel_id=1, source_target_pairs={{0,1},{1,0},{2,3},{3,2},{4,5},{5,4},{6,7},{7,6},{8,9},{9,8},{10,11... | collective-permute-start | bytes 1572872 | tf_op jit(solution)/shard_map/ppermute | solution.py:677
  62.6 19.6 %collective-permute-start.10 = (bf16[320,512]{1,0:T(8,128)(2,1)S(1)}, bf16[320,512]{1,0:T(8,128)(2,1)S(1)}, u32[]{:S(2)}, u32[]{:S(2)}) collective-permute-start(bf16[320,512]{1,0:T(8,128)(2,1)S(1)} %get-tuple-element.146), channel_id=1, source_target_pairs={{0,4},{4,8},{8,12},{12,16},{16,20},{20,24},{24,28},{28,0},{1,5},{5... | collective-permute-start | bytes 983048 | tf_op jit(solution)/shard_map/ppermute | solution.py:686
  63.0 6.5 %copy-start.7 = (bf16[512,512]{1,0:T(8,128)(2,1)}, bf16[512,512]{1,0:T(8,128)(2,1)S(1)}, u32[]{:S(2)}) copy-start(bf16[512,512]{1,0:T(8,128)(2,1)S(1)} %add_convert_fusion.4) | copy-start | bytes 1572868
  63.1 19.7 %collective-permute-start.12 = (bf16[512,512]{1,0:T(8,128)(2,1)S(1)}, bf16[512,512]{1,0:T(8,128)(2,1)S(1)}, u32[]{:S(2)}, u32[]{:S(2)}) collective-permute-start(bf16[512,512]{1,0:T(8,128)(2,1)S(1)} %get-tuple-element.206), channel_id=1, source_target_pairs={{0,2},{1,3},{2,0},{3,1},{4,6},{5,7},{6,4},{7,5},{8,10},{9,11},{10,... | collective-permute-start | bytes 1572872 | tf_op jit(solution)/shard_map/ppermute | solution.py:677
  69.6 1.7 %slice-start = ((bf16[512,512]{1,0:T(8,128)(2,1)}), bf16[256,512]{1,0:T(8,128)(2,1)S(1)}, s32[]{:S(2)}) async-start(bf16[512,512]{1,0:T(8,128)(2,1)} %copy-done.7), calls=%async_computation | async-start | bytes 524288 | tf_op jit(solution)/shard_map/slice | solution.py:939
  69.7 21.7 %collective-permute-start.15 = (bf16[512,512]{1,0:T(8,128)(2,1)S(1)}, bf16[512,512]{1,0:T(8,128)(2,1)S(1)}, u32[]{:S(2)}, u32[]{:S(2)}) collective-permute-start(bf16[512,512]{1,0:T(8,128)(2,1)S(1)} %add_convert_fusion.2), channel_id=1, source_target_pairs={{0,2},{1,3},{2,0},{3,1},{4,6},{5,7},{6,4},{7,5},{8,10},{9,11},{10,... | collective-permute-start | bytes 1572872 | tf_op jit(solution)/shard_map/ppermute | solution.py:677
  71.3 15.0 %collective-permute-start.13 = (bf16[512,512]{1,0:T(8,128)(2,1)S(1)}, bf16[512,512]{1,0:T(8,128)(2,1)S(1)}, u32[]{:S(2)}, u32[]{:S(2)}) collective-permute-start(bf16[512,512]{1,0:T(8,128)(2,1)S(1)} %pad_maximum_fusion.1), channel_id=1, source_target_pairs={{0,4},{4,0},{8,12},{12,8},{16,20},{20,16},{24,28},{28,24},{1,5},{5... | collective-permute-start | bytes 1572872 | tf_op jit(solution)/shard_map/ppermute | solution.py:681
  82.0 9.4 %collective-permute-start.14 = (bf16[512,512]{1,0:T(8,128)(2,1)S(1)}, bf16[512,512]{1,0:T(8,128)(2,1)S(1)}, u32[]{:S(2)}, u32[]{:S(2)}) collective-permute-start(bf16[512,512]{1,0:T(8,128)(2,1)S(1)} %get-tuple-element.174), channel_id=1, source_target_pairs={{0,1},{1,0},{2,3},{3,2},{4,5},{5,4},{6,7},{7,6},{8,9},{9,8},{10,11... | collective-permute-start | bytes 1572872 | tf_op jit(solution)/shard_map/ppermute | solution.py:677
  82.2 4.1 %copy-start.8 = (bf16[512,512]{1,0:T(8,128)(2,1)S(1)}, bf16[512,512]{1,0:T(8,128)(2,1)}, u32[]{:S(2)}) copy-start(bf16[512,512]{1,0:T(8,128)(2,1)} %copy-done.7) | copy-start | bytes 1572868
  82.2 65.1 %collective-permute-start.21 = (bf16[640,512]{1,0:T(8,128)(2,1)S(1)}, bf16[640,512]{1,0:T(8,128)(2,1)S(1)}, u32[]{:S(2)}, u32[]{:S(2)}) collective-permute-start(bf16[640,512]{1,0:T(8,128)(2,1)S(1)} %constant_dynamic-update-slice_fusion.refs_0_), channel_id=1, source_target_pairs={{0,1},{1,0},{2,3},{3,2},{4,5},{5,4},{6,7},{7,6},{8,9},{9,8},{10,11... | collective-permute-start | bytes 1966088 | tf_op jit(solution)/shard_map/ppermute | solution.py:677
  83.0 4.1 %copy-start.3 = (bf16[704,512]{1,0:T(8,128)(2,1)S(1)}, bf16[704,512]{1,0:T(8,128)(2,1)}, u32[]{:S(2)}) copy-start(bf16[704,512]{1,0:T(8,128)(2,1)} %get-tuple-element.163.refs_8_) | copy-start | bytes 2162692
  86.4 8.3 %collective-permute-start.31 = (bf16[256,512]{1,0:T(8,128)(2,1)S(1)}, bf16[256,512]{1,0:T(8,128)(2,1)S(1)}, u32[]{:S(2)}, u32[]{:S(2)}) collective-permute-start(bf16[256,512]{1,0:T(8,128)(2,1)S(1)} %get-tuple-element.210), channel_id=1, source_target_pairs={{0,2},{1,3},{2,0},{3,1},{4,6},{5,7},{6,4},{7,5},{8,10},{9,11},{10,... | collective-permute-start | bytes 786440 | tf_op jit(solution)/shard_map/ppermute | solution.py:677
  91.7 33.0 %collective-permute-start.24 = (bf16[320,512]{1,0:T(8,128)(2,1)S(1)}, bf16[320,512]{1,0:T(8,128)(2,1)S(1)}, u32[]{:S(2)}, u32[]{:S(2)}) collective-permute-start(bf16[320,512]{1,0:T(8,128)(2,1)S(1)} %get-tuple-element.172), channel_id=1, source_target_pairs={{0,4},{4,8},{8,12},{12,16},{16,20},{20,24},{24,28},{28,0},{1,5},{5... | collective-permute-start | bytes 983048 | tf_op jit(solution)/shard_map/ppermute | solution.py:686
  92.1 15.7 %collective-permute-start.16 = (bf16[288,512]{1,0:T(8,128)(2,1)S(1)}, bf16[288,512]{1,0:T(8,128)(2,1)S(1)}, u32[]{:S(2)}, u32[]{:S(2)}) collective-permute-start(bf16[288,512]{1,0:T(8,128)(2,1)S(1)} %pad_maximum_fusion.2), channel_id=1, source_target_pairs={{0,4},{4,0},{8,12},{12,8},{16,20},{20,16},{24,28},{28,24},{1,5},{5... | collective-permute-start | bytes 884744 | tf_op jit(solution)/shard_map/ppermute | solution.py:681
  92.6 7.5 %collective-permute-start.29 = (bf16[256,512]{1,0:T(8,128)(2,1)S(1)}, bf16[256,512]{1,0:T(8,128)(2,1)S(1)}, u32[]{:S(2)}, u32[]{:S(2)}) collective-permute-start(bf16[256,512]{1,0:T(8,128)(2,1)S(1)} %get-tuple-element.207), channel_id=1, source_target_pairs={{0,8},{4,12},{8,0},{12,4},{16,24},{20,28},{24,16},{28,20},{1,9},{5... | collective-permute-start | bytes 786440 | tf_op jit(solution)/shard_map/ppermute | solution.py:681
  94.7 45.2 %collective-permute-start.22 = (bf16[640,512]{1,0:T(8,128)(2,1)S(1)}, bf16[640,512]{1,0:T(8,128)(2,1)S(1)}, u32[]{:S(2)}, u32[]{:S(2)}) collective-permute-start(bf16[640,512]{1,0:T(8,128)(2,1)S(1)} %constant_dynamic-update-slice_fusion.refs_0_), channel_id=1, source_target_pairs={{0,2},{1,3},{2,0},{3,1},{4,6},{5,7},{6,4},{7,5},{8,10},{9,11},{10,... | collective-permute-start | bytes 1966088 | tf_op jit(solution)/shard_map/ppermute | solution.py:677
  100.2 9.0 %collective-permute-start.32 = (bf16[128,512]{1,0:T(8,128)(2,1)S(1)}, bf16[128,512]{1,0:T(8,128)(2,1)S(1)}, u32[]{:S(2)}, u32[]{:S(2)}) collective-permute-start(bf16[128,512]{1,0:T(8,128)(2,1)S(1)} %get-tuple-element.216), channel_id=1, source_target_pairs={{0,8},{4,12},{8,0},{12,4},{16,24},{20,28},{24,16},{28,20},{1,9},{5... | collective-permute-start | bytes 393224 | tf_op jit(solution)/shard_map/ppermute | solution.py:681
  107.8 5.0 %collective-permute-start.30 = (bf16[128,512]{1,0:T(8,128)(2,1)S(1)}, bf16[128,512]{1,0:T(8,128)(2,1)S(1)}, u32[]{:S(2)}, u32[]{:S(2)}) collective-permute-start(bf16[128,512]{1,0:T(8,128)(2,1)S(1)} %get-tuple-element.214), channel_id=1, source_target_pairs={{0,4},{4,0},{8,12},{12,8},{16,20},{20,16},{24,28},{28,24},{1,5},{5... | collective-permute-start | bytes 393224 | tf_op jit(solution)/shard_map/ppermute | solution.py:681
  109.2 5.4 %collective-permute-start.17 = (bf16[160,512]{1,0:T(8,128)(2,1)S(1)}, bf16[160,512]{1,0:T(8,128)(2,1)S(1)}, u32[]{:S(2)}, u32[]{:S(2)}) collective-permute-start(bf16[160,512]{1,0:T(8,128)(2,1)S(1)} %pad_maximum_fusion.4), channel_id=1, source_target_pairs={{0,8},{4,12},{8,0},{12,4},{16,24},{20,28},{24,16},{28,20},{1,9},{5... | collective-permute-start | bytes 491528 | tf_op jit(solution)/shard_map/ppermute | solution.py:681
  114.6 10.0 %collective-permute-start.18 = (bf16[96,512]{1,0:T(8,128)(2,1)S(1)}, bf16[96,512]{1,0:T(8,128)(2,1)S(1)}, u32[]{:S(2)}, u32[]{:S(2)}) collective-permute-start(bf16[96,512]{1,0:T(8,128)(2,1)S(1)} %pad_maximum_fusion.7), channel_id=1, source_target_pairs={{0,16},{4,20},{8,24},{12,28},{16,0},{20,4},{24,8},{28,12},{1,17},{... | collective-permute-start | bytes 294920 | tf_op jit(solution)/shard_map/ppermute | solution.py:681
  117.5 8.8 %collective-permute-start.33 = (bf16[128,512]{1,0:T(8,128)(2,1)S(1)}, bf16[128,512]{1,0:T(8,128)(2,1)S(1)}, u32[]{:S(2)}, u32[]{:S(2)}) collective-permute-start(bf16[128,512]{1,0:T(8,128)(2,1)S(1)} %bitcast.22), channel_id=1, source_target_pairs={{0,16},{4,20},{8,24},{12,28},{16,0},{20,4},{24,8},{28,12},{1,17},{... | collective-permute-start | bytes 393224 | tf_op jit(solution)/shard_map/ppermute | solution.py:681
  124.7 17.4 %collective-permute-start.26 = (bf16[672,512]{1,0:T(8,128)(2,1)S(1)}, bf16[672,512]{1,0:T(8,128)(2,1)S(1)}, u32[]{:S(2)}, u32[]{:S(2)}) collective-permute-start(bf16[672,512]{1,0:T(8,128)(2,1)S(1)} %pad_maximum_fusion.refs_0_), channel_id=1, source_target_pairs={{0,2},{1,3},{2,0},{3,1},{4,6},{5,7},{6,4},{7,5},{8,10},{9,11},{10,... | collective-permute-start | bytes 2064392 | tf_op jit(solution)/shard_map/ppermute | solution.py:677
  126.3 11.0 %collective-permute-start.34 = (bf16[128,512]{1,0:T(8,128)(2,1)S(1)}, bf16[128,512]{1,0:T(8,128)(2,1)S(1)}, u32[]{:S(2)}, u32[]{:S(2)}) collective-permute-start(bf16[128,512]{1,0:T(8,128)(2,1)S(1)} %add_convert_fusion.11), channel_id=1, source_target_pairs={{0,16},{4,20},{8,24},{12,28},{16,0},{20,4},{24,8},{28,12},{1,17},{... | collective-permute-start | bytes 393224 | tf_op jit(solution)/shard_map/ppermute | solution.py:681
  126.4 10.7 %collective-permute-start.19 = (bf16[64,512]{1,0:T(8,128)(2,1)S(1)}, bf16[64,512]{1,0:T(8,128)(2,1)S(1)}, u32[]{:S(2)}, u32[]{:S(2)}) collective-permute-start(bf16[64,512]{1,0:T(8,128)(2,1)S(1)} %add_convert_fusion.15), channel_id=1, source_target_pairs={{0,16},{4,20},{8,24},{12,28},{16,0},{20,4},{24,8},{28,12},{1,17},{... | collective-permute-start | bytes 196616 | tf_op jit(solution)/shard_map/ppermute | solution.py:681
  137.1 5.0 %collective-permute-start.20 = (bf16[128,512]{1,0:T(8,128)(2,1)S(1)}, bf16[128,512]{1,0:T(8,128)(2,1)S(1)}, u32[]{:S(2)}, u32[]{:S(2)}) collective-permute-start(bf16[128,512]{1,0:T(8,128)(2,1)S(1)} %pad_maximum_fusion.6), channel_id=1, source_target_pairs={{0,8},{4,12},{8,0},{12,4},{16,24},{20,28},{24,16},{28,20},{1,9},{5... | collective-permute-start | bytes 393224 | tf_op jit(solution)/shard_map/ppermute | solution.py:681
  137.3 8.2 %collective-permute-start.35 = (bf16[256,512]{1,0:T(8,128)(2,1)S(1)}, bf16[256,512]{1,0:T(8,128)(2,1)S(1)}, u32[]{:S(2)}, u32[]{:S(2)}) collective-permute-start(bf16[256,512]{1,0:T(8,128)(2,1)S(1)} %constant_dynamic-update-slice_fusion.2), channel_id=1, source_target_pairs={{0,4},{4,0},{8,12},{12,8},{16,20},{20,16},{24,28},{28,24},{1,5},{5... | collective-permute-start | bytes 786440 | tf_op jit(solution)/shard_map/ppermute | solution.py:681
  140.0 11.4 %collective-permute-start.25 = (bf16[672,512]{1,0:T(8,128)(2,1)S(1)}, bf16[672,512]{1,0:T(8,128)(2,1)S(1)}, u32[]{:S(2)}, u32[]{:S(2)}) collective-permute-start(bf16[672,512]{1,0:T(8,128)(2,1)S(1)} %pad_maximum_fusion.refs_0_), channel_id=1, source_target_pairs={{0,1},{1,0},{2,3},{3,2},{4,5},{5,4},{6,7},{7,6},{8,9},{9,8},{10,11... | collective-permute-start | bytes 2064392 | tf_op jit(solution)/shard_map/ppermute | solution.py:677
  142.2 6.9 %collective-permute-start.23 = (bf16[640,512]{1,0:T(8,128)(2,1)S(1)}, bf16[640,512]{1,0:T(8,128)(2,1)S(1)}, u32[]{:S(2)}, u32[]{:S(2)}) collective-permute-start(bf16[640,512]{1,0:T(8,128)(2,1)S(1)} %collective-permute-done.22.refs_2_), channel_id=1, source_target_pairs={{0,1},{1,0},{2,3},{3,2},{4,5},{5,4},{6,7},{7,6},{8,9},{9,8},{10,11... | collective-permute-start | bytes 1966088 | tf_op jit(solution)/shard_map/ppermute | solution.py:677
  142.2 9.2 %collective-permute-start.27 = (bf16[672,512]{1,0:T(8,128)(2,1)S(1)}, bf16[672,512]{1,0:T(8,128)(2,1)S(1)}, u32[]{:S(2)}, u32[]{:S(2)}) collective-permute-start(bf16[672,512]{1,0:T(8,128)(2,1)S(1)} %collective-permute-done.26.refs_2_), channel_id=1, source_target_pairs={{0,1},{1,0},{2,3},{3,2},{4,5},{5,4},{6,7},{7,6},{8,9},{9,8},{10,11... | collective-permute-start | bytes 2064392 | tf_op jit(solution)/shard_map/ppermute | solution.py:677
  145.5 12.3 %collective-permute-start.36 = (bf16[512,512]{1,0:T(8,128)(2,1)S(1)}, bf16[512,512]{1,0:T(8,128)(2,1)S(1)}, u32[]{:S(2)}, u32[]{:S(2)}) collective-permute-start(bf16[512,512]{1,0:T(8,128)(2,1)S(1)} %constant_dynamic-update-slice_fusion.4.refs_0_), channel_id=1, source_target_pairs={{0,8},{4,12},{8,0},{12,4},{16,24},{20,28},{24,16},{28,20},{1,9},{5... | collective-permute-start | bytes 1572872 | tf_op jit(solution)/shard_map/ppermute | solution.py:681
  147.3 7.1 %collective-permute-start.28 = (bf16[256,512]{1,0:T(8,128)(2,1)S(1)}, bf16[256,512]{1,0:T(8,128)(2,1)S(1)}, u32[]{:S(2)}, u32[]{:S(2)}) collective-permute-start(bf16[256,512]{1,0:T(8,128)(2,1)S(1)} %pad_maximum_fusion.3.refs_0_), channel_id=1, source_target_pairs={{0,4},{4,0},{8,12},{12,8},{16,20},{20,16},{24,28},{28,24},{1,5},{5... | collective-permute-start | bytes 786440 | tf_op jit(solution)/shard_map/ppermute | solution.py:681

commit v3 on v2

--- a/solution.py
+++ b/solution.py
@@ -143,7 +143,11 @@
     return lax.optimization_barrier((x, *others))[0]
 
 
-def call(kernel, args, outs, scratch=(), scalars=(), hbm=0, hbm_out=0, name=None):
+def pinned(x):
+    return pltpu.with_memory_space_constraint(x, pltpu.HBM)
+
+
+def call(kernel, args, outs, scratch=(), scalars=(), hbm=0, hbm_out=0, pin=True, name=None):
     in_hbm = pl.BlockSpec(memory_space=pltpu.HBM)
     return pl.pallas_call(
         kernel,
@@ -155,7 +159,7 @@
         compiler_params=pltpu.CompilerParams(vmem_limit_bytes=VMEM_OF.get(name, VMEM_LIMIT) * 2**20),
         cost_estimate=cost(name),
         name=name,
-    )(*scalars, *[pltpu.with_memory_space_constraint(a, pltpu.HBM) for a in args[:hbm]], *args[hbm:])
+    )(*scalars, *[pinned(a) if pin else a for a in args[:hbm]], *args[hbm:])
 
 
 def first_column(width):
@@ -422,9 +426,9 @@
     refs = list(refs)
     packs = refs[:ns]
     if first:
-        held, sems = refs[-1 - ns : -1], refs[-1]
-        copies = loads(packs, held, sems)
-        packs, refs = held, refs[: -1 - ns]
+        held, sems = refs[-2:]
+        copies = loads(packs[:1], [held], sems)
+        packs, refs = [held] + packs[1:], refs[:-2]
     z2 = refs[ns]
     refs = refs[ns + 1 :]
     if first:
@@ -453,7 +457,7 @@
                 + dot(onehot(places[r0 : r0 + n, :], STRIP), grecv[...])
             ).astype(BF)
     for k in range(ns):
-        if first:
+        if first and k == 0:
             copies[k].wait()
         ub = packs[k][2 * D : 2 * D + 1, :].astype(F32)
         dub_total = jnp.zeros((1, D), F32)
@@ -514,7 +518,7 @@
     return copies
 
 
-def attn_bwd_kernel(ns, nwl, blocks, *refs):
+def attn_bwd_kernel(ns, nwl, blocks, last, *refs):
     refs = list(refs)
 
     def take(n):
@@ -522,11 +526,17 @@
         del refs[:n]
         return found
 
-    n_in = 4 * ns
+    n_in = 4 * ns + (TP - ns if last else 0)
     sources = take(n_in)
     dhb, z1 = take(2)
+    if last:
+        tail = take(11)
     grads = take(ns)
+    if last:
+        tail += take(3)
     dpos, *dx_sc = take(1 + ns)
+    if last:
+        tail += take(2)
     dsum, do_sc = take(2)
     held = take(n_in)
     (sems,) = refs
@@ -608,19 +618,17 @@
             line = k * per + 12 + i
             dpos[line : line + 1, :] = jnp.sum(part, axis=0, keepdims=True)
         dpos[k * per + 14 : (k + 1) * per, :] = jnp.zeros((2, LANES), F32)
-
-
-def final_kernel(nwl, *refs):
-    refs = list(refs)
-    packs, dxs, refs = refs[:TP], refs[TP : 2 * TP], refs[2 * TP :]
-    x_ref, dh, vecs, vec_mlp, small3, small2, small01, dub01, dub2, dub3 = refs[:10]
-    out_up, out_low, small_out, small_f32, dz = refs[10:15]
-    held, sems = refs[15:-1], refs[-1]
-    copies = loads(packs, held, sems)
+    if last:
+        for copy in copies[4 * ns :]:
+            copy.wait()
+        end_of_backward(nwl, dx_sc, packs + held[4 * ns :], dpos, *tail)
+
+
+def end_of_backward(nwl, dxs, packs, small01, *refs):
+    dx2, dx3, x_ref, dh, vecs, vec_mlp, small3, small2, dub01, dub2, dub3 = refs[:11]
+    out_up, out_low, small_out, small_f32, dz = refs[11:]
     rows = x_ref.shape[0]
-    for copy in copies:
-        copy.wait()
-    parts = list(zip(dxs, held))
+    parts = list(zip(dxs + [dx2, dx3], packs))
     weights = [
         jnp.concatenate([pack[m * D : (m + 1) * D, :] for m in range(3)], axis=1) for _, pack in parts
     ]
@@ -878,6 +886,7 @@
         scalars=[page_bounds],
         hbm=TP,
         hbm_out=3 * TP + 2,
+        pin=False,
         name="attn_fwd",
     )
     qkv, probs, o = outs[:TP], outs[TP : 2 * TP], outs[2 * TP : 3 * TP]
@@ -897,8 +906,8 @@
             outs if last else outs + accs,
             scratch=([pltpu.VMEM(*a) for a in accs] if last else [])
             + [pltpu.VMEM((rows, D), BF)] * 2
-            + ([pltpu.VMEM((PACK2, D), BF)] * ns + [pltpu.SemaphoreType.DMA((ns,))] if first else []),
-            hbm=ns if first else 0,
+            + ([pltpu.VMEM((PACK2, D), BF), pltpu.SemaphoreType.DMA((1,))] if first else []),
+            hbm=1 if first else 0,
             name="mlp_last" if last else "mlp_first" if first else "mlp_mid",
         )
 
@@ -915,14 +924,25 @@
     got_g3 = swap_tp(g3, 1)
     lower_y = shift_rows(low_y, 1)
 
-    def attn_bwd(shards, dhb):
+    def attn_bwd(shards, dhb, tail=()):
         ns = len(shards)
         loaded = [a[s] for a in (packs1, o, qkv, probs) for s in shards]
+        outs = [((D, D), BF)] * ns
+        parts = [((ns * 16, LANES), F32)] + [((rows, 3 * LANES), BF)] * ns
+        scratch = []
+        if tail:
+            loaded += [packs1[s] for s in range(TP) if s not in shards]
+            outs += [((STRIP, D), BF)] * 2 + [((SMALL_ROWS, D), BF)]
+            scratch = [pltpu.VMEM(*p) for p in parts]
+            scratch += [pltpu.VMEM((SMALL_ROWS, D), F32), pltpu.VMEM((rows, D), BF)]
+        else:
+            outs += parts
         return call(
-            functools.partial(attn_bwd_kernel, ns, nwl, blocks),
-            loaded + [dhb, z1],
-            [((D, D), BF)] * ns + [((ns * 16, LANES), F32)] + [((rows, 3 * LANES), BF)] * ns,
-            scratch=[pltpu.VMEM((ns, STACK, LANES), F32), pltpu.VMEM((ns, rows, LANES), BF)]
+            functools.partial(attn_bwd_kernel, ns, nwl, blocks, bool(tail)),
+            loaded + [dhb, z1, *tail],
+            outs,
+            scratch=scratch
+            + [pltpu.VMEM((ns, STACK, LANES), F32), pltpu.VMEM((ns, rows, LANES), BF)]
             + [pltpu.VMEM(a.shape, a.dtype) for a in loaded]
             + [pltpu.SemaphoreType.DMA((len(loaded),))],
             hbm=len(loaded),
@@ -940,31 +960,23 @@
     a2, small2, dx2 = attn_bwd((2,), after(dhb, across_d, up0, up2))
     across_a = added([a2, got_a3])
     got_ax = swap_tp(across_a, 2)
-    a0, a1, small01, dx0, dx1 = attn_bwd((0, 1), after(dhb, across_a))
+    a0, a1, up_g, low_g, small = attn_bwd(
+        (0, 1),
+        after(dhb, across_a),
+        (dx2, dx3, x_win, dh, vecs, vec_mlp, small3, small2, dub01, dub2, dub3),
+    )
+    lower_g = shift_rows(low_g, 1)
     got_a1 = swap_tp(a1, 1)
     page_own = jnp.concatenate([after(up_y, a2), lower_y], axis=0)
     from_c = swap_tp(page_own, 1)
 
-    down = scatter_step([after(g0, a0)[:D], after(got_g1, a0)[:D], got_dx], bits[1], blocks)
-    up_got = after(up_got, down[0])
+    up_got = after(up_got, a0)
     up0 = added([up0[:half], up_got[:half]])
     up2 = added([up2[:half], up_got[half:]])
     up_x = swap_tp(up2, 2)
-    up_g, low_g, small = call(
-        functools.partial(final_kernel, nwl),
-        packs1
-        + [after(dx0, down[0], up2), dx1, dx2, dx3, x_win, dh, vecs, vec_mlp]
-        + [small3, small2, small01, dub01, dub2, dub3],
-        [((STRIP, D), BF)] * 2 + [((SMALL_ROWS, D), BF)],
-        scratch=[pltpu.VMEM((SMALL_ROWS, D), F32), pltpu.VMEM((rows, D), BF)]
-        + [pltpu.VMEM((PACK1, LANES), BF)] * TP
-        + [pltpu.SemaphoreType.DMA((TP,))],
-        hbm=TP,
-        name="final",
-    )
-    lower_g = shift_rows(low_g, 1)
-
-    attn = [after(a0, low_g), got_a1, got_ax]
+    down = scatter_step([after(g0, up2)[:D], after(got_g1, up2)[:D], got_dx], bits[1], blocks)
+
+    attn = [after(a0, up2, down[0]), got_a1, got_ax]
     small = [small]
     mlp = None
     gather_a = [b for b in reversed(bits) if b < blocks]

time: 160 us -> 156 us (0.975)
  waiting for transfers between devices: 41.2 us -> 38.5 us
    ppermute x14, waiting for transfers between devices: 39.2 us -> 33 us  [swap_rows(): lax.ppermute(x, 'rows', [(i, i ^ bit) for i in range(lax.axis_size('rows'...]
    ppermute x19, waiting for transfers between devices: 1.94 us -> 5.49 us  [swap_tp(): return lax.ppermute(x, 'tp', [(i, i ^ bit) for i in range(TP)])]
    ppermute x4, starting transfers between devices: 9.49 us -> 11.2 us  [shift_rows(): return lax.ppermute(x, 'rows', [(i, (i + distance) % n) for i in range(n)])]
    pallas_call x15 -> x14, Pallas kernels: 69 us -> 67.4 us  [call(): pl.pallas_call(kernel, out_shape=[jax.ShapeDtypeStruct(s, d) for s, d in...]
where the time goes in v3:
time: 156 us
  Pallas kernels  67.4 us (43%)
  starting transfers between devices  43.1 us (28%)
  waiting for transfers between devices  38.5 us (25%)
  local copies, waits for them, and re-layouts  2.87 us (2%)
  other arithmetic  2.29 us (1%)
    pallas_call x14, Pallas kernels, call(): pl.pallas_call(kernel, out_shape=[jax.ShapeDtypeStruct(s, d) for s, d in...  67.4 us
    ppermute x14, waiting for transfers between devices, swap_rows(): lax.ppermute(x, 'rows', [(i, i ^ bit) for i in range(lax.axis_size('rows'...  33 us
    ppermute x14, starting transfers between devices, swap_rows(): lax.ppermute(x, 'rows', [(i, i ^ bit) for i in range(lax.axis_size('rows'...  20.2 us
    ppermute x19, starting transfers between devices, swap_tp(): return lax.ppermute(x, 'tp', [(i, i ^ bit) for i in range(TP)])  11.8 us
    ppermute x4, starting transfers between devices, shift_rows(): return lax.ppermute(x, 'rows', [(i, (i + distance) % n) for i in range(n)])  11.2 us
    ppermute x19, waiting for transfers between devices, swap_tp(): return lax.ppermute(x, 'tp', [(i, i ^ bit) for i in range(TP)])  5.49 us
  transfers between devices with their start and end apart: 37, of which 12 were waited for; matrix products, arithmetic and copies ran while one was open for 2% of the time, Pallas kernels for 38%

profile of v3, /device:TPU:0, one launch (start us, length us, event | category | flops | bytes accessed | tf_op | source)
XLA Modules:
  0.0 155.5 jit_solution(14751680835456536365)
XLA Ops:
  0.7 3.0 %head.1 = (bf16[320,512]{1,0:T(8,128)(2,1)}, bf16[2080,128]{1,0:T(8,128)(2,1)}) custom-call(bf16[10,240,512]{2,1,0:T(8,128)(2,1)} %x.3, bf16[1536,128]{1,0:T(8,128)(2,1)} %bitcast.21, bf16[128,512]{1,0:T(8,128)(2,1)} %wproj.1, bf16[4,361]{1,0:T(4,128)(2,1)} %bitcast.23, bf16[2,128]{1,0:T(2,128)(2,1)} %bias.1), custom_call_target="tpu_custom_call" | custom-call | flops 600000000 | bytes 1024 | tf_op jit(solution)/shard_map/head/pallas_call | solution.py:152
  3.8 3.0 %collective-permute-start = (bf16[2080,128]{1,0:T(8,128)(2,1)}, bf16[2080,128]{1,0:T(8,128)(2,1)S(1)}, u32[]{:S(2)}, u32[]{:S(2)}) collective-permute-start(bf16[2080,128]{1,0:T(8,128)(2,1)} %get-tuple-element.109.refs_0_), channel_id=1, source_target_pairs={{0,2},{1,3},{2,0},{3,1},{4,6},{5,7},{6,4},{7,5},{8,10},{9,11},{10,... | collective-permute-start | bytes 1597448 | tf_op jit(solution)/shard_map/ppermute | solution.py:685
  6.8 4.6 %collective-permute-start.4 = (bf16[320,512]{1,0:T(8,128)(2,1)}, bf16[320,512]{1,0:T(8,128)(2,1)S(1)}, u32[]{:S(2)}, u32[]{:S(2)}) collective-permute-start(bf16[320,512]{1,0:T(8,128)(2,1)} %get-tuple-element.106), channel_id=1, source_target_pairs={{0,28},{4,0},{8,4},{12,8},{16,12},{20,16},{24,20},{28,24},{1,29},{... | collective-permute-start | bytes 983048 | tf_op jit(solution)/shard_map/ppermute | solution.py:694
  11.5 0.6 convert_element_type.190.refs_6_.refs_16_
  12.1 0.6 broadcast_in_dim.3.ubias
  12.7 4.7 %rest.1 = (bf16[320,512]{1,0:T(8,128)(2,1)}, bf16[704,512]{1,0:T(8,128)(2,1)}, bf16[704,512]{1,0:T(8,128)(2,1)}, bf16[1040,512]{1,0:T(8,128)(2,1)}) custom-call(bf16[10,240,512]{2,1,0:T(8,128)(2,1)} %x.3, bf16[10,240,512]{2,1,0:T(8,128)(2,1)} %g, bf16[512,512]{1,0:T(8,128)(2,1)} %up.1, bf16[512,512]{1,0:T(8,128)(2,1)} %down.1, ...), custom_call_target="tpu_custom_call" | custom-call | flops 1000000000 | bytes 1024 | tf_op jit(solution)/shard_map/rest/pallas_call | solution.py:152
  17.4 0.3 collective-permute-start.2
  17.7 1.4 collective-permute-done.refs_2_.refs_0_.refs_8_
  19.1 1.7 %collective-permute-start.1 = (bf16[1040,512]{1,0:T(8,128)(2,1)}, bf16[1040,512]{1,0:T(8,128)(2,1)S(1)}, u32[]{:S(2)}, u32[]{:S(2)}) collective-permute-start(bf16[1040,512]{1,0:T(8,128)(2,1)} %get-tuple-element.110.refs_0_), channel_id=1, source_target_pairs={{0,2},{1,3},{2,0},{3,1},{4,6},{5,7},{6,4},{7,5},{8,10},{9,11},{10,... | collective-permute-start | bytes 3194888 | tf_op jit(solution)/shard_map/ppermute | solution.py:685
  20.9 4.6 %collective-permute-start.6 = (bf16[320,512]{1,0:T(8,128)(2,1)}, bf16[320,512]{1,0:T(8,128)(2,1)S(1)}, u32[]{:S(2)}, u32[]{:S(2)}) collective-permute-start(bf16[320,512]{1,0:T(8,128)(2,1)} %get-tuple-element.111), channel_id=1, source_target_pairs={{0,28},{4,0},{8,4},{12,8},{16,12},{20,16},{24,20},{28,24},{1,29},{... | collective-permute-start | bytes 983048 | tf_op jit(solution)/shard_map/ppermute | solution.py:694
  25.5 0.8 copy-done.9
  26.4 12.7 %attn_fwd.1 = (bf16[3,704,128]{2,1,0:T(8,128)(2,1)}, bf16[3,704,128]{2,1,0:T(8,128)(2,1)}, bf16[3,704,128]{2,1,0:T(8,128)(2,1)}, bf16[3,704,128]{2,1,0:T(8,128)(...) custom-call(s32[1,2]{1,0:T(1,128)} %bounds.1, ...), custom_call_target="tpu_custom_call" | custom-call | flops 2800000000 | bytes 1024 | tf_op jit(solution)/shard_map/attn_fwd/pallas_call | solution.py:152
  39.1 1.1 copy-done
  40.2 6.9 %mlp_first.1 = (bf16[1024,512]{1,0:T(8,128)(2,1)S(1)}, bf16[1024,512]{1,0:T(8,128)(2,1)S(1)}, f32[8,128]{1,0:T(8,128)S(1)}, bf16[704,512]{1,0:T(8,128)(2,1)S(1)}...) custom-call(bf16[1040,512]{1,0:T(8,128)(2,1)} %get-tuple-element.110.refs_0_, ...), custom_call_target="tpu_custom_call" | custom-call | flops 1800000000 | bytes 1024 | tf_op jit(solution)/shard_map/mlp_first/pallas_call | solution.py:152
  47.1 0.2 collective-permute-start.7
  47.3 2.8 %mlp_mid.1 = (bf16[1024,512]{1,0:T(8,128)(2,1)S(1)}, f32[4,128]{1,0:T(4,128)S(1)}, f32[704,512]{1,0:T(8,128)S(1)}, f32[704,512]{1,0:T(8,128)S(1)}) custom-call(bf16[1040,512]{1,0:T(8,128)(2,1)S(1)} %collective-permute-done.1.refs_0_, bf16[704,512]{1,0:T(8,128)(2,1)S(1)} %copy-done.1, bf16[704,512]{1,0:T(8,128)(2,1)S(1)} %get-tuple-element.118.refs_2_, ...), custom_call_target="tpu_custom_call" | custom-call | flops 1000000000 | bytes 1024 | tf_op jit(solution)/shard_map/mlp_mid/pallas_call | solution.py:152
  50.1 4.2 %mlp_last.1 = (bf16[1024,512]{1,0:T(8,128)(2,1)S(1)}, f32[4,128]{1,0:T(4,128)S(1)}, bf16[320,512]{1,0:T(8,128)(2,1)S(1)}, bf16[320,512]{1,0:T(8,128)(2,1)S(1)}, ...) custom-call(bf16[1040,512]{1,0:T(8,128)(2,1)S(1)} %collective-permute-done.7.refs_0_, ...), custom_call_target="tpu_custom_call" | custom-call | flops 1000000000 | bytes 1024 | tf_op jit(solution)/shard_map/mlp_last/pallas_call | solution.py:152
  54.3 0.4 collective-permute-start.8
  54.8 0.2 collective-permute-start.9
  54.9 6.1 %attn_bwd_3.1 = (bf16[512,512]{1,0:T(8,128)(2,1)S(1)}, f32[16,128]{1,0:T(8,128)S(1)}, bf16[704,384]{1,0:T(8,128)(2,1)S(1)}) custom-call(bf16[2080,128]{1,0:T(8,128)(2,1)} %copy-done.9, bf16[704,128]{1,0:T(8,128)(2,1)} %get-tuple-element.130.refs_1_, bf16[3,704,128]{2,1,0:T(8,128)(2,1)} %get-tuple-element.131.refs_2_, ...), custom_call_target="tpu_custom_call" | custom-call | flops 1400000000 | bytes 1024 | tf_op jit(solution)/shard_map/attn_bwd_3/pallas_call | solution.py:152
  61.0 0.4 collective-permute-start.11
  61.4 0.3 add_convert_fusion.3
  61.7 0.1 add_convert_fusion.4
  61.9 0.6 collective-permute-start.13
  62.6 0.8 collective-permute-start.12
  63.4 5.9 %attn_bwd_2.1 = (bf16[512,512]{1,0:T(8,128)(2,1)S(1)}, f32[16,128]{1,0:T(8,128)S(1)}, bf16[704,384]{1,0:T(8,128)(2,1)S(1)}) custom-call(bf16[2080,128]{1,0:T(8,128)(2,1)} %copy-done.7, bf16[704,128]{1,0:T(8,128)(2,1)} %get-tuple-element.124.refs_1_, bf16[3,704,128]{2,1,0:T(8,128)(2,1)} %get-tuple-element.125.refs_2_, ...), custom_call_target="tpu_custom_call" | custom-call | flops 1400000000 | bytes 1024 | tf_op jit(solution)/shard_map/attn_bwd_2/pallas_call | solution.py:152
  69.2 0.1 add_convert_fusion.2
  69.4 1.2 collective-permute-start.15
  70.6 13.2 %attn_bwd_01.1 = (bf16[512,512]{1,0:T(8,128)(2,1)S(1)}, bf16[512,512]{1,0:T(8,128)(2,1)S(1)}, bf16[320,512]{1,0:T(8,128)(2,1)S(1)}, bf16[320,512]{1,0:T(8,128)(2,1)S(1)}, bf16[32,512]{1,0:T(8,128)(2,1)S(1)}) custom-call(bf16[2080,128]{1,0:T(8,128)(2,1)} %get-tuple-element.109.refs_0_, bf16[2080,128]{1,0:T(8,128)(2,1)} %copy-done.8, ...), custom_call_target="tpu_custom_call" | custom-call | flops 2200000000 | bytes 1024 | tf_op jit(solution)/shard_map/attn_bwd_01/pallas_call | solution.py:152
  83.9 2.0 %collective-permute-start.24 = (bf16[320,512]{1,0:T(8,128)(2,1)S(1)}, bf16[320,512]{1,0:T(8,128)(2,1)S(1)}, u32[]{:S(2)}, u32[]{:S(2)}) collective-permute-start(bf16[320,512]{1,0:T(8,128)(2,1)S(1)} %get-tuple-element.171), channel_id=1, source_target_pairs={{0,4},{4,8},{8,12},{12,16},{16,20},{20,24},{24,28},{28,0},{1,5},{5... | collective-permute-start | bytes 983048 | tf_op jit(solution)/shard_map/ppermute | solution.py:694
  85.9 0.3 collective-permute-start.21
  86.2 0.1 add_convert_fusion.7
  86.4 0.9 collective-permute-start.31
  87.3 0.2 add_convert_fusion.1
  87.6 0.2 add_convert_fusion
  87.8 1.5 collective-permute-start.16
  89.3 1.6 %collective-permute-start.29 = (bf16[256,512]{1,0:T(8,128)(2,1)S(1)}, bf16[256,512]{1,0:T(8,128)(2,1)S(1)}, u32[]{:S(2)}, u32[]{:S(2)}) collective-permute-start(bf16[256,512]{1,0:T(8,128)(2,1)S(1)} %get-tuple-element.199), channel_id=1, source_target_pairs={{0,8},{4,12},{8,0},{12,4},{16,24},{20,28},{24,16},{28,20},{1,9},{5... | collective-permute-start | bytes 786440 | tf_op jit(solution)/shard_map/ppermute | solution.py:689
  90.9 4.1 %collective-permute-done.31 = bf16[256,512]{1,0:T(8,128)(2,1)S(1)} collective-permute-done((bf16[256,512]{1,0:T(8,128)(2,1)S(1)}, bf16[256,512]{1,0:T(8,128)(2,1)S(1)}, u32[]{:S(2)}, u32[]{:S(2)}) %collective-permute-start.31) | collective-permute-done | bytes 262176 | tf_op jit(solution)/shard_map/ppermute | solution.py:685
  94.9 0.9 collective-permute-start.22
  95.9 1.3 collective-permute-done.29
  97.3 1.6 %collective-permute-start.32 = (bf16[128,512]{1,0:T(8,128)(2,1)S(1)}, bf16[128,512]{1,0:T(8,128)(2,1)S(1)}, u32[]{:S(2)}, u32[]{:S(2)}) collective-permute-start(bf16[128,512]{1,0:T(8,128)(2,1)S(1)} %get-tuple-element.208), channel_id=1, source_target_pairs={{0,8},{4,12},{8,0},{12,4},{16,24},{20,28},{24,16},{28,20},{1,9},{5... | collective-permute-start | bytes 393224 | tf_op jit(solution)/shard_map/ppermute | solution.py:689
  98.9 4.4 %collective-permute-done.16 = bf16[288,512]{1,0:T(8,128)(2,1)S(1)} collective-permute-done((bf16[288,512]{1,0:T(8,128)(2,1)S(1)}, bf16[288,512]{1,0:T(8,128)(2,1)S(1)}, u32[]{:S(2)}, u32[]{:S(2)}) %collective-permute-start.16) | collective-permute-done | bytes 294944 | tf_op jit(solution)/shard_map/ppermute | solution.py:689
  103.5 2.1 %collective-permute-start.17 = (bf16[160,512]{1,0:T(8,128)(2,1)S(1)}, bf16[160,512]{1,0:T(8,128)(2,1)S(1)}, u32[]{:S(2)}, u32[]{:S(2)}) collective-permute-start(bf16[160,512]{1,0:T(8,128)(2,1)S(1)} %pad_maximum_fusion.4), channel_id=1, source_target_pairs={{0,8},{4,12},{8,0},{12,4},{16,24},{20,28},{24,16},{28,20},{1,9},{5... | collective-permute-start | bytes 491528 | tf_op jit(solution)/shard_map/ppermute | solution.py:689
  105.6 3.1 %collective-permute-done.30 = bf16[128,512]{1,0:T(8,128)(2,1)S(1)} collective-permute-done((bf16[128,512]{1,0:T(8,128)(2,1)S(1)}, bf16[128,512]{1,0:T(8,128)(2,1)S(1)}, u32[]{:S(2)}, u32[]{:S(2)}) %collective-permute-start.30) | collective-permute-done | bytes 131104 | tf_op jit(solution)/shard_map/ppermute | solution.py:689
  108.8 0.9 collective-permute-done.17
  109.7 3.0 %collective-permute-start.18 = (bf16[96,512]{1,0:T(8,128)(2,1)S(1)}, bf16[96,512]{1,0:T(8,128)(2,1)S(1)}, u32[]{:S(2)}, u32[]{:S(2)}) collective-permute-start(bf16[96,512]{1,0:T(8,128)(2,1)S(1)} %pad_maximum_fusion.7), channel_id=1, source_target_pairs={{0,16},{4,20},{8,24},{12,28},{16,0},{20,4},{24,8},{28,12},{1,17},{... | collective-permute-start | bytes 294920 | tf_op jit(solution)/shard_map/ppermute | solution.py:689
  112.8 0.1 collective-permute-start.33
  112.9 7.5 %collective-permute-done.18 = bf16[96,512]{1,0:T(8,128)(2,1)S(1)} collective-permute-done((bf16[96,512]{1,0:T(8,128)(2,1)S(1)}, bf16[96,512]{1,0:T(8,128)(2,1)S(1)}, u32[]{:S(2)}, u32[]{:S(2)}) %collective-permute-start.18) | collective-permute-done | bytes 98336 | tf_op jit(solution)/shard_map/ppermute | solution.py:689
  120.5 0.9 collective-permute-start.26
  121.4 0.8 collective-permute-done.33
  122.4 2.9 %collective-permute-start.19 = (bf16[64,512]{1,0:T(8,128)(2,1)S(1)}, bf16[64,512]{1,0:T(8,128)(2,1)S(1)}, u32[]{:S(2)}, u32[]{:S(2)}) collective-permute-start(bf16[64,512]{1,0:T(8,128)(2,1)S(1)} %add_convert_fusion.15), channel_id=1, source_target_pairs={{0,16},{4,20},{8,24},{12,28},{16,0},{20,4},{24,8},{28,12},{1,17},{... | collective-permute-start | bytes 196616 | tf_op jit(solution)/shard_map/ppermute | solution.py:689
  125.3 8.2 %collective-permute-done.19 = bf16[64,512]{1,0:T(8,128)(2,1)S(1)} collective-permute-done((bf16[64,512]{1,0:T(8,128)(2,1)S(1)}, bf16[64,512]{1,0:T(8,128)(2,1)S(1)}, u32[]{:S(2)}, u32[]{:S(2)}) %collective-permute-start.19) | collective-permute-done | bytes 65568 | tf_op jit(solution)/shard_map/ppermute | solution.py:689
  133.6 3.0 %collective-permute-start.35 = (bf16[256,512]{1,0:T(8,128)(2,1)S(1)}, bf16[256,512]{1,0:T(8,128)(2,1)S(1)}, u32[]{:S(2)}, u32[]{:S(2)}) collective-permute-start(bf16[256,512]{1,0:T(8,128)(2,1)S(1)} %constant_dynamic-update-slice_fusion.2), channel_id=1, source_target_pairs={{0,4},{4,0},{8,12},{12,8},{16,20},{20,16},{24,28},{28,24},{1,5},{5... | collective-permute-start | bytes 786440 | tf_op jit(solution)/shard_map/ppermute | solution.py:689
  136.6 2.0 %collective-permute-done.20 = bf16[128,512]{1,0:T(8,128)(2,1)S(1)} collective-permute-done((bf16[128,512]{1,0:T(8,128)(2,1)S(1)}, bf16[128,512]{1,0:T(8,128)(2,1)S(1)}, u32[]{:S(2)}, u32[]{:S(2)}) %collective-permute-start.20) | collective-permute-done | bytes 131104 | tf_op jit(solution)/shard_map/ppermute | solution.py:689
  138.6 0.6 collective-permute-start.27
  139.2 2.7 %collective-permute-done.35 = bf16[256,512]{1,0:T(8,128)(2,1)S(1)} collective-permute-done((bf16[256,512]{1,0:T(8,128)(2,1)S(1)}, bf16[256,512]{1,0:T(8,128)(2,1)S(1)}, u32[]{:S(2)}, u32[]{:S(2)}) %collective-permute-start.35) | collective-permute-done | bytes 262176 | tf_op jit(solution)/shard_map/ppermute | solution.py:689
  141.9 1.8 %collective-permute-start.36 = (bf16[512,512]{1,0:T(8,128)(2,1)S(1)}, bf16[512,512]{1,0:T(8,128)(2,1)S(1)}, u32[]{:S(2)}, u32[]{:S(2)}) collective-permute-start(bf16[512,512]{1,0:T(8,128)(2,1)S(1)} %constant_dynamic-update-slice_fusion.4.refs_0_), channel_id=1, source_target_pairs={{0,8},{4,12},{8,0},{12,4},{16,24},{20,28},{24,16},{28,20},{1,9},{5... | collective-permute-start | bytes 1572872 | tf_op jit(solution)/shard_map/ppermute | solution.py:689
  143.7 1.7 %collective-permute-start.28 = (bf16[256,512]{1,0:T(8,128)(2,1)S(1)}, bf16[256,512]{1,0:T(8,128)(2,1)S(1)}, u32[]{:S(2)}, u32[]{:S(2)}) collective-permute-start(bf16[256,512]{1,0:T(8,128)(2,1)S(1)} %pad_maximum_fusion.3.refs_0_), channel_id=1, source_target_pairs={{0,4},{4,0},{8,12},{12,8},{16,20},{20,16},{24,28},{28,24},{1,5},{5... | collective-permute-start | bytes 786440 | tf_op jit(solution)/shard_map/ppermute | solution.py:689
  145.5 2.3 %page_y.1 = bf16[10,240,512]{2,1,0:T(8,128)(2,1)} custom-call(bf16[640,512]{1,0:T(8,128)(2,1)S(1)} %constant_dynamic-update-slice_fusion.refs_0_, bf16[640,512]{1,0:T(8,128)(2,1)S(1)} %collective-permute-done.21.refs_1_, bf16[640,512]{1,0:T(8,128)(2,1)S(1)} %collective-permute-done.22.refs_2_, bf16[640,512]{1,0:T(8,128)(2,1)S(1)} %collective-permute-done.23.refs_3_), custom_call_target="tpu_custom_call" | custom-call | flops 2000000 | bytes 1024 | tf_op jit(solution)/shard_map/page_y/pallas_call | solution.py:152
  147.8 0.6 small.1
  148.4 2.3 %page_g.1 = bf16[10,240,512]{2,1,0:T(8,128)(2,1)} custom-call(bf16[672,512]{1,0:T(8,128)(2,1)S(1)} %pad_maximum_fusion.refs_0_, bf16[672,512]{1,0:T(8,128)(2,1)S(1)} %collective-permute-done.25.refs_1_, bf16[672,512]{1,0:T(8,128)(2,1)S(1)} %collective-permute-done.26.refs_2_, bf16[672,512]{1,0:T(8,128)(2,1)S(1)} %collective-permute-done.27.refs_3_), custom_call_target="tpu_custom_call" | custom-call | flops 2000000 | bytes 1024 | tf_op jit(solution)/shard_map/page_g/pallas_call | solution.py:152
  150.8 1.1 finish_attn.1
  151.9 2.1 %collective-permute-done.36.refs_1_ = bf16[512,512]{1,0:T(8,128)(2,1)S(1)} collective-permute-done((bf16[512,512]{1,0:T(8,128)(2,1)S(1)}, bf16[512,512]{1,0:T(8,128)(2,1)S(1)}, u32[]{:S(2)}, u32[]{:S(2)}) %collective-permute-start.36) | collective-permute-done | bytes 524320 | tf_op jit(solution)/shard_map/ppermute | solution.py:689
  154.0 1.5 finish_mlp.1
  (108 shorter events, 1.3 us)
Async XLA Ops:
  0.7 10.7 %copy-start.10 = (bf16[512]{0:T(512)(128)(2,1)S(1)}, bf16[512]{0:T(512)(128)(2,1)}, u32[]{:S(2)}) copy-start(bf16[512]{0:T(512)(128)(2,1)} %param.19) | copy-start | bytes 3076
  0.7 10.7 %copy-start.11 = (bf16[512]{0:T(512)(128)(2,1)S(1)}, bf16[512]{0:T(512)(128)(2,1)}, u32[]{:S(2)}) copy-start(bf16[512]{0:T(512)(128)(2,1)} %param.20) | copy-start | bytes 3076
  0.7 10.7 %copy-start.12 = (bf16[512]{0:T(512)(128)(2,1)S(1)}, bf16[512]{0:T(512)(128)(2,1)}, u32[]{:S(2)}) copy-start(bf16[512]{0:T(512)(128)(2,1)} %param.26) | copy-start | bytes 3076
  0.7 10.7 %copy-start.13 = (bf16[512]{0:T(512)(128)(2,1)S(1)}, bf16[512]{0:T(512)(128)(2,1)}, u32[]{:S(2)}) copy-start(bf16[512]{0:T(512)(128)(2,1)} %param.27) | copy-start | bytes 3076
  0.7 10.7 %copy-start.14 = (bf16[512]{0:T(512)(128)(2,1)S(1)}, bf16[512]{0:T(512)(128)(2,1)}, u32[]{:S(2)}) copy-start(bf16[512]{0:T(512)(128)(2,1)} %param.25) | copy-start | bytes 3076
  0.7 10.7 %copy-start.15 = (bf16[512]{0:T(512)(128)(2,1)S(1)}, bf16[512]{0:T(512)(128)(2,1)}, u32[]{:S(2)}) copy-start(bf16[512]{0:T(512)(128)(2,1)} %param.31) | copy-start | bytes 3076
  0.7 11.4 %copy-start.16 = (bf16[512]{0:T(512)(128)(2,1)S(1)}, bf16[512]{0:T(512)(128)(2,1)}, u32[]{:S(2)}) copy-start(bf16[512]{0:T(512)(128)(2,1)} %param.29) | copy-start | bytes 3076
  3.8 15.3 %collective-permute-start = (bf16[2080,128]{1,0:T(8,128)(2,1)}, bf16[2080,128]{1,0:T(8,128)(2,1)S(1)}, u32[]{:S(2)}, u32[]{:S(2)}) collective-permute-start(bf16[2080,128]{1,0:T(8,128)(2,1)} %get-tuple-element.109.refs_0_), channel_id=1, source_target_pairs={{0,2},{1,3},{2,0},{3,1},{4,6},{5,7},{6,4},{7,5},{8,10},{9,11},{10,... | collective-permute-start | bytes 1597448 | tf_op jit(solution)/shard_map/ppermute | solution.py:685
  6.8 14.1 %collective-permute-start.3 = (bf16[2080,128]{1,0:T(8,128)(2,1)}, bf16[2080,128]{1,0:T(8,128)(2,1)S(1)}, u32[]{:S(2)}, u32[]{:S(2)}) collective-permute-start(bf16[2080,128]{1,0:T(8,128)(2,1)} %get-tuple-element.109.refs_0_), channel_id=1, source_target_pairs={{0,1},{1,0},{2,3},{3,2},{4,5},{5,4},{6,7},{7,6},{8,9},{9,8},{10,11... | collective-permute-start | bytes 1597448 | tf_op jit(solution)/shard_map/ppermute | solution.py:685
  6.8 14.1 %collective-permute-start.4 = (bf16[320,512]{1,0:T(8,128)(2,1)}, bf16[320,512]{1,0:T(8,128)(2,1)S(1)}, u32[]{:S(2)}, u32[]{:S(2)}) collective-permute-start(bf16[320,512]{1,0:T(8,128)(2,1)} %get-tuple-element.106), channel_id=1, source_target_pairs={{0,28},{4,0},{8,4},{12,8},{16,12},{20,16},{24,20},{28,24},{1,29},{... | collective-permute-start | bytes 983048 | tf_op jit(solution)/shard_map/ppermute | solution.py:694
  17.4 21.7 %collective-permute-start.2 = (bf16[1040,512]{1,0:T(8,128)(2,1)}, bf16[1040,512]{1,0:T(8,128)(2,1)S(1)}, u32[]{:S(2)}, u32[]{:S(2)}) collective-permute-start(bf16[1040,512]{1,0:T(8,128)(2,1)} %get-tuple-element.110.refs_0_), channel_id=1, source_target_pairs={{0,1},{1,0},{2,3},{3,2},{4,5},{5,4},{6,7},{7,6},{8,9},{9,8},{10,11... | collective-permute-start | bytes 3194888 | tf_op jit(solution)/shard_map/ppermute | solution.py:685
  19.1 6.5 %copy-start.7 = (bf16[2080,128]{1,0:T(8,128)(2,1)}, bf16[2080,128]{1,0:T(8,128)(2,1)S(1)}, u32[]{:S(2)}) copy-start(bf16[2080,128]{1,0:T(8,128)(2,1)S(1)} %collective-permute-done.refs_2_.refs_0_.refs_8_) | copy-start | bytes 1597444
  19.1 28.0 %collective-permute-start.1 = (bf16[1040,512]{1,0:T(8,128)(2,1)}, bf16[1040,512]{1,0:T(8,128)(2,1)S(1)}, u32[]{:S(2)}, u32[]{:S(2)}) collective-permute-start(bf16[1040,512]{1,0:T(8,128)(2,1)} %get-tuple-element.110.refs_0_), channel_id=1, source_target_pairs={{0,2},{1,3},{2,0},{3,1},{4,6},{5,7},{6,4},{7,5},{8,10},{9,11},{10,... | collective-permute-start | bytes 3194888 | tf_op jit(solution)/shard_map/ppermute | solution.py:685
  20.8 4.7 %copy-start.17 = (bf16[320,512]{1,0:T(8,128)(2,1)}, bf16[320,512]{1,0:T(8,128)(2,1)S(1)}, u32[]{:S(2)}) copy-start(bf16[320,512]{1,0:T(8,128)(2,1)S(1)} %collective-permute-done.4.refs_5_) | copy-start | bytes 983044
  20.8 4.7 %copy-start.8 = (bf16[2080,128]{1,0:T(8,128)(2,1)}, bf16[2080,128]{1,0:T(8,128)(2,1)S(1)}, u32[]{:S(2)}) copy-start(bf16[2080,128]{1,0:T(8,128)(2,1)S(1)} %collective-permute-done.3.refs_1_) | copy-start | bytes 1597444
  20.8 4.7 %collective-permute-start.5 = (bf16[2080,128]{1,0:T(8,128)(2,1)S(1)}, bf16[2080,128]{1,0:T(8,128)(2,1)S(1)}, u32[]{:S(2)}, u32[]{:S(2)}) collective-permute-start(bf16[2080,128]{1,0:T(8,128)(2,1)S(1)} %collective-permute-done.refs_2_.refs_0_.refs_8_), channel_id=1, source_target_pairs={{0,1},{1,0},{2,3},{3,2},{4,5},{5,4},{6,7},{7,6},{8,9},{9,8},{10,11... | collective-permute-start | bytes 1597448 | tf_op jit(solution)/shard_map/ppermute | solution.py:685
  20.9 18.1 %collective-permute-start.6 = (bf16[320,512]{1,0:T(8,128)(2,1)}, bf16[320,512]{1,0:T(8,128)(2,1)S(1)}, u32[]{:S(2)}, u32[]{:S(2)}) collective-permute-start(bf16[320,512]{1,0:T(8,128)(2,1)} %get-tuple-element.111), channel_id=1, source_target_pairs={{0,28},{4,0},{8,4},{12,8},{16,12},{20,16},{24,20},{28,24},{1,29},{... | collective-permute-start | bytes 983048 | tf_op jit(solution)/shard_map/ppermute | solution.py:694
  25.5 0.8 copy-start.9
  26.3 12.7 %copy-start.6 = (bf16[704,512]{1,0:T(8,128)(2,1)S(1)}, bf16[704,512]{1,0:T(8,128)(2,1)}, u32[]{:S(2)}) copy-start(bf16[704,512]{1,0:T(8,128)(2,1)} %get-tuple-element.115.refs_3_) | copy-start | bytes 2162692
  39.1 1.1 copy-start
  40.2 7.1 %copy-start.1 = (bf16[704,512]{1,0:T(8,128)(2,1)S(1)}, bf16[704,512]{1,0:T(8,128)(2,1)}, u32[]{:S(2)}) copy-start(bf16[704,512]{1,0:T(8,128)(2,1)} %get-tuple-element.114.refs_2_.refs_1_) | copy-start | bytes 2162692
  47.1 3.0 %collective-permute-start.7 = (bf16[1040,512]{1,0:T(8,128)(2,1)S(1)}, bf16[1040,512]{1,0:T(8,128)(2,1)S(1)}, u32[]{:S(2)}, u32[]{:S(2)}) collective-permute-start(bf16[1040,512]{1,0:T(8,128)(2,1)S(1)} %collective-permute-done.1.refs_0_), channel_id=1, source_target_pairs={{0,1},{1,0},{2,3},{3,2},{4,5},{5,4},{6,7},{7,6},{8,9},{9,8},{10,11... | collective-permute-start | bytes 3194888 | tf_op jit(solution)/shard_map/ppermute | solution.py:685
  47.3 2.8 %copy-start.2 = (f32[704,512]{1,0:T(8,128)S(1)}, f32[704,512]{1,0:T(8,128)}, u32[]{:S(2)}) copy-start(f32[704,512]{1,0:T(8,128)} %get-tuple-element.122.refs_5_) | copy-start | bytes 4325380
  47.3 2.8 %copy-start.5 = (f32[6,512]{1,0:T(8,128)S(1)}, f32[6,512]{1,0:T(8,128)}, u32[]{:S(2)}) copy-start(f32[6,512]{1,0:T(8,128)} %convert_element_type.190.refs_6_.refs_16_) | copy-start | bytes 36868
  50.1 4.8 %copy-start.4 = (bf16[704,512]{1,0:T(8,128)(2,1)S(1)}, bf16[704,512]{1,0:T(8,128)(2,1)}, u32[]{:S(2)}) copy-start(bf16[704,512]{1,0:T(8,128)(2,1)} %get-tuple-element.133.refs_5_.refs_11_) | copy-start | bytes 2162692
  54.3 7.1 %collective-permute-start.8 = (bf16[1024,512]{1,0:T(8,128)(2,1)S(1)}, bf16[1024,512]{1,0:T(8,128)(2,1)S(1)}, u32[]{:S(2)}, u32[]{:S(2)}) collective-permute-start(bf16[1024,512]{1,0:T(8,128)(2,1)S(1)} %get-tuple-element.129), channel_id=1, source_target_pairs={{0,1},{1,0},{2,3},{3,2},{4,5},{5,4},{6,7},{7,6},{8,9},{9,8},{10,11... | collective-permute-start | bytes 3145736 | tf_op jit(solution)/shard_map/ppermute | solution.py:685
  54.8 7.0 %collective-permute-start.9 = (bf16[1024,512]{1,0:T(8,128)(2,1)S(1)}, bf16[1024,512]{1,0:T(8,128)(2,1)S(1)}, u32[]{:S(2)}, u32[]{:S(2)}) collective-permute-start(bf16[1024,512]{1,0:T(8,128)(2,1)S(1)} %get-tuple-element.138), channel_id=1, source_target_pairs={{0,1},{1,0},{2,3},{3,2},{4,5},{5,4},{6,7},{7,6},{8,9},{9,8},{10,11... | collective-permute-start | bytes 3145736 | tf_op jit(solution)/shard_map/ppermute | solution.py:685
  61.0 8.2 %collective-permute-start.11 = (bf16[512,512]{1,0:T(8,128)(2,1)S(1)}, bf16[512,512]{1,0:T(8,128)(2,1)S(1)}, u32[]{:S(2)}, u32[]{:S(2)}) collective-permute-start(bf16[512,512]{1,0:T(8,128)(2,1)S(1)} %get-tuple-element.134), channel_id=1, source_target_pairs={{0,1},{1,0},{2,3},{3,2},{4,5},{5,4},{6,7},{7,6},{8,9},{9,8},{10,11... | collective-permute-start | bytes 1572872 | tf_op jit(solution)/shard_map/ppermute | solution.py:685
  61.4 22.5 %collective-permute-start.10 = (bf16[320,512]{1,0:T(8,128)(2,1)S(1)}, bf16[320,512]{1,0:T(8,128)(2,1)S(1)}, u32[]{:S(2)}, u32[]{:S(2)}) collective-permute-start(bf16[320,512]{1,0:T(8,128)(2,1)S(1)} %get-tuple-element.142), channel_id=1, source_target_pairs={{0,4},{4,8},{8,12},{12,16},{16,20},{20,24},{24,28},{28,0},{1,5},{5... | collective-permute-start | bytes 983048 | tf_op jit(solution)/shard_map/ppermute | solution.py:694
  61.9 24.4 %collective-permute-start.13 = (bf16[512,512]{1,0:T(8,128)(2,1)S(1)}, bf16[512,512]{1,0:T(8,128)(2,1)S(1)}, u32[]{:S(2)}, u32[]{:S(2)}) collective-permute-start(bf16[512,512]{1,0:T(8,128)(2,1)S(1)} %get-tuple-element.198), channel_id=1, source_target_pairs={{0,2},{1,3},{2,0},{3,1},{4,6},{5,7},{6,4},{7,5},{8,10},{9,11},{10,... | collective-permute-start | bytes 1572872 | tf_op jit(solution)/shard_map/ppermute | solution.py:685
  62.6 23.4 %collective-permute-start.12 = (bf16[512,512]{1,0:T(8,128)(2,1)S(1)}, bf16[512,512]{1,0:T(8,128)(2,1)S(1)}, u32[]{:S(2)}, u32[]{:S(2)}) collective-permute-start(bf16[512,512]{1,0:T(8,128)(2,1)S(1)} %pad_maximum_fusion.1), channel_id=1, source_target_pairs={{0,4},{4,0},{8,12},{12,8},{16,20},{20,16},{24,28},{28,24},{1,5},{5... | collective-permute-start | bytes 1572872 | tf_op jit(solution)/shard_map/ppermute | solution.py:689
  69.2 1.3 copy-start.3
  69.4 18.2 %collective-permute-start.15 = (bf16[512,512]{1,0:T(8,128)(2,1)S(1)}, bf16[512,512]{1,0:T(8,128)(2,1)S(1)}, u32[]{:S(2)}, u32[]{:S(2)}) collective-permute-start(bf16[512,512]{1,0:T(8,128)(2,1)S(1)} %add_convert_fusion.2), channel_id=1, source_target_pairs={{0,2},{1,3},{2,0},{3,1},{4,6},{5,7},{6,4},{7,5},{8,10},{9,11},{10,... | collective-permute-start | bytes 1572872 | tf_op jit(solution)/shard_map/ppermute | solution.py:685
  83.8 3.8 %collective-permute-start.14 = (bf16[512,512]{1,0:T(8,128)(2,1)S(1)}, bf16[512,512]{1,0:T(8,128)(2,1)S(1)}, u32[]{:S(2)}, u32[]{:S(2)}) collective-permute-start(bf16[512,512]{1,0:T(8,128)(2,1)S(1)} %get-tuple-element.165), channel_id=1, source_target_pairs={{0,1},{1,0},{2,3},{3,2},{4,5},{5,4},{6,7},{7,6},{8,9},{9,8},{10,11... | collective-permute-start | bytes 1572872 | tf_op jit(solution)/shard_map/ppermute | solution.py:685
  83.9 36.5 %collective-permute-start.24 = (bf16[320,512]{1,0:T(8,128)(2,1)S(1)}, bf16[320,512]{1,0:T(8,128)(2,1)S(1)}, u32[]{:S(2)}, u32[]{:S(2)}) collective-permute-start(bf16[320,512]{1,0:T(8,128)(2,1)S(1)} %get-tuple-element.171), channel_id=1, source_target_pairs={{0,4},{4,8},{8,12},{12,16},{16,20},{20,24},{24,28},{28,0},{1,5},{5... | collective-permute-start | bytes 983048 | tf_op jit(solution)/shard_map/ppermute | solution.py:694
  85.9 57.8 %collective-permute-start.21 = (bf16[640,512]{1,0:T(8,128)(2,1)S(1)}, bf16[640,512]{1,0:T(8,128)(2,1)S(1)}, u32[]{:S(2)}, u32[]{:S(2)}) collective-permute-start(bf16[640,512]{1,0:T(8,128)(2,1)S(1)} %constant_dynamic-update-slice_fusion.refs_0_), channel_id=1, source_target_pairs={{0,1},{1,0},{2,3},{3,2},{4,5},{5,4},{6,7},{7,6},{8,9},{9,8},{10,11... | collective-permute-start | bytes 1966088 | tf_op jit(solution)/shard_map/ppermute | solution.py:685
  86.4 8.6 %collective-permute-start.31 = (bf16[256,512]{1,0:T(8,128)(2,1)S(1)}, bf16[256,512]{1,0:T(8,128)(2,1)S(1)}, u32[]{:S(2)}, u32[]{:S(2)}) collective-permute-start(bf16[256,512]{1,0:T(8,128)(2,1)S(1)} %get-tuple-element.202), channel_id=1, source_target_pairs={{0,2},{1,3},{2,0},{3,1},{4,6},{5,7},{6,4},{7,5},{8,10},{9,11},{10,... | collective-permute-start | bytes 786440 | tf_op jit(solution)/shard_map/ppermute | solution.py:685
  87.8 15.5 %collective-permute-start.16 = (bf16[288,512]{1,0:T(8,128)(2,1)S(1)}, bf16[288,512]{1,0:T(8,128)(2,1)S(1)}, u32[]{:S(2)}, u32[]{:S(2)}) collective-permute-start(bf16[288,512]{1,0:T(8,128)(2,1)S(1)} %pad_maximum_fusion.2), channel_id=1, source_target_pairs={{0,4},{4,0},{8,12},{12,8},{16,20},{20,16},{24,28},{28,24},{1,5},{5... | collective-permute-start | bytes 884744 | tf_op jit(solution)/shard_map/ppermute | solution.py:689
  89.3 8.0 %collective-permute-start.29 = (bf16[256,512]{1,0:T(8,128)(2,1)S(1)}, bf16[256,512]{1,0:T(8,128)(2,1)S(1)}, u32[]{:S(2)}, u32[]{:S(2)}) collective-permute-start(bf16[256,512]{1,0:T(8,128)(2,1)S(1)} %get-tuple-element.199), channel_id=1, source_target_pairs={{0,8},{4,12},{8,0},{12,4},{16,24},{20,28},{24,16},{28,20},{1,9},{5... | collective-permute-start | bytes 786440 | tf_op jit(solution)/shard_map/ppermute | solution.py:689
  94.9 41.6 %collective-permute-start.22 = (bf16[640,512]{1,0:T(8,128)(2,1)S(1)}, bf16[640,512]{1,0:T(8,128)(2,1)S(1)}, u32[]{:S(2)}, u32[]{:S(2)}) collective-permute-start(bf16[640,512]{1,0:T(8,128)(2,1)S(1)} %constant_dynamic-update-slice_fusion.refs_0_), channel_id=1, source_target_pairs={{0,2},{1,3},{2,0},{3,1},{4,6},{5,7},{6,4},{7,5},{8,10},{9,11},{10,... | collective-permute-start | bytes 1966088 | tf_op jit(solution)/shard_map/ppermute | solution.py:685
  97.3 6.2 %collective-permute-start.32 = (bf16[128,512]{1,0:T(8,128)(2,1)S(1)}, bf16[128,512]{1,0:T(8,128)(2,1)S(1)}, u32[]{:S(2)}, u32[]{:S(2)}) collective-permute-start(bf16[128,512]{1,0:T(8,128)(2,1)S(1)} %get-tuple-element.208), channel_id=1, source_target_pairs={{0,8},{4,12},{8,0},{12,4},{16,24},{20,28},{24,16},{28,20},{1,9},{5... | collective-permute-start | bytes 393224 | tf_op jit(solution)/shard_map/ppermute | solution.py:689
  103.3 5.4 %collective-permute-start.30 = (bf16[128,512]{1,0:T(8,128)(2,1)S(1)}, bf16[128,512]{1,0:T(8,128)(2,1)S(1)}, u32[]{:S(2)}, u32[]{:S(2)}) collective-permute-start(bf16[128,512]{1,0:T(8,128)(2,1)S(1)} %get-tuple-element.206), channel_id=1, source_target_pairs={{0,4},{4,0},{8,12},{12,8},{16,20},{20,16},{24,28},{28,24},{1,5},{5... | collective-permute-start | bytes 393224 | tf_op jit(solution)/shard_map/ppermute | solution.py:689
  103.5 6.2 %collective-permute-start.17 = (bf16[160,512]{1,0:T(8,128)(2,1)S(1)}, bf16[160,512]{1,0:T(8,128)(2,1)S(1)}, u32[]{:S(2)}, u32[]{:S(2)}) collective-permute-start(bf16[160,512]{1,0:T(8,128)(2,1)S(1)} %pad_maximum_fusion.4), channel_id=1, source_target_pairs={{0,8},{4,12},{8,0},{12,4},{16,24},{20,28},{24,16},{28,20},{1,9},{5... | collective-permute-start | bytes 491528 | tf_op jit(solution)/shard_map/ppermute | solution.py:689
  109.7 10.6 %collective-permute-start.18 = (bf16[96,512]{1,0:T(8,128)(2,1)S(1)}, bf16[96,512]{1,0:T(8,128)(2,1)S(1)}, u32[]{:S(2)}, u32[]{:S(2)}) collective-permute-start(bf16[96,512]{1,0:T(8,128)(2,1)S(1)} %pad_maximum_fusion.7), channel_id=1, source_target_pairs={{0,16},{4,20},{8,24},{12,28},{16,0},{20,4},{24,8},{28,12},{1,17},{... | collective-permute-start | bytes 294920 | tf_op jit(solution)/shard_map/ppermute | solution.py:689
  112.8 9.4 %collective-permute-start.33 = (bf16[128,512]{1,0:T(8,128)(2,1)S(1)}, bf16[128,512]{1,0:T(8,128)(2,1)S(1)}, u32[]{:S(2)}, u32[]{:S(2)}) collective-permute-start(bf16[128,512]{1,0:T(8,128)(2,1)S(1)} %bitcast.22), channel_id=1, source_target_pairs={{0,16},{4,20},{8,24},{12,28},{16,0},{20,4},{24,8},{28,12},{1,17},{... | collective-permute-start | bytes 393224 | tf_op jit(solution)/shard_map/ppermute | solution.py:689
  120.5 18.1 %collective-permute-start.26 = (bf16[672,512]{1,0:T(8,128)(2,1)S(1)}, bf16[672,512]{1,0:T(8,128)(2,1)S(1)}, u32[]{:S(2)}, u32[]{:S(2)}) collective-permute-start(bf16[672,512]{1,0:T(8,128)(2,1)S(1)} %pad_maximum_fusion.refs_0_), channel_id=1, source_target_pairs={{0,2},{1,3},{2,0},{3,1},{4,6},{5,7},{6,4},{7,5},{8,10},{9,11},{10,... | collective-permute-start | bytes 2064392 | tf_op jit(solution)/shard_map/ppermute | solution.py:685
  122.3 11.3 %collective-permute-start.34 = (bf16[128,512]{1,0:T(8,128)(2,1)S(1)}, bf16[128,512]{1,0:T(8,128)(2,1)S(1)}, u32[]{:S(2)}, u32[]{:S(2)}) collective-permute-start(bf16[128,512]{1,0:T(8,128)(2,1)S(1)} %add_convert_fusion.11), channel_id=1, source_target_pairs={{0,16},{4,20},{8,24},{12,28},{16,0},{20,4},{24,8},{28,12},{1,17},{... | collective-permute-start | bytes 393224 | tf_op jit(solution)/shard_map/ppermute | solution.py:689
  122.4 11.1 %collective-permute-start.19 = (bf16[64,512]{1,0:T(8,128)(2,1)S(1)}, bf16[64,512]{1,0:T(8,128)(2,1)S(1)}, u32[]{:S(2)}, u32[]{:S(2)}) collective-permute-start(bf16[64,512]{1,0:T(8,128)(2,1)S(1)} %add_convert_fusion.15), channel_id=1, source_target_pairs={{0,16},{4,20},{8,24},{12,28},{16,0},{20,4},{24,8},{28,12},{1,17},{... | collective-permute-start | bytes 196616 | tf_op jit(solution)/shard_map/ppermute | solution.py:689
  133.5 5.0 %collective-permute-start.20 = (bf16[128,512]{1,0:T(8,128)(2,1)S(1)}, bf16[128,512]{1,0:T(8,128)(2,1)S(1)}, u32[]{:S(2)}, u32[]{:S(2)}) collective-permute-start(bf16[128,512]{1,0:T(8,128)(2,1)S(1)} %pad_maximum_fusion.6), channel_id=1, source_target_pairs={{0,8},{4,12},{8,0},{12,4},{16,24},{20,28},{24,16},{28,20},{1,9},{5... | collective-permute-start | bytes 393224 | tf_op jit(solution)/shard_map/ppermute | solution.py:689
  133.6 8.3 %collective-permute-start.35 = (bf16[256,512]{1,0:T(8,128)(2,1)S(1)}, bf16[256,512]{1,0:T(8,128)(2,1)S(1)}, u32[]{:S(2)}, u32[]{:S(2)}) collective-permute-start(bf16[256,512]{1,0:T(8,128)(2,1)S(1)} %constant_dynamic-update-slice_fusion.2), channel_id=1, source_target_pairs={{0,4},{4,0},{8,12},{12,8},{16,20},{20,16},{24,28},{28,24},{1,5},{5... | collective-permute-start | bytes 786440 | tf_op jit(solution)/shard_map/ppermute | solution.py:689
  136.6 11.2 %collective-permute-start.25 = (bf16[672,512]{1,0:T(8,128)(2,1)S(1)}, bf16[672,512]{1,0:T(8,128)(2,1)S(1)}, u32[]{:S(2)}, u32[]{:S(2)}) collective-permute-start(bf16[672,512]{1,0:T(8,128)(2,1)S(1)} %pad_maximum_fusion.refs_0_), channel_id=1, source_target_pairs={{0,1},{1,0},{2,3},{3,2},{4,5},{5,4},{6,7},{7,6},{8,9},{9,8},{10,11... | collective-permute-start | bytes 2064392 | tf_op jit(solution)/shard_map/ppermute | solution.py:685
  138.5 6.9 %collective-permute-start.23 = (bf16[640,512]{1,0:T(8,128)(2,1)S(1)}, bf16[640,512]{1,0:T(8,128)(2,1)S(1)}, u32[]{:S(2)}, u32[]{:S(2)}) collective-permute-start(bf16[640,512]{1,0:T(8,128)(2,1)S(1)} %collective-permute-done.22.refs_2_), channel_id=1, source_target_pairs={{0,1},{1,0},{2,3},{3,2},{4,5},{5,4},{6,7},{7,6},{8,9},{9,8},{10,11... | collective-permute-start | bytes 1966088 | tf_op jit(solution)/shard_map/ppermute | solution.py:685
  138.6 9.2 %collective-permute-start.27 = (bf16[672,512]{1,0:T(8,128)(2,1)S(1)}, bf16[672,512]{1,0:T(8,128)(2,1)S(1)}, u32[]{:S(2)}, u32[]{:S(2)}) collective-permute-start(bf16[672,512]{1,0:T(8,128)(2,1)S(1)} %collective-permute-done.26.refs_2_), channel_id=1, source_target_pairs={{0,1},{1,0},{2,3},{3,2},{4,5},{5,4},{6,7},{7,6},{8,9},{9,8},{10,11... | collective-permute-start | bytes 2064392 | tf_op jit(solution)/shard_map/ppermute | solution.py:685
  141.9 12.1 %collective-permute-start.36 = (bf16[512,512]{1,0:T(8,128)(2,1)S(1)}, bf16[512,512]{1,0:T(8,128)(2,1)S(1)}, u32[]{:S(2)}, u32[]{:S(2)}) collective-permute-start(bf16[512,512]{1,0:T(8,128)(2,1)S(1)} %constant_dynamic-update-slice_fusion.4.refs_0_), channel_id=1, source_target_pairs={{0,8},{4,12},{8,0},{12,4},{16,24},{20,28},{24,16},{28,20},{1,9},{5... | collective-permute-start | bytes 1572872 | tf_op jit(solution)/shard_map/ppermute | solution.py:689
  143.7 7.1 %collective-permute-start.28 = (bf16[256,512]{1,0:T(8,128)(2,1)S(1)}, bf16[256,512]{1,0:T(8,128)(2,1)S(1)}, u32[]{:S(2)}, u32[]{:S(2)}) collective-permute-start(bf16[256,512]{1,0:T(8,128)(2,1)S(1)} %pad_maximum_fusion.3.refs_0_), channel_id=1, source_target_pairs={{0,4},{4,0},{8,12},{12,8},{16,20},{20,16},{24,28},{28,24},{1,5},{5... | collective-permute-start | bytes 786440 | tf_op jit(solution)/shard_map/ppermute | solution.py:689

commit v4 on v3

--- a/solution.py
+++ b/solution.py
@@ -965,7 +965,6 @@
         after(dhb, across_a),
         (dx2, dx3, x_win, dh, vecs, vec_mlp, small3, small2, dub01, dub2, dub3),
     )
-    lower_g = shift_rows(low_g, 1)
     got_a1 = swap_tp(a1, 1)
     page_own = jnp.concatenate([after(up_y, a2), lower_y], axis=0)
     from_c = swap_tp(page_own, 1)
@@ -990,6 +989,7 @@
             mark = added(attn) if i == len(bits) else jnp.concatenate(attn, axis=0)
             attn = [mark, swap_rows(mark, gather_a[i - len(bits)])]
         if i == 0:
+            lower_g = shift_rows(after(low_g, mark), 1)
             down = scatter_step([after(down[0], mark), down[1]], bits[0], blocks)
             up = scatter_step([after(up0, mark), up_x], bits[1], blocks)
             from_x = swap_tp(after(page_own, mark), 2)

time: 156 us -> 154 us (0.987)
  starting transfers between devices: 43.1 us -> 41.1 us
where the time goes in v4:
time: 154 us
  Pallas kernels  67.4 us (44%)
  starting transfers between devices  41.1 us (27%)
  waiting for transfers between devices  38.8 us (25%)
  local copies, waits for them, and re-layouts  2.87 us (2%)
  other arithmetic  2.29 us (1%)
    pallas_call x14, Pallas kernels, call(): pl.pallas_call(kernel, out_shape=[jax.ShapeDtypeStruct(s, d) for s, d in...  67.4 us
    ppermute x14, waiting for transfers between devices, swap_rows(): lax.ppermute(x, 'rows', [(i, i ^ bit) for i in range(lax.axis_size('rows'...  32.9 us
    ppermute x14, starting transfers between devices, swap_rows(): lax.ppermute(x, 'rows', [(i, i ^ bit) for i in range(lax.axis_size('rows'...  19.7 us
    ppermute x19, starting transfers between devices, swap_tp(): return lax.ppermute(x, 'tp', [(i, i ^ bit) for i in range(TP)])  11.5 us
    ppermute x4, starting transfers between devices, shift_rows(): return lax.ppermute(x, 'rows', [(i, (i + distance) % n) for i in range(n)])  9.85 us
    ppermute x19, waiting for transfers between devices, swap_tp(): return lax.ppermute(x, 'tp', [(i, i ^ bit) for i in range(TP)])  5.86 us
  transfers between devices with their start and end apart: 37, of which 12 were waited for; matrix products, arithmetic and copies ran while one was open for 2% of the time, Pallas kernels for 38%

profile of v4, /device:TPU:0, one launch (start us, length us, event | category | flops | bytes accessed | tf_op | source)
XLA Modules:
  0.0 153.7 jit_solution(531131659587541519)
XLA Ops:
  0.7 3.0 %head.1 = (bf16[320,512]{1,0:T(8,128)(2,1)}, bf16[2080,128]{1,0:T(8,128)(2,1)}) custom-call(bf16[10,240,512]{2,1,0:T(8,128)(2,1)} %x.3, bf16[1536,128]{1,0:T(8,128)(2,1)} %bitcast.21, bf16[128,512]{1,0:T(8,128)(2,1)} %wproj.1, bf16[4,361]{1,0:T(4,128)(2,1)} %bitcast.23, bf16[2,128]{1,0:T(2,128)(2,1)} %bias.1), custom_call_target="tpu_custom_call" | custom-call | flops 600000000 | bytes 1024 | tf_op jit(solution)/shard_map/head/pallas_call | solution.py:152
  3.8 3.0 %collective-permute-start = (bf16[2080,128]{1,0:T(8,128)(2,1)}, bf16[2080,128]{1,0:T(8,128)(2,1)S(1)}, u32[]{:S(2)}, u32[]{:S(2)}) collective-permute-start(bf16[2080,128]{1,0:T(8,128)(2,1)} %get-tuple-element.110.refs_0_), channel_id=1, source_target_pairs={{0,2},{1,3},{2,0},{3,1},{4,6},{5,7},{6,4},{7,5},{8,10},{9,11},{10,... | collective-permute-start | bytes 1597448 | tf_op jit(solution)/shard_map/ppermute | solution.py:685
  6.8 4.6 %collective-permute-start.4 = (bf16[320,512]{1,0:T(8,128)(2,1)}, bf16[320,512]{1,0:T(8,128)(2,1)S(1)}, u32[]{:S(2)}, u32[]{:S(2)}) collective-permute-start(bf16[320,512]{1,0:T(8,128)(2,1)} %get-tuple-element.107), channel_id=1, source_target_pairs={{0,28},{4,0},{8,4},{12,8},{16,12},{20,16},{24,20},{28,24},{1,29},{... | collective-permute-start | bytes 983048 | tf_op jit(solution)/shard_map/ppermute | solution.py:694
  11.5 0.6 convert_element_type.190.refs_6_.refs_16_
  12.1 0.6 broadcast_in_dim.3.ubias
  12.7 4.7 %rest.1 = (bf16[320,512]{1,0:T(8,128)(2,1)}, bf16[704,512]{1,0:T(8,128)(2,1)}, bf16[704,512]{1,0:T(8,128)(2,1)}, bf16[1040,512]{1,0:T(8,128)(2,1)}) custom-call(bf16[10,240,512]{2,1,0:T(8,128)(2,1)} %x.3, bf16[10,240,512]{2,1,0:T(8,128)(2,1)} %g, bf16[512,512]{1,0:T(8,128)(2,1)} %up.1, bf16[512,512]{1,0:T(8,128)(2,1)} %down.1, ...), custom_call_target="tpu_custom_call" | custom-call | flops 1000000000 | bytes 1024 | tf_op jit(solution)/shard_map/rest/pallas_call | solution.py:152
  17.4 0.3 collective-permute-start.2
  17.7 1.4 collective-permute-done.refs_2_.refs_0_.refs_8_
  19.1 1.7 %collective-permute-start.1 = (bf16[1040,512]{1,0:T(8,128)(2,1)}, bf16[1040,512]{1,0:T(8,128)(2,1)S(1)}, u32[]{:S(2)}, u32[]{:S(2)}) collective-permute-start(bf16[1040,512]{1,0:T(8,128)(2,1)} %get-tuple-element.111.refs_0_), channel_id=1, source_target_pairs={{0,2},{1,3},{2,0},{3,1},{4,6},{5,7},{6,4},{7,5},{8,10},{9,11},{10,... | collective-permute-start | bytes 3194888 | tf_op jit(solution)/shard_map/ppermute | solution.py:685
  20.9 4.6 %collective-permute-start.6 = (bf16[320,512]{1,0:T(8,128)(2,1)}, bf16[320,512]{1,0:T(8,128)(2,1)S(1)}, u32[]{:S(2)}, u32[]{:S(2)}) collective-permute-start(bf16[320,512]{1,0:T(8,128)(2,1)} %get-tuple-element.112), channel_id=1, source_target_pairs={{0,28},{4,0},{8,4},{12,8},{16,12},{20,16},{24,20},{28,24},{1,29},{... | collective-permute-start | bytes 983048 | tf_op jit(solution)/shard_map/ppermute | solution.py:694
  25.5 0.8 copy-done.9
  26.4 12.7 %attn_fwd.1 = (bf16[3,704,128]{2,1,0:T(8,128)(2,1)}, bf16[3,704,128]{2,1,0:T(8,128)(2,1)}, bf16[3,704,128]{2,1,0:T(8,128)(2,1)}, bf16[3,704,128]{2,1,0:T(8,128)(...) custom-call(s32[1,2]{1,0:T(1,128)} %bounds.1, ...), custom_call_target="tpu_custom_call" | custom-call | flops 2800000000 | bytes 1024 | tf_op jit(solution)/shard_map/attn_fwd/pallas_call | solution.py:152
  39.1 1.1 copy-done
  40.2 6.9 %mlp_first.1 = (bf16[1024,512]{1,0:T(8,128)(2,1)S(1)}, bf16[1024,512]{1,0:T(8,128)(2,1)S(1)}, f32[8,128]{1,0:T(8,128)S(1)}, bf16[704,512]{1,0:T(8,128)(2,1)S(1)}...) custom-call(bf16[1040,512]{1,0:T(8,128)(2,1)} %get-tuple-element.111.refs_0_, ...), custom_call_target="tpu_custom_call" | custom-call | flops 1800000000 | bytes 1024 | tf_op jit(solution)/shard_map/mlp_first/pallas_call | solution.py:152
  47.1 0.2 collective-permute-start.7
  47.3 2.8 %mlp_mid.1 = (bf16[1024,512]{1,0:T(8,128)(2,1)S(1)}, f32[4,128]{1,0:T(4,128)S(1)}, f32[704,512]{1,0:T(8,128)S(1)}, f32[704,512]{1,0:T(8,128)S(1)}) custom-call(bf16[1040,512]{1,0:T(8,128)(2,1)S(1)} %collective-permute-done.1.refs_0_, bf16[704,512]{1,0:T(8,128)(2,1)S(1)} %copy-done.1, bf16[704,512]{1,0:T(8,128)(2,1)S(1)} %get-tuple-element.119.refs_2_, ...), custom_call_target="tpu_custom_call" | custom-call | flops 1000000000 | bytes 1024 | tf_op jit(solution)/shard_map/mlp_mid/pallas_call | solution.py:152
  50.1 4.2 %mlp_last.1 = (bf16[1024,512]{1,0:T(8,128)(2,1)S(1)}, f32[4,128]{1,0:T(4,128)S(1)}, bf16[320,512]{1,0:T(8,128)(2,1)S(1)}, bf16[320,512]{1,0:T(8,128)(2,1)S(1)}, ...) custom-call(bf16[1040,512]{1,0:T(8,128)(2,1)S(1)} %collective-permute-done.7.refs_0_, ...), custom_call_target="tpu_custom_call" | custom-call | flops 1000000000 | bytes 1024 | tf_op jit(solution)/shard_map/mlp_last/pallas_call | solution.py:152
  54.3 0.4 collective-permute-start.8
  54.8 0.2 collective-permute-start.9
  54.9 6.1 %attn_bwd_3.1 = (bf16[512,512]{1,0:T(8,128)(2,1)S(1)}, f32[16,128]{1,0:T(8,128)S(1)}, bf16[704,384]{1,0:T(8,128)(2,1)S(1)}) custom-call(bf16[2080,128]{1,0:T(8,128)(2,1)} %copy-done.9, bf16[704,128]{1,0:T(8,128)(2,1)} %get-tuple-element.131.refs_1_, bf16[3,704,128]{2,1,0:T(8,128)(2,1)} %get-tuple-element.132.refs_2_, ...), custom_call_target="tpu_custom_call" | custom-call | flops 1400000000 | bytes 1024 | tf_op jit(solution)/shard_map/attn_bwd_3/pallas_call | solution.py:152
  61.0 0.4 collective-permute-start.11
  61.4 0.3 add_convert_fusion.3
  61.7 0.1 add_convert_fusion.4
  61.9 0.6 collective-permute-start.13
  62.6 0.8 collective-permute-start.12
  63.4 5.9 %attn_bwd_2.1 = (bf16[512,512]{1,0:T(8,128)(2,1)S(1)}, f32[16,128]{1,0:T(8,128)S(1)}, bf16[704,384]{1,0:T(8,128)(2,1)S(1)}) custom-call(bf16[2080,128]{1,0:T(8,128)(2,1)} %copy-done.7, bf16[704,128]{1,0:T(8,128)(2,1)} %get-tuple-element.125.refs_1_, bf16[3,704,128]{2,1,0:T(8,128)(2,1)} %get-tuple-element.126.refs_2_, ...), custom_call_target="tpu_custom_call" | custom-call | flops 1400000000 | bytes 1024 | tf_op jit(solution)/shard_map/attn_bwd_2/pallas_call | solution.py:152
  69.2 0.1 add_convert_fusion.2
  69.4 1.2 collective-permute-start.15
  70.6 13.2 %attn_bwd_01.1 = (bf16[512,512]{1,0:T(8,128)(2,1)S(1)}, bf16[512,512]{1,0:T(8,128)(2,1)S(1)}, bf16[320,512]{1,0:T(8,128)(2,1)S(1)}, bf16[320,512]{1,0:T(8,128)(2,1)S(1)}, bf16[32,512]{1,0:T(8,128)(2,1)S(1)}) custom-call(bf16[2080,128]{1,0:T(8,128)(2,1)} %get-tuple-element.110.refs_0_, bf16[2080,128]{1,0:T(8,128)(2,1)} %copy-done.8, ...), custom_call_target="tpu_custom_call" | custom-call | flops 2200000000 | bytes 1024 | tf_op jit(solution)/shard_map/attn_bwd_01/pallas_call | solution.py:152
  83.9 0.6 collective-permute-start.21
  84.5 0.1 add_convert_fusion.7
  84.6 1.0 collective-permute-start.31
  85.6 0.2 add_convert_fusion.1
  85.9 1.3 collective-permute-done.15
  87.2 0.2 add_convert_fusion
  87.5 0.4 collective-permute-start.16
  87.9 1.3 collective-permute-start.29
  89.1 0.7 collective-permute-start.24
  89.8 3.1 %collective-permute-done.31 = bf16[256,512]{1,0:T(8,128)(2,1)S(1)} collective-permute-done((bf16[256,512]{1,0:T(8,128)(2,1)S(1)}, bf16[256,512]{1,0:T(8,128)(2,1)S(1)}, u32[]{:S(2)}, u32[]{:S(2)}) %collective-permute-start.31) | collective-permute-done | bytes 262176 | tf_op jit(solution)/shard_map/ppermute | solution.py:685
  92.9 0.9 collective-permute-start.22
  93.9 1.9 %collective-permute-done.29 = bf16[256,512]{1,0:T(8,128)(2,1)S(1)} collective-permute-done((bf16[256,512]{1,0:T(8,128)(2,1)S(1)}, bf16[256,512]{1,0:T(8,128)(2,1)S(1)}, u32[]{:S(2)}, u32[]{:S(2)}) %collective-permute-start.29) | collective-permute-done | bytes 262176 | tf_op jit(solution)/shard_map/ppermute | solution.py:689
  95.8 0.4 collective-permute-start.32
  96.3 2.9 %collective-permute-start.30 = (bf16[128,512]{1,0:T(8,128)(2,1)S(1)}, bf16[128,512]{1,0:T(8,128)(2,1)S(1)}, u32[]{:S(2)}, u32[]{:S(2)}) collective-permute-start(bf16[128,512]{1,0:T(8,128)(2,1)S(1)} %get-tuple-element.208), channel_id=1, source_target_pairs={{0,4},{4,0},{8,12},{12,8},{16,20},{20,16},{24,28},{28,24},{1,5},{5... | collective-permute-start | bytes 393224 | tf_op jit(solution)/shard_map/ppermute | solution.py:689
  99.3 1.5 collective-permute-done.32
  100.8 0.4 collective-permute-start.17
  101.2 6.1 %collective-permute-done.30 = bf16[128,512]{1,0:T(8,128)(2,1)S(1)} collective-permute-done((bf16[128,512]{1,0:T(8,128)(2,1)S(1)}, bf16[128,512]{1,0:T(8,128)(2,1)S(1)}, u32[]{:S(2)}, u32[]{:S(2)}) %collective-permute-start.30) | collective-permute-done | bytes 131104 | tf_op jit(solution)/shard_map/ppermute | solution.py:689
  107.5 3.0 %collective-permute-start.18 = (bf16[96,512]{1,0:T(8,128)(2,1)S(1)}, bf16[96,512]{1,0:T(8,128)(2,1)S(1)}, u32[]{:S(2)}, u32[]{:S(2)}) collective-permute-start(bf16[96,512]{1,0:T(8,128)(2,1)S(1)} %pad_maximum_fusion.7), channel_id=1, source_target_pairs={{0,16},{4,20},{8,24},{12,28},{16,0},{20,4},{24,8},{28,12},{1,17},{... | collective-permute-start | bytes 294920 | tf_op jit(solution)/shard_map/ppermute | solution.py:689
  110.5 7.9 %collective-permute-done.18 = bf16[96,512]{1,0:T(8,128)(2,1)S(1)} collective-permute-done((bf16[96,512]{1,0:T(8,128)(2,1)S(1)}, bf16[96,512]{1,0:T(8,128)(2,1)S(1)}, u32[]{:S(2)}, u32[]{:S(2)}) %collective-permute-start.18) | collective-permute-done | bytes 98336 | tf_op jit(solution)/shard_map/ppermute | solution.py:689
  118.6 0.3 collective-permute-start.26
  118.9 1.3 collective-permute-done.33
  120.4 2.9 %collective-permute-start.19 = (bf16[64,512]{1,0:T(8,128)(2,1)S(1)}, bf16[64,512]{1,0:T(8,128)(2,1)S(1)}, u32[]{:S(2)}, u32[]{:S(2)}) collective-permute-start(bf16[64,512]{1,0:T(8,128)(2,1)S(1)} %add_convert_fusion.15), channel_id=1, source_target_pairs={{0,16},{4,20},{8,24},{12,28},{16,0},{20,4},{24,8},{28,12},{1,17},{... | collective-permute-start | bytes 196616 | tf_op jit(solution)/shard_map/ppermute | solution.py:689
  123.3 8.0 %collective-permute-done.19 = bf16[64,512]{1,0:T(8,128)(2,1)S(1)} collective-permute-done((bf16[64,512]{1,0:T(8,128)(2,1)S(1)}, bf16[64,512]{1,0:T(8,128)(2,1)S(1)}, u32[]{:S(2)}, u32[]{:S(2)}) %collective-permute-start.19) | collective-permute-done | bytes 65568 | tf_op jit(solution)/shard_map/ppermute | solution.py:689
  131.5 4.2 %collective-permute-start.35 = (bf16[256,512]{1,0:T(8,128)(2,1)S(1)}, bf16[256,512]{1,0:T(8,128)(2,1)S(1)}, u32[]{:S(2)}, u32[]{:S(2)}) collective-permute-start(bf16[256,512]{1,0:T(8,128)(2,1)S(1)} %constant_dynamic-update-slice_fusion.2), channel_id=1, source_target_pairs={{0,4},{4,0},{8,12},{12,8},{16,20},{20,16},{24,28},{28,24},{1,5},{5... | collective-permute-start | bytes 786440 | tf_op jit(solution)/shard_map/ppermute | solution.py:689
  135.6 0.8 collective-permute-done.20
  136.4 0.6 collective-permute-start.27
  137.0 3.5 %collective-permute-done.35 = bf16[256,512]{1,0:T(8,128)(2,1)S(1)} collective-permute-done((bf16[256,512]{1,0:T(8,128)(2,1)S(1)}, bf16[256,512]{1,0:T(8,128)(2,1)S(1)}, u32[]{:S(2)}, u32[]{:S(2)}) %collective-permute-start.35) | collective-permute-done | bytes 262176 | tf_op jit(solution)/shard_map/ppermute | solution.py:689
  140.5 1.3 collective-permute-start.36
  141.9 2.0 %collective-permute-start.28 = (bf16[256,512]{1,0:T(8,128)(2,1)S(1)}, bf16[256,512]{1,0:T(8,128)(2,1)S(1)}, u32[]{:S(2)}, u32[]{:S(2)}) collective-permute-start(bf16[256,512]{1,0:T(8,128)(2,1)S(1)} %pad_maximum_fusion.3.refs_0_), channel_id=1, source_target_pairs={{0,4},{4,0},{8,12},{12,8},{16,20},{20,16},{24,28},{28,24},{1,5},{5... | collective-permute-start | bytes 786440 | tf_op jit(solution)/shard_map/ppermute | solution.py:689
  143.9 2.3 %page_y.1 = bf16[10,240,512]{2,1,0:T(8,128)(2,1)} custom-call(bf16[640,512]{1,0:T(8,128)(2,1)S(1)} %constant_dynamic-update-slice_fusion.refs_0_, bf16[640,512]{1,0:T(8,128)(2,1)S(1)} %collective-permute-done.21.refs_1_, bf16[640,512]{1,0:T(8,128)(2,1)S(1)} %collective-permute-done.22.refs_2_, bf16[640,512]{1,0:T(8,128)(2,1)S(1)} %collective-permute-done.23.refs_3_), custom_call_target="tpu_custom_call" | custom-call | flops 2000000 | bytes 1024 | tf_op jit(solution)/shard_map/page_y/pallas_call | solution.py:152
  146.2 0.6 small.1
  146.9 2.3 %page_g.1 = bf16[10,240,512]{2,1,0:T(8,128)(2,1)} custom-call(bf16[672,512]{1,0:T(8,128)(2,1)S(1)} %pad_maximum_fusion.refs_0_, bf16[672,512]{1,0:T(8,128)(2,1)S(1)} %collective-permute-done.25.refs_1_, bf16[672,512]{1,0:T(8,128)(2,1)S(1)} %collective-permute-done.26.refs_2_, bf16[672,512]{1,0:T(8,128)(2,1)S(1)} %collective-permute-done.27.refs_3_), custom_call_target="tpu_custom_call" | custom-call | flops 2000000 | bytes 1024 | tf_op jit(solution)/shard_map/page_g/pallas_call | solution.py:152
  149.2 1.1 finish_attn.1
  150.3 1.9 %collective-permute-done.36.refs_1_ = bf16[512,512]{1,0:T(8,128)(2,1)S(1)} collective-permute-done((bf16[512,512]{1,0:T(8,128)(2,1)S(1)}, bf16[512,512]{1,0:T(8,128)(2,1)S(1)}, u32[]{:S(2)}, u32[]{:S(2)}) %collective-permute-start.36) | collective-permute-done | bytes 524320 | tf_op jit(solution)/shard_map/ppermute | solution.py:689
  152.2 1.5 finish_mlp.1
  (108 shorter events, 1.4 us)
Async XLA Ops:
  0.7 10.7 %copy-start.10 = (bf16[512]{0:T(512)(128)(2,1)S(1)}, bf16[512]{0:T(512)(128)(2,1)}, u32[]{:S(2)}) copy-start(bf16[512]{0:T(512)(128)(2,1)} %param.19) | copy-start | bytes 3076
  0.7 10.7 %copy-start.11 = (bf16[512]{0:T(512)(128)(2,1)S(1)}, bf16[512]{0:T(512)(128)(2,1)}, u32[]{:S(2)}) copy-start(bf16[512]{0:T(512)(128)(2,1)} %param.20) | copy-start | bytes 3076
  0.7 10.7 %copy-start.12 = (bf16[512]{0:T(512)(128)(2,1)S(1)}, bf16[512]{0:T(512)(128)(2,1)}, u32[]{:S(2)}) copy-start(bf16[512]{0:T(512)(128)(2,1)} %param.26) | copy-start | bytes 3076
  0.7 10.7 %copy-start.13 = (bf16[512]{0:T(512)(128)(2,1)S(1)}, bf16[512]{0:T(512)(128)(2,1)}, u32[]{:S(2)}) copy-start(bf16[512]{0:T(512)(128)(2,1)} %param.27) | copy-start | bytes 3076
  0.7 10.7 %copy-start.14 = (bf16[512]{0:T(512)(128)(2,1)S(1)}, bf16[512]{0:T(512)(128)(2,1)}, u32[]{:S(2)}) copy-start(bf16[512]{0:T(512)(128)(2,1)} %param.25) | copy-start | bytes 3076
  0.7 10.7 %copy-start.15 = (bf16[512]{0:T(512)(128)(2,1)S(1)}, bf16[512]{0:T(512)(128)(2,1)}, u32[]{:S(2)}) copy-start(bf16[512]{0:T(512)(128)(2,1)} %param.31) | copy-start | bytes 3076
  0.7 11.4 %copy-start.16 = (bf16[512]{0:T(512)(128)(2,1)S(1)}, bf16[512]{0:T(512)(128)(2,1)}, u32[]{:S(2)}) copy-start(bf16[512]{0:T(512)(128)(2,1)} %param.29) | copy-start | bytes 3076
  3.8 15.3 %collective-permute-start = (bf16[2080,128]{1,0:T(8,128)(2,1)}, bf16[2080,128]{1,0:T(8,128)(2,1)S(1)}, u32[]{:S(2)}, u32[]{:S(2)}) collective-permute-start(bf16[2080,128]{1,0:T(8,128)(2,1)} %get-tuple-element.110.refs_0_), channel_id=1, source_target_pairs={{0,2},{1,3},{2,0},{3,1},{4,6},{5,7},{6,4},{7,5},{8,10},{9,11},{10,... | collective-permute-start | bytes 1597448 | tf_op jit(solution)/shard_map/ppermute | solution.py:685
  6.8 14.1 %collective-permute-start.3 = (bf16[2080,128]{1,0:T(8,128)(2,1)}, bf16[2080,128]{1,0:T(8,128)(2,1)S(1)}, u32[]{:S(2)}, u32[]{:S(2)}) collective-permute-start(bf16[2080,128]{1,0:T(8,128)(2,1)} %get-tuple-element.110.refs_0_), channel_id=1, source_target_pairs={{0,1},{1,0},{2,3},{3,2},{4,5},{5,4},{6,7},{7,6},{8,9},{9,8},{10,11... | collective-permute-start | bytes 1597448 | tf_op jit(solution)/shard_map/ppermute | solution.py:685
  6.8 14.1 %collective-permute-start.4 = (bf16[320,512]{1,0:T(8,128)(2,1)}, bf16[320,512]{1,0:T(8,128)(2,1)S(1)}, u32[]{:S(2)}, u32[]{:S(2)}) collective-permute-start(bf16[320,512]{1,0:T(8,128)(2,1)} %get-tuple-element.107), channel_id=1, source_target_pairs={{0,28},{4,0},{8,4},{12,8},{16,12},{20,16},{24,20},{28,24},{1,29},{... | collective-permute-start | bytes 983048 | tf_op jit(solution)/shard_map/ppermute | solution.py:694
  17.4 21.7 %collective-permute-start.2 = (bf16[1040,512]{1,0:T(8,128)(2,1)}, bf16[1040,512]{1,0:T(8,128)(2,1)S(1)}, u32[]{:S(2)}, u32[]{:S(2)}) collective-permute-start(bf16[1040,512]{1,0:T(8,128)(2,1)} %get-tuple-element.111.refs_0_), channel_id=1, source_target_pairs={{0,1},{1,0},{2,3},{3,2},{4,5},{5,4},{6,7},{7,6},{8,9},{9,8},{10,11... | collective-permute-start | bytes 3194888 | tf_op jit(solution)/shard_map/ppermute | solution.py:685
  19.1 6.5 %copy-start.7 = (bf16[2080,128]{1,0:T(8,128)(2,1)}, bf16[2080,128]{1,0:T(8,128)(2,1)S(1)}, u32[]{:S(2)}) copy-start(bf16[2080,128]{1,0:T(8,128)(2,1)S(1)} %collective-permute-done.refs_2_.refs_0_.refs_8_) | copy-start | bytes 1597444
  19.1 28.0 %collective-permute-start.1 = (bf16[1040,512]{1,0:T(8,128)(2,1)}, bf16[1040,512]{1,0:T(8,128)(2,1)S(1)}, u32[]{:S(2)}, u32[]{:S(2)}) collective-permute-start(bf16[1040,512]{1,0:T(8,128)(2,1)} %get-tuple-element.111.refs_0_), channel_id=1, source_target_pairs={{0,2},{1,3},{2,0},{3,1},{4,6},{5,7},{6,4},{7,5},{8,10},{9,11},{10,... | collective-permute-start | bytes 3194888 | tf_op jit(solution)/shard_map/ppermute | solution.py:685
  20.8 4.7 %copy-start.17 = (bf16[320,512]{1,0:T(8,128)(2,1)}, bf16[320,512]{1,0:T(8,128)(2,1)S(1)}, u32[]{:S(2)}) copy-start(bf16[320,512]{1,0:T(8,128)(2,1)S(1)} %collective-permute-done.4.refs_5_) | copy-start | bytes 983044
  20.8 4.7 %copy-start.8 = (bf16[2080,128]{1,0:T(8,128)(2,1)}, bf16[2080,128]{1,0:T(8,128)(2,1)S(1)}, u32[]{:S(2)}) copy-start(bf16[2080,128]{1,0:T(8,128)(2,1)S(1)} %collective-permute-done.3.refs_1_) | copy-start | bytes 1597444
  20.8 4.7 %collective-permute-start.5 = (bf16[2080,128]{1,0:T(8,128)(2,1)S(1)}, bf16[2080,128]{1,0:T(8,128)(2,1)S(1)}, u32[]{:S(2)}, u32[]{:S(2)}) collective-permute-start(bf16[2080,128]{1,0:T(8,128)(2,1)S(1)} %collective-permute-done.refs_2_.refs_0_.refs_8_), channel_id=1, source_target_pairs={{0,1},{1,0},{2,3},{3,2},{4,5},{5,4},{6,7},{7,6},{8,9},{9,8},{10,11... | collective-permute-start | bytes 1597448 | tf_op jit(solution)/shard_map/ppermute | solution.py:685
  20.9 18.1 %collective-permute-start.6 = (bf16[320,512]{1,0:T(8,128)(2,1)}, bf16[320,512]{1,0:T(8,128)(2,1)S(1)}, u32[]{:S(2)}, u32[]{:S(2)}) collective-permute-start(bf16[320,512]{1,0:T(8,128)(2,1)} %get-tuple-element.112), channel_id=1, source_target_pairs={{0,28},{4,0},{8,4},{12,8},{16,12},{20,16},{24,20},{28,24},{1,29},{... | collective-permute-start | bytes 983048 | tf_op jit(solution)/shard_map/ppermute | solution.py:694
  25.5 0.8 copy-start.9
  26.3 12.7 %copy-start.6 = (bf16[704,512]{1,0:T(8,128)(2,1)S(1)}, bf16[704,512]{1,0:T(8,128)(2,1)}, u32[]{:S(2)}) copy-start(bf16[704,512]{1,0:T(8,128)(2,1)} %get-tuple-element.116.refs_3_) | copy-start | bytes 2162692
  39.1 1.1 copy-start
  40.2 7.1 %copy-start.1 = (bf16[704,512]{1,0:T(8,128)(2,1)S(1)}, bf16[704,512]{1,0:T(8,128)(2,1)}, u32[]{:S(2)}) copy-start(bf16[704,512]{1,0:T(8,128)(2,1)} %get-tuple-element.115.refs_2_.refs_1_) | copy-start | bytes 2162692
  47.1 3.0 %collective-permute-start.7 = (bf16[1040,512]{1,0:T(8,128)(2,1)S(1)}, bf16[1040,512]{1,0:T(8,128)(2,1)S(1)}, u32[]{:S(2)}, u32[]{:S(2)}) collective-permute-start(bf16[1040,512]{1,0:T(8,128)(2,1)S(1)} %collective-permute-done.1.refs_0_), channel_id=1, source_target_pairs={{0,1},{1,0},{2,3},{3,2},{4,5},{5,4},{6,7},{7,6},{8,9},{9,8},{10,11... | collective-permute-start | bytes 3194888 | tf_op jit(solution)/shard_map/ppermute | solution.py:685
  47.3 2.8 %copy-start.2 = (f32[704,512]{1,0:T(8,128)S(1)}, f32[704,512]{1,0:T(8,128)}, u32[]{:S(2)}) copy-start(f32[704,512]{1,0:T(8,128)} %get-tuple-element.123.refs_5_) | copy-start | bytes 4325380
  47.3 2.8 %copy-start.5 = (f32[6,512]{1,0:T(8,128)S(1)}, f32[6,512]{1,0:T(8,128)}, u32[]{:S(2)}) copy-start(f32[6,512]{1,0:T(8,128)} %convert_element_type.190.refs_6_.refs_16_) | copy-start | bytes 36868
  50.1 4.8 %copy-start.4 = (bf16[704,512]{1,0:T(8,128)(2,1)S(1)}, bf16[704,512]{1,0:T(8,128)(2,1)}, u32[]{:S(2)}) copy-start(bf16[704,512]{1,0:T(8,128)(2,1)} %get-tuple-element.134.refs_5_.refs_11_) | copy-start | bytes 2162692
  54.3 7.1 %collective-permute-start.8 = (bf16[1024,512]{1,0:T(8,128)(2,1)S(1)}, bf16[1024,512]{1,0:T(8,128)(2,1)S(1)}, u32[]{:S(2)}, u32[]{:S(2)}) collective-permute-start(bf16[1024,512]{1,0:T(8,128)(2,1)S(1)} %get-tuple-element.130), channel_id=1, source_target_pairs={{0,1},{1,0},{2,3},{3,2},{4,5},{5,4},{6,7},{7,6},{8,9},{9,8},{10,11... | collective-permute-start | bytes 3145736 | tf_op jit(solution)/shard_map/ppermute | solution.py:685
  54.8 7.0 %collective-permute-start.9 = (bf16[1024,512]{1,0:T(8,128)(2,1)S(1)}, bf16[1024,512]{1,0:T(8,128)(2,1)S(1)}, u32[]{:S(2)}, u32[]{:S(2)}) collective-permute-start(bf16[1024,512]{1,0:T(8,128)(2,1)S(1)} %get-tuple-element.139), channel_id=1, source_target_pairs={{0,1},{1,0},{2,3},{3,2},{4,5},{5,4},{6,7},{7,6},{8,9},{9,8},{10,11... | collective-permute-start | bytes 3145736 | tf_op jit(solution)/shard_map/ppermute | solution.py:685
  61.0 8.2 %collective-permute-start.11 = (bf16[512,512]{1,0:T(8,128)(2,1)S(1)}, bf16[512,512]{1,0:T(8,128)(2,1)S(1)}, u32[]{:S(2)}, u32[]{:S(2)}) collective-permute-start(bf16[512,512]{1,0:T(8,128)(2,1)S(1)} %get-tuple-element.135), channel_id=1, source_target_pairs={{0,1},{1,0},{2,3},{3,2},{4,5},{5,4},{6,7},{7,6},{8,9},{9,8},{10,11... | collective-permute-start | bytes 1572872 | tf_op jit(solution)/shard_map/ppermute | solution.py:685
  61.4 22.5 %collective-permute-start.10 = (bf16[320,512]{1,0:T(8,128)(2,1)S(1)}, bf16[320,512]{1,0:T(8,128)(2,1)S(1)}, u32[]{:S(2)}, u32[]{:S(2)}) collective-permute-start(bf16[320,512]{1,0:T(8,128)(2,1)S(1)} %get-tuple-element.143), channel_id=1, source_target_pairs={{0,4},{4,8},{8,12},{12,16},{16,20},{20,24},{24,28},{28,0},{1,5},{5... | collective-permute-start | bytes 983048 | tf_op jit(solution)/shard_map/ppermute | solution.py:694
  61.9 23.7 %collective-permute-start.13 = (bf16[512,512]{1,0:T(8,128)(2,1)S(1)}, bf16[512,512]{1,0:T(8,128)(2,1)S(1)}, u32[]{:S(2)}, u32[]{:S(2)}) collective-permute-start(bf16[512,512]{1,0:T(8,128)(2,1)S(1)} %get-tuple-element.200), channel_id=1, source_target_pairs={{0,2},{1,3},{2,0},{3,1},{4,6},{5,7},{6,4},{7,5},{8,10},{9,11},{10,... | collective-permute-start | bytes 1572872 | tf_op jit(solution)/shard_map/ppermute | solution.py:685
  62.6 21.9 %collective-permute-start.12 = (bf16[512,512]{1,0:T(8,128)(2,1)S(1)}, bf16[512,512]{1,0:T(8,128)(2,1)S(1)}, u32[]{:S(2)}, u32[]{:S(2)}) collective-permute-start(bf16[512,512]{1,0:T(8,128)(2,1)S(1)} %pad_maximum_fusion.1), channel_id=1, source_target_pairs={{0,4},{4,0},{8,12},{12,8},{16,20},{20,16},{24,28},{28,24},{1,5},{5... | collective-permute-start | bytes 1572872 | tf_op jit(solution)/shard_map/ppermute | solution.py:689
  69.2 1.3 copy-start.3
  69.4 17.8 %collective-permute-start.15 = (bf16[512,512]{1,0:T(8,128)(2,1)S(1)}, bf16[512,512]{1,0:T(8,128)(2,1)S(1)}, u32[]{:S(2)}, u32[]{:S(2)}) collective-permute-start(bf16[512,512]{1,0:T(8,128)(2,1)S(1)} %add_convert_fusion.2), channel_id=1, source_target_pairs={{0,2},{1,3},{2,0},{3,1},{4,6},{5,7},{6,4},{7,5},{8,10},{9,11},{10,... | collective-permute-start | bytes 1572872 | tf_op jit(solution)/shard_map/ppermute | solution.py:685
  83.8 2.1 %collective-permute-start.14 = (bf16[512,512]{1,0:T(8,128)(2,1)S(1)}, bf16[512,512]{1,0:T(8,128)(2,1)S(1)}, u32[]{:S(2)}, u32[]{:S(2)}) collective-permute-start(bf16[512,512]{1,0:T(8,128)(2,1)S(1)} %get-tuple-element.166), channel_id=1, source_target_pairs={{0,1},{1,0},{2,3},{3,2},{4,5},{5,4},{6,7},{7,6},{8,9},{9,8},{10,11... | collective-permute-start | bytes 1572872 | tf_op jit(solution)/shard_map/ppermute | solution.py:685
  83.9 57.9 %collective-permute-start.21 = (bf16[640,512]{1,0:T(8,128)(2,1)S(1)}, bf16[640,512]{1,0:T(8,128)(2,1)S(1)}, u32[]{:S(2)}, u32[]{:S(2)}) collective-permute-start(bf16[640,512]{1,0:T(8,128)(2,1)S(1)} %constant_dynamic-update-slice_fusion.refs_0_), channel_id=1, source_target_pairs={{0,1},{1,0},{2,3},{3,2},{4,5},{5,4},{6,7},{7,6},{8,9},{9,8},{10,11... | collective-permute-start | bytes 1966088 | tf_op jit(solution)/shard_map/ppermute | solution.py:685
  84.6 8.3 %collective-permute-start.31 = (bf16[256,512]{1,0:T(8,128)(2,1)S(1)}, bf16[256,512]{1,0:T(8,128)(2,1)S(1)}, u32[]{:S(2)}, u32[]{:S(2)}) collective-permute-start(bf16[256,512]{1,0:T(8,128)(2,1)S(1)} %get-tuple-element.204), channel_id=1, source_target_pairs={{0,2},{1,3},{2,0},{3,1},{4,6},{5,7},{6,4},{7,5},{8,10},{9,11},{10,... | collective-permute-start | bytes 786440 | tf_op jit(solution)/shard_map/ppermute | solution.py:685
  87.5 8.8 %collective-permute-start.16 = (bf16[288,512]{1,0:T(8,128)(2,1)S(1)}, bf16[288,512]{1,0:T(8,128)(2,1)S(1)}, u32[]{:S(2)}, u32[]{:S(2)}) collective-permute-start(bf16[288,512]{1,0:T(8,128)(2,1)S(1)} %pad_maximum_fusion.2), channel_id=1, source_target_pairs={{0,4},{4,0},{8,12},{12,8},{16,20},{20,16},{24,28},{28,24},{1,5},{5... | collective-permute-start | bytes 884744 | tf_op jit(solution)/shard_map/ppermute | solution.py:689
  87.9 8.0 %collective-permute-start.29 = (bf16[256,512]{1,0:T(8,128)(2,1)S(1)}, bf16[256,512]{1,0:T(8,128)(2,1)S(1)}, u32[]{:S(2)}, u32[]{:S(2)}) collective-permute-start(bf16[256,512]{1,0:T(8,128)(2,1)S(1)} %get-tuple-element.201), channel_id=1, source_target_pairs={{0,8},{4,12},{8,0},{12,4},{16,24},{20,28},{24,16},{28,20},{1,9},{5... | collective-permute-start | bytes 786440 | tf_op jit(solution)/shard_map/ppermute | solution.py:689
  89.1 29.4 %collective-permute-start.24 = (bf16[320,512]{1,0:T(8,128)(2,1)S(1)}, bf16[320,512]{1,0:T(8,128)(2,1)S(1)}, u32[]{:S(2)}, u32[]{:S(2)}) collective-permute-start(bf16[320,512]{1,0:T(8,128)(2,1)S(1)} %get-tuple-element.173), channel_id=1, source_target_pairs={{0,4},{4,8},{8,12},{12,16},{16,20},{20,24},{24,28},{28,0},{1,5},{5... | collective-permute-start | bytes 983048 | tf_op jit(solution)/shard_map/ppermute | solution.py:694
  92.9 42.7 %collective-permute-start.22 = (bf16[640,512]{1,0:T(8,128)(2,1)S(1)}, bf16[640,512]{1,0:T(8,128)(2,1)S(1)}, u32[]{:S(2)}, u32[]{:S(2)}) collective-permute-start(bf16[640,512]{1,0:T(8,128)(2,1)S(1)} %constant_dynamic-update-slice_fusion.refs_0_), channel_id=1, source_target_pairs={{0,2},{1,3},{2,0},{3,1},{4,6},{5,7},{6,4},{7,5},{8,10},{9,11},{10,... | collective-permute-start | bytes 1966088 | tf_op jit(solution)/shard_map/ppermute | solution.py:685
  95.8 5.0 %collective-permute-start.32 = (bf16[128,512]{1,0:T(8,128)(2,1)S(1)}, bf16[128,512]{1,0:T(8,128)(2,1)S(1)}, u32[]{:S(2)}, u32[]{:S(2)}) collective-permute-start(bf16[128,512]{1,0:T(8,128)(2,1)S(1)} %get-tuple-element.210), channel_id=1, source_target_pairs={{0,8},{4,12},{8,0},{12,4},{16,24},{20,28},{24,16},{28,20},{1,9},{5... | collective-permute-start | bytes 393224 | tf_op jit(solution)/shard_map/ppermute | solution.py:689
  96.3 11.0 %collective-permute-start.30 = (bf16[128,512]{1,0:T(8,128)(2,1)S(1)}, bf16[128,512]{1,0:T(8,128)(2,1)S(1)}, u32[]{:S(2)}, u32[]{:S(2)}) collective-permute-start(bf16[128,512]{1,0:T(8,128)(2,1)S(1)} %get-tuple-element.208), channel_id=1, source_target_pairs={{0,4},{4,0},{8,12},{12,8},{16,20},{20,16},{24,28},{28,24},{1,5},{5... | collective-permute-start | bytes 393224 | tf_op jit(solution)/shard_map/ppermute | solution.py:689
  100.8 6.5 %collective-permute-start.17 = (bf16[160,512]{1,0:T(8,128)(2,1)S(1)}, bf16[160,512]{1,0:T(8,128)(2,1)S(1)}, u32[]{:S(2)}, u32[]{:S(2)}) collective-permute-start(bf16[160,512]{1,0:T(8,128)(2,1)S(1)} %pad_maximum_fusion.4), channel_id=1, source_target_pairs={{0,8},{4,12},{8,0},{12,4},{16,24},{20,28},{24,16},{28,20},{1,9},{5... | collective-permute-start | bytes 491528 | tf_op jit(solution)/shard_map/ppermute | solution.py:689
  107.5 11.0 %collective-permute-start.18 = (bf16[96,512]{1,0:T(8,128)(2,1)S(1)}, bf16[96,512]{1,0:T(8,128)(2,1)S(1)}, u32[]{:S(2)}, u32[]{:S(2)}) collective-permute-start(bf16[96,512]{1,0:T(8,128)(2,1)S(1)} %pad_maximum_fusion.7), channel_id=1, source_target_pairs={{0,16},{4,20},{8,24},{12,28},{16,0},{20,4},{24,8},{28,12},{1,17},{... | collective-permute-start | bytes 294920 | tf_op jit(solution)/shard_map/ppermute | solution.py:689
  110.5 9.8 %collective-permute-start.33 = (bf16[128,512]{1,0:T(8,128)(2,1)S(1)}, bf16[128,512]{1,0:T(8,128)(2,1)S(1)}, u32[]{:S(2)}, u32[]{:S(2)}) collective-permute-start(bf16[128,512]{1,0:T(8,128)(2,1)S(1)} %bitcast.22), channel_id=1, source_target_pairs={{0,16},{4,20},{8,24},{12,28},{16,0},{20,4},{24,8},{28,12},{1,17},{... | collective-permute-start | bytes 393224 | tf_op jit(solution)/shard_map/ppermute | solution.py:689
  118.6 17.8 %collective-permute-start.26 = (bf16[672,512]{1,0:T(8,128)(2,1)S(1)}, bf16[672,512]{1,0:T(8,128)(2,1)S(1)}, u32[]{:S(2)}, u32[]{:S(2)}) collective-permute-start(bf16[672,512]{1,0:T(8,128)(2,1)S(1)} %pad_maximum_fusion.refs_0_), channel_id=1, source_target_pairs={{0,2},{1,3},{2,0},{3,1},{4,6},{5,7},{6,4},{7,5},{8,10},{9,11},{10,... | collective-permute-start | bytes 2064392 | tf_op jit(solution)/shard_map/ppermute | solution.py:685
  120.3 11.1 %collective-permute-start.34 = (bf16[128,512]{1,0:T(8,128)(2,1)S(1)}, bf16[128,512]{1,0:T(8,128)(2,1)S(1)}, u32[]{:S(2)}, u32[]{:S(2)}) collective-permute-start(bf16[128,512]{1,0:T(8,128)(2,1)S(1)} %add_convert_fusion.11), channel_id=1, source_target_pairs={{0,16},{4,20},{8,24},{12,28},{16,0},{20,4},{24,8},{28,12},{1,17},{... | collective-permute-start | bytes 393224 | tf_op jit(solution)/shard_map/ppermute | solution.py:689
  120.4 11.0 %collective-permute-start.19 = (bf16[64,512]{1,0:T(8,128)(2,1)S(1)}, bf16[64,512]{1,0:T(8,128)(2,1)S(1)}, u32[]{:S(2)}, u32[]{:S(2)}) collective-permute-start(bf16[64,512]{1,0:T(8,128)(2,1)S(1)} %add_convert_fusion.15), channel_id=1, source_target_pairs={{0,16},{4,20},{8,24},{12,28},{16,0},{20,4},{24,8},{28,12},{1,17},{... | collective-permute-start | bytes 196616 | tf_op jit(solution)/shard_map/ppermute | solution.py:689
  131.3 5.0 %collective-permute-start.20 = (bf16[128,512]{1,0:T(8,128)(2,1)S(1)}, bf16[128,512]{1,0:T(8,128)(2,1)S(1)}, u32[]{:S(2)}, u32[]{:S(2)}) collective-permute-start(bf16[128,512]{1,0:T(8,128)(2,1)S(1)} %pad_maximum_fusion.6), channel_id=1, source_target_pairs={{0,8},{4,12},{8,0},{12,4},{16,24},{20,28},{24,16},{28,20},{1,9},{5... | collective-permute-start | bytes 393224 | tf_op jit(solution)/shard_map/ppermute | solution.py:689
  131.5 9.1 %collective-permute-start.35 = (bf16[256,512]{1,0:T(8,128)(2,1)S(1)}, bf16[256,512]{1,0:T(8,128)(2,1)S(1)}, u32[]{:S(2)}, u32[]{:S(2)}) collective-permute-start(bf16[256,512]{1,0:T(8,128)(2,1)S(1)} %constant_dynamic-update-slice_fusion.2), channel_id=1, source_target_pairs={{0,4},{4,0},{8,12},{12,8},{16,20},{20,16},{24,28},{28,24},{1,5},{5... | collective-permute-start | bytes 786440 | tf_op jit(solution)/shard_map/ppermute | solution.py:689
  135.6 10.6 %collective-permute-start.25 = (bf16[672,512]{1,0:T(8,128)(2,1)S(1)}, bf16[672,512]{1,0:T(8,128)(2,1)S(1)}, u32[]{:S(2)}, u32[]{:S(2)}) collective-permute-start(bf16[672,512]{1,0:T(8,128)(2,1)S(1)} %pad_maximum_fusion.refs_0_), channel_id=1, source_target_pairs={{0,1},{1,0},{2,3},{3,2},{4,5},{5,4},{6,7},{7,6},{8,9},{9,8},{10,11... | collective-permute-start | bytes 2064392 | tf_op jit(solution)/shard_map/ppermute | solution.py:685
  136.4 7.5 %collective-permute-start.23 = (bf16[640,512]{1,0:T(8,128)(2,1)S(1)}, bf16[640,512]{1,0:T(8,128)(2,1)S(1)}, u32[]{:S(2)}, u32[]{:S(2)}) collective-permute-start(bf16[640,512]{1,0:T(8,128)(2,1)S(1)} %collective-permute-done.22.refs_2_), channel_id=1, source_target_pairs={{0,1},{1,0},{2,3},{3,2},{4,5},{5,4},{6,7},{7,6},{8,9},{9,8},{10,11... | collective-permute-start | bytes 1966088 | tf_op jit(solution)/shard_map/ppermute | solution.py:685
  136.4 9.8 %collective-permute-start.27 = (bf16[672,512]{1,0:T(8,128)(2,1)S(1)}, bf16[672,512]{1,0:T(8,128)(2,1)S(1)}, u32[]{:S(2)}, u32[]{:S(2)}) collective-permute-start(bf16[672,512]{1,0:T(8,128)(2,1)S(1)} %collective-permute-done.26.refs_2_), channel_id=1, source_target_pairs={{0,1},{1,0},{2,3},{3,2},{4,5},{5,4},{6,7},{7,6},{8,9},{9,8},{10,11... | collective-permute-start | bytes 2064392 | tf_op jit(solution)/shard_map/ppermute | solution.py:685
  140.5 11.7 %collective-permute-start.36 = (bf16[512,512]{1,0:T(8,128)(2,1)S(1)}, bf16[512,512]{1,0:T(8,128)(2,1)S(1)}, u32[]{:S(2)}, u32[]{:S(2)}) collective-permute-start(bf16[512,512]{1,0:T(8,128)(2,1)S(1)} %constant_dynamic-update-slice_fusion.4.refs_0_), channel_id=1, source_target_pairs={{0,8},{4,12},{8,0},{12,4},{16,24},{20,28},{24,16},{28,20},{1,9},{5... | collective-permute-start | bytes 1572872 | tf_op jit(solution)/shard_map/ppermute | solution.py:689
  141.9 7.4 %collective-permute-start.28 = (bf16[256,512]{1,0:T(8,128)(2,1)S(1)}, bf16[256,512]{1,0:T(8,128)(2,1)S(1)}, u32[]{:S(2)}, u32[]{:S(2)}) collective-permute-start(bf16[256,512]{1,0:T(8,128)(2,1)S(1)} %pad_maximum_fusion.3.refs_0_), channel_id=1, source_target_pairs={{0,4},{4,0},{8,12},{12,8},{16,20},{20,16},{24,28},{28,24},{1,5},{5... | collective-permute-start | bytes 786440 | tf_op jit(solution)/shard_map/ppermute | solution.py:689
